TPU v7x, 32 devices: a whole 2x2x4 slice. The times are simulated.
32 devices in a mesh: subj: 8 (over z, x), space: 4 (over y, core).
Axes of the slice: x: 2, y: 2, z: 4, core: 2. Of those that a mesh axis runs over, the one named last changes fastest.
Arguments:
- template_warped: bfloat16 [16, 256, 256, 256], P('subj', 'space'), may hold values from -6 to 6
- subject_images: bfloat16 [16, 256, 256, 256], P('subj', 'space'), may hold values from -5 to 5.5, as said below
- jacobians: bfloat16 [16, 256, 256, 256], P('subj', 'space'), may hold values from 0.29882812 to 3
- velocity: float32 [256, 256, 256], P('space', 'subj'), may hold values from -6 to 6
Outputs:
- velocity_new: float32 [256, 256, 256], P('space', 'subj')
Inputs may be any that keep to these rules, and one draw needn't show every extreme that they name: `subject_images`: intensities of the subjects' scans.
All inputs are finite; a program needn't handle non-finite values.
Results may differ from a plain program's by a relative error of at most 0.0003.
Values sent between devices are 32-bit elements; how exact they have to be, the bound alone decides.
No kernel may reach another device: no remote copies, remote signals or barrier semaphores. Data moves between devices by JAX's collectives and lax.ppermute only.
A program may use at most 256 MiB of HBM per device.

v0:
```python
import math

import jax
import jax.numpy as jnp
from jax import lax
from jax.sharding import PartitionSpec as P

sigma_sq = 0.05
step_size = 0.25
alpha_reach = 16.0
highest = lax.Precision.HIGHEST


def smoothing_symbol(first, second, third, length):

    def damping(freq):
        turns = (freq % length).astype(jnp.float32)
        return 2.0 - 2.0 * jnp.cos(turns * (2.0 * math.pi / length))

    total = damping(first) + damping(second) + damping(third)
    return 1.0 / (1.0 + alpha_reach * total) ** 2


def phase_tables(length):
    index = jnp.arange(length, dtype=jnp.int32)
    turns = index[:, None] * index[None, :] % length
    angle = turns.astype(jnp.float32) * (2.0 * math.pi / length)
    return (jnp.cos(angle), jnp.sin(angle))


def packed_tables(length):
    half = length // 2
    index = jnp.arange(length, dtype=jnp.int32)
    freq = jnp.where(index <= half, index, index - half)
    turns = index[:, None] * freq[None, :] % length
    angle = turns.astype(jnp.float32) * (2.0 * math.pi / length)
    forward = jnp.where(index[None, :] <= half, jnp.cos(angle), jnp.sin(angle))
    weight = jnp.where((index == 0) | (index == half), 1.0, 2.0) / length
    inverse = jnp.transpose(forward * weight[None, :])
    return (forward, inverse)


def body(template_warped, subject_images, jacobians, velocity):
    length = template_warped.shape[3]
    half = length // 2
    warped = template_warped.astype(jnp.float32)
    slope = (jnp.roll(warped, -1, axis=3) - jnp.roll(warped, 1, axis=3)) * 0.5
    partial_value = jnp.sum(
        jacobians.astype(jnp.float32) * (subject_images.astype(jnp.float32) - warped) * slope,
        axis=0,
    )
    forward_pack, inverse_pack = packed_tables(length)
    packed = jnp.einsum("xyz,zp->xpy", partial_value, forward_pack, precision=highest)
    packed = lax.psum_scatter(packed, "subj", scatter_dimension=1, tiled=True)
    packed = packed * (2.0 / sigma_sq)
    cosine, sine = phase_tables(length)
    first_table = jnp.stack([cosine, -sine])
    spectra = jnp.einsum("xpy,cyk->ckpx", packed, first_table, precision=highest)
    lines = lax.all_to_all(spectra, "space", split_axis=1, concat_axis=3, tiled=True)
    forward_table = jnp.stack([jnp.stack([cosine, -sine]), jnp.stack([sine, cosine])])
    freq_lines = jnp.einsum("ckpx,cdxw->dkpw", lines, forward_table, precision=highest)
    ky_index = lax.axis_index("space") * lines.shape[1] + jnp.arange(
        lines.shape[1], dtype=jnp.int32
    )
    p_index = lax.axis_index("subj") * lines.shape[2] + jnp.arange(lines.shape[2], dtype=jnp.int32)
    p_freq = jnp.where(p_index <= half, p_index, p_index - half)
    kx_index = jnp.arange(length, dtype=jnp.int32)
    symbol = smoothing_symbol(
        ky_index[:, None, None], p_freq[None, :, None], kx_index[None, None, :], length
    )
    filtered = freq_lines * symbol[None]
    inverse_table = jnp.stack([jnp.stack([cosine, sine]), jnp.stack([-sine, cosine])]) / length
    back_lines = jnp.einsum("ckpw,cdwx->dxpk", filtered, inverse_table, precision=highest)
    columns = lax.all_to_all(back_lines, "space", split_axis=1, concat_axis=3, tiled=True)
    last_table = jnp.stack([cosine, -sine]) / length
    real_field = jnp.einsum("cxpk,cky->xpy", columns, last_table, precision=highest)
    depth_lines = lax.all_to_all(real_field, "subj", split_axis=2, concat_axis=1, tiled=True)
    smoothed = jnp.einsum("xpy,pz->xyz", depth_lines, inverse_pack, precision=highest)
    return velocity - step_size * (2.0 * velocity - smoothed)


def solution(mesh):
    return jax.shard_map(
        body,
        mesh=mesh,
        in_specs=(
            P("subj", "space", None, None),
            P("subj", "space", None, None),
            P("subj", "space", None, None),
            P("space", "subj", None),
        ),
        out_specs=P("space", "subj", None),
        check_vma=False,
    )
```

profile of v0, /device:TPU:0, one launch (start us, length us, event | category | flops | bytes accessed | tf_op | source)
XLA Modules:
  0.0 805.3 jit_solution(11946959617867671953)
XLA Ops:
  6.5 35.1 %fusion.75 = (f32[2,64,256,255]{3,2,1,0:T(8,128)}, f32[2,64,256,255]{3,2,1,0:T(8,128)}) fusion(bf16[2,64,256,256]{3,2,1,0:T(8,128)(2,1)} %param.4), kind=kLoop, calls=%fused_computation.107 | loop fusion | bytes 133693440 | tf_op jit(solution)/shard_map/jit(_roll_static)/slice | solution.py:47
  41.7 16.8 %fusion.74 = (f32[2,64,256,1]{3,2,1,0:T(8,128)}, f32[2,64,256,1]{3,2,1,0:T(8,128)}) fusion(bf16[2,64,256,256]{3,2,1,0:T(8,128)(2,1)} %param.4), kind=kLoop, calls=%fused_computation.106 | loop fusion | bytes 524288 | tf_op jit(solution)/shard_map/jit(_roll_static)/slice | solution.py:47
  58.5 53.5 %fusion.2 = f32[64,256,256]{2,1,0:T(8,128)} fusion(f32[2,64,256,1]{3,2,1,0:T(8,128)} %get-tuple-element.6, f32[2,64,256,255]{3,2,1,0:T(8,128)} %get-tuple-element.8, f32[2,64,256,255]{3,2,1,0:T(8,128)} %get-tuple-element.7, f32[2,64,256,1]{3,2,1,0:T(8,128)} %get-tuple-element.5, bf16[2,64,256,256]{3,2,1,0:T(8,128)(2,1)} %param.5, ...), kind=kLoop, calls=%fused_computation.3 | loop fusion | flops 88080384 | bytes 134217728 | tf_op jit(solution)/shard_map/reduce_sum | solution.py:48
  112.0 35.7 %convolution_bitcast_fusion = f32[64,256,256]{2,1,0:T(8,128)} fusion(f32[64,256,256]{2,1,0:T(8,128)} %fusion.2, s32[256]{0:T(256)S(1)} %add_select_fusion.2, pred[256]{0:T(512)(128)(4,1)S(1)} %iota_compare_fusion), kind=kOutput, calls=%fused_computation.4 | convolution fusion | flops 12885884928 | bytes 33555712 | tf_op jit(solution)/shard_map/xyz,zp->xpy/dot_general | solution.py:53
  148.8 284.5 %reduce-scatter.2.cloned.1.call-done = f32[64,32,256]{2,1,0:T(8,128)} async-done(((f32[64,256,256]{2,1,0:T(8,128)}), f32[64,32,256]{2,1,0:T(8,128)}) %reduce-scatter.2.cloned.1.call-update) | async-done | bytes 2097168 | tf_op jit(solution)/shard_map/reduce_scatter | solution.py:54
  440.7 9.1 %copy.29 = f32[2,256,32,64]{3,2,0,1:T(8,128)} copy(f32[2,256,32,64]{1,3,2,0:T(8,128)} %convolution_bitcast_fusion.1) | data formatting | bytes 8388608 | tf_op jit(solution)/shard_map/xpy,cyk->ckpx/transpose | solution.py:58
  449.9 8.6 %reshape.238 = f32[4,1,262144]{2,1,0:T(1,128)} reshape(f32[256,2,32,64]{3,2,1,0:T(8,128)} %bitcast.83) | data formatting | bytes 8388608
  466.2 45.3 %all-to-all-done = f32[4,1,262144]{2,1,0:T(1,128)} async-done(((f32[4,1,262144]{2,1,0:T(1,128)}), f32[4,1,262144]{2,1,0:T(1,128)}, u32[]{:S(2)}, u32[]{:S(2)}) %all-to-all-start) | async-done | bytes 4194336 | tf_op jit(solution)/shard_map/all_to_all | solution.py:59
  512.1 15.3 %reduce = f32[4,262144]{1,0:T(4,128)} reduce(f32[4,1,262144]{2,1,0:T(1,128)} %all-to-all-done, f32[]{:T(128)} %broadcast.412), dimensions={1}, to_apply=%all_to_all.39.reduce_sub_computation | reduce | bytes 8388612 | tf_op jit(solution)/shard_map/all_to_all | solution.py:59
  527.4 9.3 %reshape.239 = f32[256,2,32,64]{3,2,1,0:T(8,128)} reshape(f32[4,262144]{1,0:T(4,128)} %reduce) | data formatting | bytes 8388608
  536.7 15.2 %copy.68 = f32[2,4,64,32,64]{4,1,3,2,0:T(4,128)} copy(f32[2,4,64,32,64]{4,3,0,2,1:T(8,128)} %bitcast.85) | data formatting | bytes 8388608 | tf_op jit(solution)/shard_map/all_to_all | solution.py:59
  551.9 8.6 %all_to_all.42 = f32[2,64,32,256]{3,2,1,0:T(8,128)} reshape(f32[2,64,32,4,64]{4,3,2,1,0:T(4,128)} %bitcast.86) | data formatting | bytes 8388608 | tf_op jit(solution)/shard_map/all_to_all | solution.py:59
  560.5 11.3 %fusion.6 = f32[2,256,64,32,1]{1,2,4,0,3:T(8,128)S(1)} fusion(f32[2,64,32,256,1]{3,2,1,0,4:T(8,128)} %bitcast.89, f32[1,2,256,256]{3,2,1,0:T(8,128)} %get-tuple-element.10, f32[1,2,256,256]{3,2,1,0:T(8,128)} %get-tuple-element.13), kind=kOutput, calls=%fused_computation.10 | convolution fusion | flops 6442713088 | bytes 9437184 | tf_op jit(solution)/shard_map/ckpx,cdxw->dkpw/dot_general | solution.py:61
  571.8 8.4 %fusion.8 = f32[2,256,32,64]{1,3,2,0:T(8,128)} fusion(f32[2,256,64,32,1]{1,2,4,0,3:T(8,128)S(1)} %fusion.6, f32[64,32,256]{2,0,1:T(8,128)S(1)} %multiply_divide_fusion, f32[1,2,256,256]{3,2,1,0:T(8,128)S(1)} %copy-done, f32[1,2,256,256]{3,2,1,0:T(8,128)S(1)} %get-tuple-element.9), kind=kOutput, calls=%fused_computation.12 | convolution fusion | flops 6444023808 | bytes 11534336 | tf_op jit(solution)/shard_map/ckpw,cdwx->dxpk/dot_general | solution.py:73
  580.2 9.1 %copy.34 = f32[2,256,32,64]{3,2,0,1:T(8,128)} copy(f32[2,256,32,64]{1,3,2,0:T(8,128)} %fusion.8) | data formatting | bytes 8388608 | tf_op jit(solution)/shard_map/ckpw,cdwx->dxpk/transpose | solution.py:73
  589.4 8.6 %reshape.240 = f32[4,1,262144]{2,1,0:T(1,128)} reshape(f32[256,2,32,64]{3,2,1,0:T(8,128)} %bitcast.84) | data formatting | bytes 8388608
  598.0 53.9 %all_to_all.54 = f32[4,1,262144]{2,1,0:T(1,128)} all-to-all(f32[4,1,262144]{2,1,0:T(1,128)} %reshape.240), channel_id=1, replica_groups=mesh['subj'=8,'space'=4] {'space'}, dimensions={0} | all-to-all | bytes 8388608 | tf_op jit(solution)/shard_map/all_to_all | solution.py:74
  651.9 15.3 %reduce.1 = f32[4,262144]{1,0:T(4,128)} reduce(f32[4,1,262144]{2,1,0:T(1,128)} %all_to_all.54, f32[]{:T(128)} %broadcast.412), dimensions={1}, to_apply=%all_to_all.43.reduce_sub_computation | reduce | bytes 8388612 | tf_op jit(solution)/shard_map/all_to_all | solution.py:74
  667.2 9.3 %reshape.241 = f32[256,2,32,64]{3,2,1,0:T(8,128)} reshape(f32[4,262144]{1,0:T(4,128)} %reduce.1) | data formatting | bytes 8388608
  676.4 15.2 %copy.67 = f32[2,4,64,32,64]{4,1,3,0,2:T(4,128)} copy(f32[2,4,64,32,64]{4,3,0,2,1:T(8,128)} %bitcast.87) | data formatting | bytes 8388608 | tf_op jit(solution)/shard_map/all_to_all | solution.py:74
  691.6 8.6 %all_to_all.46 = f32[2,64,32,256]{3,2,0,1:T(8,128)} reshape(f32[2,64,32,4,64]{4,3,2,0,1:T(4,128)} %bitcast.88) | data formatting | bytes 8388608 | tf_op jit(solution)/shard_map/all_to_all | solution.py:74
  710.5 7.2 reshape.242
  722.1 48.1 %all-to-all-done.2 = f32[8,1,65536]{2,1,0:T(1,128)} async-done(((f32[8,1,65536]{2,1,0:T(1,128)}), f32[8,1,65536]{2,1,0:T(1,128)}, u32[]{:S(2)}, u32[]{:S(2)}) %all-to-all-start.2) | async-done | bytes 2097184 | tf_op jit(solution)/shard_map/all_to_all | solution.py:77
  770.2 7.1 reduce.2
  (26 shorter events, 52.1 us)
Async XLA Ops:
  6.5 426.7 %reduce-scatter.2.cloned.1.call-start = ((), (), s32[]{:S(2)}) async-start(), calls=%async_computation.4 | async-start | bytes 18874368 | tf_op jit(solution)/shard_map/reduce_scatter | solution.py:54
  458.5 53.1 %all-to-all-start = ((f32[4,1,262144]{2,1,0:T(1,128)}), f32[4,1,262144]{2,1,0:T(1,128)}, u32[]{:S(2)}, u32[]{:S(2)}) async-start(f32[4,1,262144]{2,1,0:T(1,128)} %reshape.238), calls=%async_computation.1 | async-start | bytes 8388608 | tf_op jit(solution)/shard_map/all_to_all | solution.py:59
  560.5 11.3 %copy-start = (f32[1,2,256,256]{3,2,1,0:T(8,128)S(1)}, f32[1,2,256,256]{3,2,1,0:T(8,128)}, u32[]{:S(2)}) copy-start(f32[1,2,256,256]{3,2,1,0:T(8,128)} %get-tuple-element.14) | copy-start | bytes 1572868
  717.7 52.5 %all-to-all-start.2 = ((f32[8,1,65536]{2,1,0:T(1,128)}), f32[8,1,65536]{2,1,0:T(1,128)}, u32[]{:S(2)}, u32[]{:S(2)}) async-start(f32[8,1,65536]{2,1,0:T(1,128)} %reshape.242), calls=%async_computation.3 | async-start | bytes 4194304 | tf_op jit(solution)/shard_map/all_to_all | solution.py:77
Sparse Core Ops, SparseCore 0:
  147.8 285.3 reduce-scatter.1
where the time goes:
time: 811 us; the launch traced here: 805 us
  waiting for transfers between devices  378 us (47%)
  local copies, waits for them, and re-layouts  181 us (22%)
  other arithmetic  97 us (12%)
  matrix products  72.8 us (9%)
  blocking collectives  53.9 us (7%)
  between operations  13.9 us (2%)
  starting transfers between devices  9.2 us (1%)
    reduce_scatter x1, waiting for transfers between devices, body(): packed = lax.psum_scatter(packed, 'subj', scatter_dimension=1, tiled=True)  284 us
    all_to_all x1, blocking collectives, body(): lax.all_to_all(back_lines, 'space', split_axis=1, concat_axis=3, tiled=True)  53.9 us
    reduce_sum x1, other arithmetic, body(): jnp.sum(jacobians.astype(jnp.float32) * (subject_images.astype(jnp.float3...  53.5 us
    slice x2, local copies, waits for them, and re-layouts, body(): slope = (jnp.roll(warped, -1, axis=3) - jnp.roll(warped, 1, axis=3)) * 0.5  51.9 us
    all_to_all x1, waiting for transfers between devices, body(): lax.all_to_all(real_field, 'subj', split_axis=2, concat_axis=1, tiled=True)  48.1 us
    unnamed x8, local copies, waits for them, and re-layouts  46.5 us
    all_to_all x1, waiting for transfers between devices, body(): lax.all_to_all(spectra, 'space', split_axis=1, concat_axis=3, tiled=True)  45.3 us
    dot_general x1, matrix products, body(): jnp.einsum('xyz,zp->xpy', partial_value, forward_pack, precision=highest)  35.7 us
  transfers between devices with their start and end apart: 3, of which 3 were waited for; matrix products, arithmetic and copies ran while one was open for 0% of the time, Pallas kernels for 0%

commit v1 on v0

v1 whole, which is shorter than its diff:
```python
import functools
import math

import jax
import jax.numpy as jnp
import ml_dtypes
import numpy as np
from jax import lax
from jax.experimental import pallas as pl
from jax.experimental.pallas import tpu as pltpu
from jax.sharding import PartitionSpec as P

sigma_sq = 0.05
step_size = 0.25
alpha_reach = 16.0
highest = lax.Precision.HIGHEST
vmem_bytes = 30 * 1024 * 1024
lane = 128
chunk_eighths = (4, 3, 1)


def split_bf16(table):
    high = table.astype(ml_dtypes.bfloat16)
    low = (table - high.astype(np.float64)).astype(ml_dtypes.bfloat16)
    return high, low


def packed_np(length):
    half = length // 2
    index = np.arange(length)
    freq = np.where(index <= half, index, index - half)
    angle = (index[:, None] * freq[None, :] % length) * (2.0 * math.pi / length)
    forward = np.where(index[None, :] <= half, np.cos(angle), np.sin(angle))
    weight = np.where((index == 0) | (index == half), 1.0, 2.0) / length
    lam = 2.0 - 2.0 * np.cos(freq * (2.0 * math.pi / length))
    return forward, (forward * weight[None, :]).T, lam


class Plan:
    def __init__(self, length, rows_x, subj, space):
        self.length, self.xl, self.subj, self.space = length, rows_x, subj, space
        self.yl = length // subj
        self.lanes = self.yl * self.xl
        self.half = self.lanes // 2
        self.ty = lane // self.xl if self.xl < lane else 1
        self.tiles = self.lanes // lane
        eighth = length // 8
        self.chunks = [e * eighth for e in chunk_eighths]
        self.offs = np.concatenate([[0], np.cumsum(self.chunks)])[:-1].tolist()
        self.groups = [c // space for c in self.chunks]
        ring = list(range(0, subj, 2)) + list(range(subj - 1, 0, -2))
        self.ring = ring
        self.place = [ring.index(j) for j in range(subj)]
        forward, inverse, lam = packed_np(length)
        order = np.stack(
            [
                np.concatenate(
                    [
                        off + (s ^ d) * g + np.arange(g)
                        for off, g in zip(self.offs, self.groups)
                        for d in range(space)
                    ]
                )
                for s in range(space)
            ]
        )
        high, low = split_bf16(forward.T)
        self.t_table = np.concatenate([high, high, low], axis=1)[order]
        high, low = split_bf16(inverse)
        self.i_table = np.stack([high, low], 0)[:, order].transpose(1, 0, 2, 3)
        eye = np.eye(self.ty)
        blocks = forward.reshape(space, self.xl, length)
        wide = np.einsum("ab,sxw->saxbw", eye, blocks).reshape(space, lane, self.ty * length)
        high, low = split_bf16(wide)
        self.w_table = np.concatenate([high, high, low], axis=1)
        blocks = inverse.reshape(length, space, self.xl)
        wide = np.einsum("ab,wsx->sawbx", eye, blocks).reshape(space, self.ty * length, lane)
        high, low = split_bf16(wide)
        self.v_table = np.concatenate([high, high, low], axis=1)
        index = np.arange(length)
        slope = np.zeros((length, length))
        slope[(index + 1) % length, index] += 0.5
        slope[(index - 1) % length, index] -= 0.5
        self.d_table = slope.astype(ml_dtypes.bfloat16)
        centre = (1.0 + alpha_reach * (lam[:, None] + lam[None, :])) / alpha_reach + 2.0
        r = 2.0 / (centre + np.sqrt(centre * centre - 4.0))
        q = r * r
        scale = (2.0 / sigma_sq) * q / (alpha_reach * alpha_reach)
        self.r_table = np.stack(
            [r, scale * (1 + q) / (1 - q) ** 3, scale / (1 - q) ** 2, np.log(r)]
        ).astype(np.float32)


def split(value):
    high = value.astype(jnp.bfloat16)
    low = (value - high.astype(jnp.float32)).astype(jnp.bfloat16)
    return high, low


def params(**kw):
    return pltpu.CompilerParams(vmem_limit_bytes=vmem_bytes, **kw)


def force_kernel(plan, step_x, place_ref, warped, images, jac, d_ref, t_ref, *rest):
    outs, field = rest[:-1], rest[-1]
    n = len(plan.chunks)
    way, at = pl.program_id(0), pl.program_id(1)
    yh = plan.yl // 2
    count = warped.shape[0]
    length = plan.length
    rows = step_x * yh

    total = None
    for b in range(count):
        w = warped[b].reshape(rows, length)
        slope = jnp.dot(w, d_ref[...], preferred_element_type=jnp.float32)
        diff = images[b].reshape(rows, length).astype(jnp.float32) - w.astype(jnp.float32)
        term = jac[b].reshape(rows, length).astype(jnp.float32) * diff * slope
        total = term if total is None else total + term
    start = pl.multiple_of(at * rows, rows)
    for h in range(length // lane):
        field[h, pl.ds(start, rows), :] = total[:, h * lane : (h + 1) * lane]

    def transform(refs):
        per = max(1, 256 // plan.xl)
        for y0 in range(0, yh, per):
            lines = jnp.concatenate(
                [
                    jnp.concatenate(
                        [
                            field[h, pl.ds(y, plan.xl, stride=yh), :]
                            for h in range(length // lane)
                        ],
                        axis=1,
                    )
                    for y in range(y0, y0 + per)
                ],
                axis=0,
            )
            high, low = split(lines)
            both = jnp.concatenate([high, low, high], axis=1)
            out = lax.dot_general(
                t_ref[0], both, (((1,), (1,)), ((), ())), preferred_element_type=jnp.float32
            )
            for ref, off, size in zip(refs, plan.offs, plan.chunks):
                ref[:, y0 * plan.xl : (y0 + per) * plan.xl] = out[off : off + size]

    last = at == pl.num_programs(1) - 1

    @pl.when(jnp.logical_and(last, way == 0))
    def _():
        transform(outs[:n])

    @pl.when(jnp.logical_and(last, way == 1))
    def _():
        transform(outs[n:])


def force_blocks(plan, place, warped, images, jac):
    count, xl, _, length = warped.shape
    yh = plan.yl // 2
    step_x = min(16, xl)
    source = pl.BlockSpec(
        (count, step_x, yh, length), lambda way, at, place: (0, at, 2 * place[way] + way, 0)
    )
    shapes = [jax.ShapeDtypeStruct((c, plan.half), jnp.float32) for c in plan.chunks] * 2
    outs = pl.pallas_call(
        functools.partial(force_kernel, plan, step_x),
        out_shape=shapes,
        grid_spec=pltpu.PrefetchScalarGridSpec(
            num_scalar_prefetch=1,
            grid=(2, xl // step_x),
            in_specs=[
                source,
                source,
                source,
                pl.BlockSpec((length, length), lambda way, at, place: (0, 0)),
                pl.BlockSpec((1, length, 3 * length), lambda way, at, place: (place[2], 0, 0)),
            ],
            out_specs=[pl.BlockSpec(s.shape, lambda way, at, place: (0, 0)) for s in shapes],
            scratch_shapes=[pltpu.VMEM((length // lane, xl * yh, lane), jnp.float32)],
        ),
        compiler_params=params(),
        cost_estimate=pl.CostEstimate(
            flops=16 * xl * yh * length * length,
            bytes_accessed=12 * count * xl * yh * length + 8 * xl * yh * length,
            transcendentals=0,
        ),
        name="force",
    )(place, warped, images, jac, jnp.asarray(plan.d_table), jnp.asarray(plan.t_table))
    n = len(plan.chunks)
    return outs[:n], outs[n:]


def join_kernel(plan, g, right, right_local, left, left_local, *outs):
    for d, out in enumerate(outs):
        rows = slice(d * g, (d + 1) * g)
        out[:, : plan.half] = right[rows] + right_local[rows]
        out[:, plan.half :] = left[rows] + left_local[rows]


def join(plan, g, right, right_local, left, left_local):
    return pl.pallas_call(
        functools.partial(join_kernel, plan, g),
        out_shape=[jax.ShapeDtypeStruct((g, plan.lanes), jnp.float32)] * plan.space,
        compiler_params=params(),
        name="join",
    )(right, right_local, left, left_local)


def forward_kernel(plan, g, place_ref, w_ref, r_ref, *rest):
    pieces, f_ref, ends_ref = rest[: plan.space], rest[-2], rest[-1]
    me = place_ref[0]
    total = None
    for d, piece in enumerate(pieces):
        lines = jnp.concatenate(
            [piece[:, t * lane : (t + 1) * lane] for t in range(plan.tiles)], axis=0
        )
        high, low = split(lines)
        both = jnp.concatenate([high, low, high], axis=1)
        term = jnp.dot(both, w_ref[me ^ d], preferred_element_type=jnp.float32)
        total = term if total is None else total + term
    f_ref[...] = total
    r = r_ref[0]
    length = plan.length

    def line(y):
        t, a = y // plan.ty, y % plan.ty
        return f_ref[t * g : (t + 1) * g, a * length : (a + 1) * length]

    zero = jnp.zeros_like(r)
    v, w = zero, zero
    for y in range(plan.yl):
        w = r * (w + v)
        v = line(y) + r * v
    ends_ref[0], ends_ref[1] = v, w
    v, w = zero, zero
    for y in range(plan.yl - 1, -1, -1):
        v = v + line(y)
        w = r * (w + v)
        v = r * v
    ends_ref[2], ends_ref[3] = v, w


def forward_lines(plan, g, place, r_tab, pieces):
    rows = plan.tiles * g
    return pl.pallas_call(
        functools.partial(forward_kernel, plan, g),
        out_shape=[
            jax.ShapeDtypeStruct((rows, plan.ty * plan.length), jnp.float32),
            jax.ShapeDtypeStruct((4, g, plan.length), jnp.float32),
        ],
        in_specs=[pl.BlockSpec(memory_space=pltpu.SMEM)]
        + [pl.BlockSpec(memory_space=pltpu.VMEM)] * (2 + plan.space),
        out_specs=[pl.BlockSpec(memory_space=pltpu.VMEM)] * 2,
        compiler_params=params(),
        name="first_forward",
    )(place, jnp.asarray(plan.w_table), r_tab, *pieces)


def combine(ends, other, right, power, span):
    hi = [jnp.where(right, ends[i], other[i]) for i in range(4)]
    lo = [jnp.where(right, other[i], ends[i]) for i in range(4)]
    return (
        hi[0] + power * lo[0],
        hi[1] + power * (lo[1] + span * lo[0]),
        lo[2] + power * hi[2],
        lo[3] + power * (hi[3] + span * hi[2]),
    )


def merge_kernel(plan, stage, place_ref, r_ref, ends_ref, other_ref, out_ref):
    span = float(plan.yl << stage)
    right = (place_ref[0] >> stage) % 2 == 1
    power = jnp.exp(span * r_ref[3])
    ends = [ends_ref[i] for i in range(4)]
    other = [other_ref[i] for i in range(4)]
    for i, value in enumerate(combine(ends, other, right, power, span)):
        out_ref[i] = value


def merge(plan, stage, place, r_tab, ends, other):
    return pl.pallas_call(
        functools.partial(merge_kernel, plan, stage),
        out_shape=jax.ShapeDtypeStruct(ends.shape, jnp.float32),
        in_specs=[pl.BlockSpec(memory_space=pltpu.SMEM)]
        + [pl.BlockSpec(memory_space=pltpu.VMEM)] * 3,
        out_specs=pl.BlockSpec(memory_space=pltpu.VMEM),
        compiler_params=params(),
        name="merge",
    )(place, r_tab, ends, other)


def backward_kernel(plan, g, stages, place_ref, v_ref, r_ref, f_ref, ends_ref, *rest):
    others, outs, u_ref = rest[:stages], rest[stages:-1], rest[-1]
    me, block = place_ref[0], place_ref[1]
    length = plan.length
    r, alpha, beta, log_r = r_ref[0], r_ref[1], r_ref[2], r_ref[3]
    ends = [ends_ref[i] for i in range(4)]
    zero = jnp.zeros_like(r)
    carry = [zero] * 4
    for stage in range(stages):
        other = [others[stage][i] for i in range(4)]
        size = 1 << stage
        right = (block >> stage) % 2 == 1
        inside = block % size
        before = (inside * plan.yl).astype(jnp.float32)
        after = ((size - 1 - inside) * plan.yl).astype(jnp.float32)
        reach = jnp.where(right, before, after)
        power = jnp.exp(reach * log_r)
        for i in (0, 2):
            take = jnp.where(right, 1.0, 0.0) if i == 0 else jnp.where(right, 0.0, 1.0)
            carry[i] = carry[i] + take * (power * other[i])
            carry[i + 1] = carry[i + 1] + take * (power * (other[i + 1] + reach * other[i]))
        if stage == stages - 1:
            span = float(plan.yl << stage)
            ends = combine(ends, other, right, jnp.exp(span * log_r), span)
    full = jnp.exp(float(length) * log_r)
    inverse = 1.0 / (1.0 - full)
    for i in (0, 2):
        v = ends[i] * inverse
        w = (ends[i + 1] + full * (float(length) * v)) * inverse
        reach = (block if i == 0 else plan.subj - 1 - block) * plan.yl
        reach = reach.astype(jnp.float32)
        power = jnp.exp(reach * log_r)
        carry[i] = carry[i] + power * v
        carry[i + 1] = carry[i + 1] + power * (w + reach * v)

    def line(y):
        t, a = y // plan.ty, y % plan.ty
        return (slice(t * g, (t + 1) * g), slice(a * length, (a + 1) * length))

    v, w = carry[0], carry[1]
    for y in range(plan.yl):
        w = r * (w + v)
        v = f_ref[line(y)] + r * v
        u_ref[line(y)] = alpha * v + beta * w
    v, w = carry[2], carry[3]
    for y in range(plan.yl - 1, -1, -1):
        u_ref[line(y)] = u_ref[line(y)] + (alpha * v + beta * w)
        v = v + f_ref[line(y)]
        w = r * (w + v)
        v = r * v
    high, low = split(u_ref[...])
    both = jnp.concatenate([high, low, high], axis=1)
    for d, out in enumerate(outs):
        back = jnp.dot(both, v_ref[me ^ d], preferred_element_type=jnp.float32)
        for t in range(plan.tiles):
            out[:, t * lane : (t + 1) * lane] = back[t * g : (t + 1) * g]


def backward_lines(plan, g, place, r_tab, f, ends, others):
    stages = len(others)
    return pl.pallas_call(
        functools.partial(backward_kernel, plan, g, stages),
        out_shape=[jax.ShapeDtypeStruct((g, plan.lanes), jnp.float32)] * plan.space,
        in_specs=[pl.BlockSpec(memory_space=pltpu.SMEM)]
        + [pl.BlockSpec(memory_space=pltpu.VMEM)] * (4 + stages),
        out_specs=[pl.BlockSpec(memory_space=pltpu.VMEM)] * plan.space,
        scratch_shapes=[pltpu.VMEM(f.shape, jnp.float32)],
        compiler_params=params(),
        name="second_and_back",
    )(place, jnp.asarray(plan.v_table), r_tab, f, ends, *others)


def finish_kernel(plan, y_step, place_ref, i_ref, velocity, *rest):
    pieces, out, field = rest[:-2], rest[-2], rest[-1]
    length, xl = plan.length, plan.xl
    high_table, low_table = i_ref[0, 0], i_ref[0, 1]
    table = jnp.concatenate([high_table, high_table, low_table], axis=0)
    for t in range(y_step // plan.ty):
        columns = jnp.concatenate([p[:, t * lane : (t + 1) * lane] for p in pieces], axis=0)
        high, low = split(columns.T)
        both = jnp.concatenate([high, low, high], axis=1)
        lines = jnp.dot(both, table, preferred_element_type=jnp.float32)
        for a in range(plan.ty):
            y = t * plan.ty + a
            for h in range(length // lane):
                field[h, pl.ds(y, xl, stride=y_step), :] = lines[
                    a * xl : (a + 1) * xl, h * lane : (h + 1) * lane
                ]
    for h in range(length // lane):
        cols = slice(h * lane, (h + 1) * lane)
        vel = velocity[:, :, cols]
        smoothed = field[h].reshape(xl, y_step, lane)
        out[:, :, cols] = vel - step_size * (2.0 * vel - smoothed)


def finish(plan, place, velocity, pieces):
    xl, yl, length = velocity.shape
    y_step = 8
    width = y_step * xl
    return pl.pallas_call(
        functools.partial(finish_kernel, plan, y_step),
        out_shape=jax.ShapeDtypeStruct(velocity.shape, jnp.float32),
        grid_spec=pltpu.PrefetchScalarGridSpec(
            num_scalar_prefetch=1,
            grid=(yl // y_step,),
            in_specs=[
                pl.BlockSpec((1, 2, length, length), lambda at, place: (place[0], 0, 0, 0)),
                pl.BlockSpec((xl, y_step, length), lambda at, place: (0, at, 0)),
            ]
            + [pl.BlockSpec((p.shape[0], width), lambda at, place: (0, at)) for p in pieces],
            out_specs=pl.BlockSpec((xl, y_step, length), lambda at, place: (0, at, 0)),
            scratch_shapes=[pltpu.VMEM((length // lane, xl * y_step, lane), jnp.float32)],
        ),
        compiler_params=params(),
        name="last_back",
    )(place, jnp.asarray(plan.i_table), velocity, *pieces)


def ring_body(plan, template_warped, subject_images, jacobians, velocity):
    subj, space = plan.subj, plan.space
    j, s = lax.axis_index("subj"), lax.axis_index("space")
    ring = jnp.asarray(plan.ring, jnp.int32)
    at = jnp.asarray(plan.place, jnp.int32)[j]
    place = jnp.stack([s, j]).astype(jnp.int32)
    to_right = [(plan.ring[i], plan.ring[(i + 1) % subj]) for i in range(subj)]
    to_left = [(b, a) for a, b in to_right]
    chunks = range(len(plan.chunks))
    r_tabs = [
        lax.dynamic_slice_in_dim(jnp.asarray(plan.r_table), off + s * g, g, axis=1)
        for off, g in zip(plan.offs, plan.groups)
    ]

    local = []
    for k in range(subj):
        blocks = jnp.stack([ring[(at - 1 - k) % subj], ring[(at + 1 + k) % subj], s])
        local.append(
            force_blocks(
                plan, blocks.astype(jnp.int32), template_warped, subject_images, jacobians
            )
        )

    stages = subj.bit_length() - 1
    gate = None
    finished = []
    for c in chunks:
        g = plan.groups[c]
        right, left = local[0][0][c], local[0][1][c]
        if gate is not None:
            right, left, _ = lax.optimization_barrier((right, left, gate))
        for k in range(1, subj):
            right = lax.ppermute(right, "subj", to_right)
            left = lax.ppermute(left, "subj", to_left)
            if k < subj - 1:
                right = right + local[k][0][c]
                left = left + local[k][1][c]
        pieces = join(plan, g, right, local[-1][0][c], left, local[-1][1][c])
        gate = pieces[0]
        pieces = [pieces[0]] + [
            lax.ppermute(pieces[d], "space", [(i, i ^ d) for i in range(space)])
            for d in range(1, space)
        ]
        f, ends = forward_lines(plan, g, place, r_tabs[c], pieces)
        others = []
        for stage in range(stages):
            size = 1 << stage
            other = lax.ppermute(ends, "subj", [(i, i ^ size) for i in range(subj)])
            others.append(other)
            if stage < stages - 1:
                ends = merge(plan, stage, place[1:], r_tabs[c], ends, other)
        pieces = backward_lines(plan, g, place, r_tabs[c], f, ends, others)
        finished += [pieces[0]] + [
            lax.ppermute(pieces[d], "space", [(i, i ^ d) for i in range(space)])
            for d in range(1, space)
        ]
    return finish(plan, place, velocity, finished)


def smoothing_symbol(first, second, third, length):
    def damping(freq):
        turns = (freq % length).astype(jnp.float32)
        return 2.0 - 2.0 * jnp.cos(turns * (2.0 * math.pi / length))

    total = damping(first) + damping(second) + damping(third)
    return 1.0 / (1.0 + alpha_reach * total) ** 2


def transposing_body(template_warped, subject_images, jacobians, velocity):
    length = template_warped.shape[3]
    half = length // 2
    warped = template_warped.astype(jnp.float32)
    slope = (jnp.roll(warped, -1, axis=3) - jnp.roll(warped, 1, axis=3)) * 0.5
    partial_value = jnp.sum(
        jacobians.astype(jnp.float32) * (subject_images.astype(jnp.float32) - warped) * slope,
        axis=0,
    )
    forward, inverse, _ = packed_np(length)
    forward, inverse = forward.astype(np.float32), inverse.astype(np.float32)
    packed = jnp.einsum("xyz,zp->xpy", partial_value, forward, precision=highest)
    packed = lax.psum_scatter(packed, "subj", scatter_dimension=1, tiled=True)
    packed = packed * (2.0 / sigma_sq)
    spectra = jnp.einsum("xpy,yk->kpx", packed, forward, precision=highest)
    lines = lax.all_to_all(spectra, "space", split_axis=0, concat_axis=2, tiled=True)
    freq_lines = jnp.einsum("kpx,xw->kpw", lines, forward, precision=highest)

    def true_freq(index):
        return jnp.where(index <= half, index, index - half)

    def mine(axis, size):
        return true_freq(lax.axis_index(axis) * size + jnp.arange(size, dtype=jnp.int32))

    symbol = smoothing_symbol(
        mine("space", lines.shape[0])[:, None, None],
        mine("subj", lines.shape[1])[None, :, None],
        true_freq(jnp.arange(length, dtype=jnp.int32))[None, None, :],
        length,
    )
    back_lines = jnp.einsum("kpw,wx->xpk", freq_lines * symbol, inverse, precision=highest)
    columns = lax.all_to_all(back_lines, "space", split_axis=0, concat_axis=2, tiled=True)
    real_field = jnp.einsum("xpk,ky->xpy", columns, inverse, precision=highest)
    depth_lines = lax.all_to_all(real_field, "subj", split_axis=2, concat_axis=1, tiled=True)
    smoothed = jnp.einsum("xpy,pz->xyz", depth_lines, inverse, precision=highest)
    return velocity - step_size * (2.0 * velocity - smoothed)


def body(subj, space, template_warped, subject_images, jacobians, velocity):
    _, xl, _, length = template_warped.shape
    yl = velocity.shape[1]
    power_of_two = subj & (subj - 1) == 0 and space & (space - 1) == 0
    fits = (
        subj > 1
        and power_of_two
        and length % lane == 0
        and yl % 32 == 0
        and xl >= 16
        and lane % xl == 0
        and length // 8 // space % 8 == 0
    )
    if not fits:
        return transposing_body(template_warped, subject_images, jacobians, velocity)
    plan = Plan(length, xl, subj, space)
    return ring_body(plan, template_warped, subject_images, jacobians, velocity)


def solution(mesh):
    return jax.shard_map(
        functools.partial(body, mesh.shape["subj"], mesh.shape["space"]),
        mesh=mesh,
        in_specs=(
            P("subj", "space", None, None),
            P("subj", "space", None, None),
            P("subj", "space", None, None),
            P("space", "subj", None),
        ),
        out_specs=P("space", "subj", None),
        check_vma=False,
    )
```

time: 811 us -> 315 us (0.39)
  waiting for transfers between devices: 378 us -> 90.9 us
  local copies, waits for them, and re-layouts: 181 us -> 31.7 us
  Pallas kernels: 0 us -> 86.1 us
  other arithmetic: 97 us -> 18.2 us
  matrix products: 72.8 us -> 0 us
  starting transfers between devices: 9.2 us -> 74.9 us
  blocking collectives: 53.9 us -> 0 us
    reduce_scatter x1 -> x0, waiting for transfers between devices: 284 us -> none  [body(): packed = lax.psum_scatter(packed, 'subj', scatter_dimension=1, tiled=True)]
    all_to_all x2 -> x0, waiting for transfers between devices: 93.5 us -> none  [the longest x1 48.1 us: body(): lax.all_to_all(real_field, 'subj', split_axis=2, concat_axis=1, tiled=True)]
    ppermute x0 -> x69, waiting for transfers between devices: none -> 90.9 us  [the longest x21 65.4 us: ring_body(): left = lax.ppermute(left, 'subj', to_left)]
    pallas_call x0 -> x24, Pallas kernels: none -> 86.1 us  [the longest x8 63.4 us: force_blocks(): pl.pallas_call(functools.partial(force_kernel, plan, step_x), out_shape=s...]
    ppermute x0 -> x69, starting transfers between devices: none -> 74.9 us  [the longest x21 24 us: ring_body(): left = lax.ppermute(left, 'subj', to_left)]
    dot_general x6 -> x0, matrix products: 72.8 us -> none  [the longest x1 35.7 us: body(): jnp.einsum('xyz,zp->xpy', partial_value, forward_pack, precision=highest)]
    all_to_all x7 -> x0, local copies, waits for them, and re-layouts: 59.3 us -> none  [the longest x3 24.3 us: body(): lax.all_to_all(spectra, 'space', split_axis=1, concat_axis=3, tiled=True)]
    all_to_all x1 -> x0, blocking collectives: 53.9 us -> none  [body(): lax.all_to_all(back_lines, 'space', split_axis=1, concat_axis=3, tiled=True)]
  transfers between devices with their start and end apart: 3 -> 69, of which waited for: 3 -> 30; matrix products, arithmetic and copies ran while one was open for 0% -> 6% of each run, Pallas kernels for 0% -> 23%
where the time goes in v1:
time: 315 us; the launch traced here: 313 us
  waiting for transfers between devices  90.9 us (29%)
  Pallas kernels  86.1 us (27%)
  starting transfers between devices  74.9 us (24%)
  local copies, waits for them, and re-layouts  31.7 us (10%)
  other arithmetic  18.2 us (6%)
  between operations  11.3 us (4%)
    ppermute x21, waiting for transfers between devices, ring_body(): left = lax.ppermute(left, 'subj', to_left)  65.4 us
    pallas_call x8, Pallas kernels, force_blocks(): pl.pallas_call(functools.partial(force_kernel, plan, step_x), out_shape=s...  63.4 us
    unnamed x70, local copies, waits for them, and re-layouts  25.9 us
    ppermute x21, starting transfers between devices, ring_body(): left = lax.ppermute(left, 'subj', to_left)  24 us
    ppermute x21, starting transfers between devices, ring_body(): right = lax.ppermute(right, 'subj', to_right)  22.3 us
    ppermute x9, starting transfers between devices, ring_body(): other = lax.ppermute(ends, 'subj', [(i, i ^ size) for i in range(subj)])  15.5 us
    ppermute x18, waiting for transfers between devices, ring_body(): lax.ppermute(pieces[d], 'space', [(i, i ^ d) for i in range(space)])  15.2 us
    ppermute x18, starting transfers between devices, ring_body(): lax.ppermute(pieces[d], 'space', [(i, i ^ d) for i in range(space)])  13.1 us
  transfers between devices with their start and end apart: 69, of which 30 were waited for; matrix products, arithmetic and copies ran while one was open for 6% of the time, Pallas kernels for 23%

profile of v1, /device:TPU:0, one launch (start us, length us, event | category | flops | bytes accessed | tf_op | source)
XLA Modules:
  0.0 313.1 jit_solution(440592189656658340)
XLA Ops:
  16.6 5.8 %copy-done = bf16[2,64,256,256]{3,2,1,0:T(8,128)(2,1)S(1)} copy-done((bf16[2,64,256,256]{3,2,1,0:T(8,128)(2,1)S(1)}, bf16[2,64,256,256]{3,2,1,0:T(8,128)(2,1)}, u32[]{:S(2)}) %copy-start) | copy-done | bytes 16777240
  24.7 7.9 %force.8 = (f32[128,1024]{1,0:T(8,128)S(1)}, f32[96,1024]{1,0:T(8,128)S(1)}, f32[32,1024]{1,0:T(8,128)S(1)}, f32[128,1024]{1,0:T(8,128)S(1)}, f32[96,1024]{1,0:T(8,128)S(1)}, /*index=5*/f32[32,1024]{1,0:T(8,128)S(1)}) custom-call(s32[3]{0:T(128)S(1)} %get-tuple-element.185.place_ref, bf16[2,64,256,256]{3,2,1,0:T(8,128)(2,1)S(1)} %copy-done, ...), custom_call_target="tpu_custom_call" | custom-call | flops 1073741824 | bytes 8388608 | tf_op jit(solution)/shard_map/force/pallas_call | solution.py:167
  32.6 3.0 collective-permute-start.7
  35.7 5.8 %copy-done.1 = bf16[2,64,256,256]{3,2,1,0:T(8,128)(2,1)S(1)} copy-done((bf16[2,64,256,256]{3,2,1,0:T(8,128)(2,1)S(1)}, bf16[2,64,256,256]{3,2,1,0:T(8,128)(2,1)}, u32[]{:S(2)}) %copy-start.1) | copy-done | bytes 16777240
  41.5 7.9 %force.9 = (f32[128,1024]{1,0:T(8,128)S(1)}, f32[96,1024]{1,0:T(8,128)S(1)}, f32[32,1024]{1,0:T(8,128)S(1)}, f32[128,1024]{1,0:T(8,128)S(1)}, f32[96,1024]{1,0:T(8,128)S(1)}, /*index=5*/f32[32,1024]{1,0:T(8,128)S(1)}) custom-call(s32[3]{0:T(128)S(1)} %get-tuple-element.186.place_ref, bf16[2,64,256,256]{3,2,1,0:T(8,128)(2,1)S(1)} %copy-done.1, ...), custom_call_target="tpu_custom_call" | custom-call | flops 1073741824 | bytes 8388608 | tf_op jit(solution)/shard_map/force/pallas_call | solution.py:167
  54.3 7.9 %force.10 = (f32[128,1024]{1,0:T(8,128)S(1)}, f32[96,1024]{1,0:T(8,128)S(1)}, f32[32,1024]{1,0:T(8,128)S(1)}, f32[128,1024]{1,0:T(8,128)S(1)}, f32[96,1024]{1,0:T(8,128)S(1)}, /*index=5*/f32[32,1024]{1,0:T(8,128)S(1)}) custom-call(s32[3]{0:T(128)S(1)} %get-tuple-element.187.place_ref, bf16[2,64,256,256]{3,2,1,0:T(8,128)(2,1)S(1)} %copy-done.1, ...), custom_call_target="tpu_custom_call" | custom-call | flops 1073741824 | bytes 8388608 | tf_op jit(solution)/shard_map/force/pallas_call | solution.py:167
  65.2 7.9 %force.11 = (f32[128,1024]{1,0:T(8,128)S(1)}, f32[96,1024]{1,0:T(8,128)S(1)}, f32[32,1024]{1,0:T(8,128)S(1)}, f32[128,1024]{1,0:T(8,128)S(1)}, f32[96,1024]{1,0:T(8,128)S(1)}, /*index=5*/f32[32,1024]{1,0:T(8,128)S(1)}) custom-call(s32[3]{0:T(128)S(1)} %get-tuple-element.188.place_ref, bf16[2,64,256,256]{3,2,1,0:T(8,128)(2,1)S(1)} %copy-done.1, ...), custom_call_target="tpu_custom_call" | custom-call | flops 1073741824 | bytes 8388608 | tf_op jit(solution)/shard_map/force/pallas_call | solution.py:167
  80.2 7.9 %force.12 = (f32[128,1024]{1,0:T(8,128)S(1)}, f32[96,1024]{1,0:T(8,128)S(1)}, f32[32,1024]{1,0:T(8,128)S(1)}, f32[128,1024]{1,0:T(8,128)S(1)}, f32[96,1024]{1,0:T(8,128)S(1)}, /*index=5*/f32[32,1024]{1,0:T(8,128)S(1)}) custom-call(s32[3]{0:T(128)S(1)} %get-tuple-element.189.place_ref, bf16[2,64,256,256]{3,2,1,0:T(8,128)(2,1)S(1)} %copy-done.1, ...), custom_call_target="tpu_custom_call" | custom-call | flops 1073741824 | bytes 8388608 | tf_op jit(solution)/shard_map/force/pallas_call | solution.py:167
  90.6 7.9 %force.13 = (f32[128,1024]{1,0:T(8,128)S(1)}, f32[96,1024]{1,0:T(8,128)S(1)}, f32[32,1024]{1,0:T(8,128)S(1)}, f32[128,1024]{1,0:T(8,128)S(1)}, f32[96,1024]{1,0:T(8,128)S(1)}, /*index=5*/f32[32,1024]{1,0:T(8,128)S(1)}) custom-call(s32[3]{0:T(128)S(1)} %get-tuple-element.190.place_ref, bf16[2,64,256,256]{3,2,1,0:T(8,128)(2,1)S(1)} %copy-done.1, ...), custom_call_target="tpu_custom_call" | custom-call | flops 1073741824 | bytes 8388608 | tf_op jit(solution)/shard_map/force/pallas_call | solution.py:167
  105.2 7.9 %force.14 = (f32[128,1024]{1,0:T(8,128)S(1)}, f32[96,1024]{1,0:T(8,128)S(1)}, f32[32,1024]{1,0:T(8,128)S(1)}, f32[128,1024]{1,0:T(8,128)S(1)}, f32[96,1024]{1,0:T(8,128)S(1)}, /*index=5*/f32[32,1024]{1,0:T(8,128)S(1)}) custom-call(s32[3]{0:T(128)S(1)} %get-tuple-element.191.place_ref, bf16[2,64,256,256]{3,2,1,0:T(8,128)(2,1)S(1)} %copy-done.1, ...), custom_call_target="tpu_custom_call" | custom-call | flops 1073741824 | bytes 8388608 | tf_op jit(solution)/shard_map/force/pallas_call | solution.py:167
  116.7 7.9 %force.15 = (f32[128,1024]{1,0:T(8,128)S(1)}, f32[96,1024]{1,0:T(8,128)S(1)}, f32[32,1024]{1,0:T(8,128)S(1)}, f32[128,1024]{1,0:T(8,128)S(1)}, f32[96,1024]{1,0:T(8,128)S(1)}, /*index=5*/f32[32,1024]{1,0:T(8,128)S(1)}) custom-call(s32[3]{0:T(128)S(1)} %get-tuple-element.192.place_ref, bf16[2,64,256,256]{3,2,1,0:T(8,128)(2,1)S(1)} %copy-done.1, ...), custom_call_target="tpu_custom_call" | custom-call | flops 1073741824 | bytes 8388608 | tf_op jit(solution)/shard_map/force/pallas_call | solution.py:167
  130.4 8.5 %collective-permute-done.30 = f32[96,1024]{1,0:T(8,128)S(1)} collective-permute-done((f32[96,1024]{1,0:T(8,128)S(1)}, f32[96,1024]{1,0:T(8,128)S(1)}, u32[]{:S(2)}, u32[]{:S(2)}) %collective-permute-start.30) | collective-permute-done | bytes 393248 | tf_op jit(solution)/shard_map/ppermute | solution.py:445
  141.2 8.3 %collective-permute-done.31 = f32[96,1024]{1,0:T(8,128)S(1)} collective-permute-done((f32[96,1024]{1,0:T(8,128)S(1)}, f32[96,1024]{1,0:T(8,128)S(1)}, u32[]{:S(2)}, u32[]{:S(2)}) %collective-permute-start.31) | collective-permute-done | bytes 393248 | tf_op jit(solution)/shard_map/ppermute | solution.py:445
  151.8 7.9 %collective-permute-done.32 = f32[96,1024]{1,0:T(8,128)S(1)} collective-permute-done((f32[96,1024]{1,0:T(8,128)S(1)}, f32[96,1024]{1,0:T(8,128)S(1)}, u32[]{:S(2)}, u32[]{:S(2)}) %collective-permute-start.32) | collective-permute-done | bytes 393248 | tf_op jit(solution)/shard_map/ppermute | solution.py:445
  161.9 7.0 %collective-permute-done.33 = f32[96,1024]{1,0:T(8,128)S(1)} collective-permute-done((f32[96,1024]{1,0:T(8,128)S(1)}, f32[96,1024]{1,0:T(8,128)S(1)}, u32[]{:S(2)}, u32[]{:S(2)}) %collective-permute-start.33) | collective-permute-done | bytes 393248 | tf_op jit(solution)/shard_map/ppermute | solution.py:445
  171.1 7.0 %collective-permute-done.34 = f32[96,1024]{1,0:T(8,128)S(1)} collective-permute-done((f32[96,1024]{1,0:T(8,128)S(1)}, f32[96,1024]{1,0:T(8,128)S(1)}, u32[]{:S(2)}, u32[]{:S(2)}) %collective-permute-start.34) | collective-permute-done | bytes 393248 | tf_op jit(solution)/shard_map/ppermute | solution.py:445
  180.4 6.1 %collective-permute-done.35 = f32[96,1024]{1,0:T(8,128)S(1)} collective-permute-done((f32[96,1024]{1,0:T(8,128)S(1)}, f32[96,1024]{1,0:T(8,128)S(1)}, u32[]{:S(2)}, u32[]{:S(2)}) %collective-permute-start.35) | collective-permute-done | bytes 393248 | tf_op jit(solution)/shard_map/ppermute | solution.py:445
  189.2 6.6 %collective-permute-done.36.left = f32[96,1024]{1,0:T(8,128)S(1)} collective-permute-done((f32[96,1024]{1,0:T(8,128)S(1)}, f32[96,1024]{1,0:T(8,128)S(1)}, u32[]{:S(2)}, u32[]{:S(2)}) %collective-permute-start.36) | collective-permute-done | bytes 393248 | tf_op jit(solution)/shard_map/ppermute | solution.py:445
  199.4 2.9 collective-permute-done.53
  250.2 3.4 %collective-permute-start.19 = (f32[4,32,256]{2,1,0:T(8,128)S(1)}, f32[4,32,256]{2,1,0:T(8,128)S(1)}, u32[]{:S(2)}, u32[]{:S(2)}) collective-permute-start(f32[4,32,256]{2,1,0:T(8,128)S(1)} %merge.7.ends_ref), channel_id=1, source_target_pairs={{0,16},{4,20},{8,24},{12,28},{16,0},{20,4},{24,8},{28,12},{1,17},{... | collective-permute-start | bytes 393224 | tf_op jit(solution)/shard_map/ppermute | solution.py:459
  260.0 3.1 second_and_back.3
  271.1 9.7 %collective-permute-done.62.rest_3_ = f32[8,2048]{1,0:T(8,128)S(1)} collective-permute-done((f32[8,2048]{1,0:T(8,128)}, f32[8,2048]{1,0:T(8,128)S(1)}, u32[]{:S(2)}, u32[]{:S(2)}) %collective-permute-start.62) | collective-permute-done | bytes 65568 | tf_op jit(solution)/shard_map/ppermute | solution.py:452
  283.1 3.5 %collective-permute-start.63 = (f32[4,8,256]{2,1,0:T(8,128)S(1)}, f32[4,8,256]{2,1,0:T(8,128)S(1)}, u32[]{:S(2)}, u32[]{:S(2)}) collective-permute-start(f32[4,8,256]{2,1,0:T(8,128)S(1)} %get-tuple-element.164.ends_ref), channel_id=1, source_target_pairs={{0,4},{4,0},{8,12},{12,8},{16,20},{20,16},{24,28},{28,24},{1,5},{5... | collective-permute-start | bytes 98312 | tf_op jit(solution)/shard_map/ppermute | solution.py:459
  308.0 5.0 %last_back.1 = f32[64,32,256]{2,1,0:T(8,128)} custom-call(s32[2]{0:T(128)S(1)} %pad_add_fusion.place_ref, bf16[4,2,256,256]{3,2,1,0:T(8,128)(2,1)S(1)} %copy-done.10, f32[64,32,256]{2,1,0:T(8,128)S(1)} %copy-done.7, f32[32,2048]{1,0:T(8,128)S(1)} %copy-done.16, f32[32,2048]{1,0:T(8,128)} %collective-permute-done.20.rest_1_, ...), custom_call_target="tpu_custom_call" | custom-call | tf_op jit(solution)/shard_map/last_back/pallas_call | solution.py:393
  (254 shorter events, 144.6 us)
Async XLA Ops:
  32.6 16.9 %collective-permute-start.7 = (f32[128,1024]{1,0:T(8,128)S(1)}, f32[128,1024]{1,0:T(8,128)S(1)}, u32[]{:S(2)}, u32[]{:S(2)}) collective-permute-start(f32[128,1024]{1,0:T(8,128)S(1)} %get-tuple-element.95), channel_id=1, source_target_pairs={{8,0},{16,8},{24,16},{28,24},{20,28},{12,20},{4,12},{0,4},{9,1},{1... | collective-permute-start | bytes 1572872 | tf_op jit(solution)/shard_map/ppermute | solution.py:445
  35.6 15.9 %collective-permute-start = (f32[128,1024]{1,0:T(8,128)S(1)}, f32[128,1024]{1,0:T(8,128)S(1)}, u32[]{:S(2)}, u32[]{:S(2)}) collective-permute-start(f32[128,1024]{1,0:T(8,128)S(1)} %get-tuple-element.87), channel_id=1, source_target_pairs={{0,8},{8,16},{16,24},{24,28},{28,20},{20,12},{12,4},{4,0},{1,9},{9... | collective-permute-start | bytes 1572872 | tf_op jit(solution)/shard_map/ppermute | solution.py:444
  49.5 13.4 %collective-permute-start.8 = (f32[128,1024]{1,0:T(8,128)S(1)}, f32[128,1024]{1,0:T(8,128)S(1)}, u32[]{:S(2)}, u32[]{:S(2)}) collective-permute-start(f32[128,1024]{1,0:T(8,128)S(1)} %add.376), channel_id=1, source_target_pairs={{8,0},{16,8},{24,16},{28,24},{20,28},{12,20},{4,12},{0,4},{9,1},{1... | collective-permute-start | bytes 1572872 | tf_op jit(solution)/shard_map/ppermute | solution.py:445
  51.5 13.2 %collective-permute-start.1 = (f32[128,1024]{1,0:T(8,128)S(1)}, f32[128,1024]{1,0:T(8,128)S(1)}, u32[]{:S(2)}, u32[]{:S(2)}) collective-permute-start(f32[128,1024]{1,0:T(8,128)S(1)} %add.334), channel_id=1, source_target_pairs={{0,8},{8,16},{16,24},{24,28},{28,20},{20,12},{12,4},{4,0},{1,9},{9... | collective-permute-start | bytes 1572872 | tf_op jit(solution)/shard_map/ppermute | solution.py:444
  63.0 12.5 %collective-permute-start.9 = (f32[128,1024]{1,0:T(8,128)S(1)}, f32[128,1024]{1,0:T(8,128)S(1)}, u32[]{:S(2)}, u32[]{:S(2)}) collective-permute-start(f32[128,1024]{1,0:T(8,128)S(1)} %add.377), channel_id=1, source_target_pairs={{8,0},{16,8},{24,16},{28,24},{20,28},{12,20},{4,12},{0,4},{9,1},{1... | collective-permute-start | bytes 1572872 | tf_op jit(solution)/shard_map/ppermute | solution.py:445
  64.8 12.2 %collective-permute-start.2 = (f32[128,1024]{1,0:T(8,128)S(1)}, f32[128,1024]{1,0:T(8,128)S(1)}, u32[]{:S(2)}, u32[]{:S(2)}) collective-permute-start(f32[128,1024]{1,0:T(8,128)S(1)} %add.341), channel_id=1, source_target_pairs={{0,8},{8,16},{16,24},{24,28},{28,20},{20,12},{12,4},{4,0},{1,9},{9... | collective-permute-start | bytes 1572872 | tf_op jit(solution)/shard_map/ppermute | solution.py:444
  75.6 12.6 %collective-permute-start.10 = (f32[128,1024]{1,0:T(8,128)S(1)}, f32[128,1024]{1,0:T(8,128)S(1)}, u32[]{:S(2)}, u32[]{:S(2)}) collective-permute-start(f32[128,1024]{1,0:T(8,128)S(1)} %add.378), channel_id=1, source_target_pairs={{8,0},{16,8},{24,16},{28,24},{20,28},{12,20},{4,12},{0,4},{9,1},{1... | collective-permute-start | bytes 1572872 | tf_op jit(solution)/shard_map/ppermute | solution.py:445
  77.1 12.6 %collective-permute-start.3 = (f32[128,1024]{1,0:T(8,128)S(1)}, f32[128,1024]{1,0:T(8,128)S(1)}, u32[]{:S(2)}, u32[]{:S(2)}) collective-permute-start(f32[128,1024]{1,0:T(8,128)S(1)} %add.348), channel_id=1, source_target_pairs={{0,8},{8,16},{16,24},{24,28},{28,20},{20,12},{12,4},{4,0},{1,9},{9... | collective-permute-start | bytes 1572872 | tf_op jit(solution)/shard_map/ppermute | solution.py:444
  88.2 12.0 %collective-permute-start.11 = (f32[128,1024]{1,0:T(8,128)S(1)}, f32[128,1024]{1,0:T(8,128)S(1)}, u32[]{:S(2)}, u32[]{:S(2)}) collective-permute-start(f32[128,1024]{1,0:T(8,128)S(1)} %add.379), channel_id=1, source_target_pairs={{8,0},{16,8},{24,16},{28,24},{20,28},{12,20},{4,12},{0,4},{9,1},{1... | collective-permute-start | bytes 1572872 | tf_op jit(solution)/shard_map/ppermute | solution.py:445
  89.7 12.1 %collective-permute-start.4 = (f32[128,1024]{1,0:T(8,128)S(1)}, f32[128,1024]{1,0:T(8,128)S(1)}, u32[]{:S(2)}, u32[]{:S(2)}) collective-permute-start(f32[128,1024]{1,0:T(8,128)S(1)} %add.355), channel_id=1, source_target_pairs={{0,8},{8,16},{16,24},{24,28},{28,20},{20,12},{12,4},{4,0},{1,9},{9... | collective-permute-start | bytes 1572872 | tf_op jit(solution)/shard_map/ppermute | solution.py:444
  100.3 14.2 %collective-permute-start.12 = (f32[128,1024]{1,0:T(8,128)S(1)}, f32[128,1024]{1,0:T(8,128)S(1)}, u32[]{:S(2)}, u32[]{:S(2)}) collective-permute-start(f32[128,1024]{1,0:T(8,128)S(1)} %add.380), channel_id=1, source_target_pairs={{8,0},{16,8},{24,16},{28,24},{20,28},{12,20},{4,12},{0,4},{9,1},{1... | collective-permute-start | bytes 1572872 | tf_op jit(solution)/shard_map/ppermute | solution.py:445
  101.9 14.1 %collective-permute-start.5 = (f32[128,1024]{1,0:T(8,128)S(1)}, f32[128,1024]{1,0:T(8,128)S(1)}, u32[]{:S(2)}, u32[]{:S(2)}) collective-permute-start(f32[128,1024]{1,0:T(8,128)S(1)} %add.362), channel_id=1, source_target_pairs={{0,8},{8,16},{16,24},{24,28},{28,20},{20,12},{12,4},{4,0},{1,9},{9... | collective-permute-start | bytes 1572872 | tf_op jit(solution)/shard_map/ppermute | solution.py:444
  209.6 13.9 %collective-permute-start.14 = (f32[32,2048]{1,0:T(8,128)}, f32[32,2048]{1,0:T(8,128)S(1)}, u32[]{:S(2)}, u32[]{:S(2)}) collective-permute-start(f32[32,2048]{1,0:T(8,128)} %get-tuple-element.104), channel_id=1, source_target_pairs={{0,1},{1,0},{2,3},{3,2},{4,5},{5,4},{6,7},{7,6},{8,9},{9,8},{10,11... | collective-permute-start | bytes 786440 | tf_op jit(solution)/shard_map/ppermute | solution.py:452
  209.6 14.1 %collective-permute-start.15 = (f32[32,2048]{1,0:T(8,128)}, f32[32,2048]{1,0:T(8,128)S(1)}, u32[]{:S(2)}, u32[]{:S(2)}) collective-permute-start(f32[32,2048]{1,0:T(8,128)} %get-tuple-element.105), channel_id=1, source_target_pairs={{0,2},{1,3},{2,0},{3,1},{4,6},{5,7},{6,4},{7,5},{8,10},{9,11},{10,... | collective-permute-start | bytes 786440 | tf_op jit(solution)/shard_map/ppermute | solution.py:452
  211.3 12.5 %collective-permute-start.16 = (f32[32,2048]{1,0:T(8,128)}, f32[32,2048]{1,0:T(8,128)S(1)}, u32[]{:S(2)}, u32[]{:S(2)}) collective-permute-start(f32[32,2048]{1,0:T(8,128)} %get-tuple-element.106), channel_id=1, source_target_pairs={{0,3},{1,2},{2,1},{3,0},{4,7},{5,6},{6,5},{7,4},{8,11},{9,10},{10,... | collective-permute-start | bytes 786440 | tf_op jit(solution)/shard_map/ppermute | solution.py:452
  218.4 17.0 %collective-permute-start.37 = (f32[24,2048]{1,0:T(8,128)}, f32[24,2048]{1,0:T(8,128)S(1)}, u32[]{:S(2)}, u32[]{:S(2)}) collective-permute-start(f32[24,2048]{1,0:T(8,128)} %copy-done.33), channel_id=1, source_target_pairs={{0,1},{1,0},{2,3},{3,2},{4,5},{5,4},{6,7},{7,6},{8,9},{9,8},{10,11... | collective-permute-start | bytes 589832 | tf_op jit(solution)/shard_map/ppermute | solution.py:452
  231.4 13.2 %collective-permute-start.58 = (f32[32,1024]{1,0:T(8,128)}, f32[32,1024]{1,0:T(8,128)}, u32[]{:S(2)}, u32[]{:S(2)}) collective-permute-start(f32[32,1024]{1,0:T(8,128)} %add.406), channel_id=1, source_target_pairs={{8,0},{16,8},{24,16},{28,24},{20,28},{12,20},{4,12},{0,4},{9,1},{1... | collective-permute-start | bytes 393224 | tf_op jit(solution)/shard_map/ppermute | solution.py:445
  232.6 14.9 %collective-permute-start.51 = (f32[32,1024]{1,0:T(8,128)}, f32[32,1024]{1,0:T(8,128)}, u32[]{:S(2)}, u32[]{:S(2)}) collective-permute-start(f32[32,1024]{1,0:T(8,128)} %add.400), channel_id=1, source_target_pairs={{0,8},{8,16},{16,24},{24,28},{28,20},{20,12},{12,4},{4,0},{1,9},{9... | collective-permute-start | bytes 393224 | tf_op jit(solution)/shard_map/ppermute | solution.py:444
  236.1 13.1 %collective-permute-start.18 = (f32[4,32,256]{2,1,0:T(8,128)}, f32[4,32,256]{2,1,0:T(8,128)}, u32[]{:S(2)}, u32[]{:S(2)}) collective-permute-start(f32[4,32,256]{2,1,0:T(8,128)} %merge.6.ends_ref), channel_id=1, source_target_pairs={{0,8},{4,12},{8,0},{12,4},{16,24},{20,28},{24,16},{28,20},{1,9},{5... | collective-permute-start | bytes 393224 | tf_op jit(solution)/shard_map/ppermute | solution.py:459
  254.8 12.2 %collective-permute-start.41 = (f32[4,24,256]{2,1,0:T(8,128)}, f32[4,24,256]{2,1,0:T(8,128)}, u32[]{:S(2)}, u32[]{:S(2)}) collective-permute-start(f32[4,24,256]{2,1,0:T(8,128)} %merge.8.ends_ref), channel_id=1, source_target_pairs={{0,8},{4,12},{8,0},{12,4},{16,24},{20,28},{24,16},{28,20},{1,9},{5... | collective-permute-start | bytes 294920 | tf_op jit(solution)/shard_map/ppermute | solution.py:459
  265.3 28.4 %collective-permute-start.20 = (f32[32,2048]{1,0:T(8,128)}, f32[32,2048]{1,0:T(8,128)}, u32[]{:S(2)}, u32[]{:S(2)}) collective-permute-start(f32[32,2048]{1,0:T(8,128)} %get-tuple-element.110), channel_id=1, source_target_pairs={{0,1},{1,0},{2,3},{3,2},{4,5},{5,4},{6,7},{7,6},{8,9},{9,8},{10,11... | collective-permute-start | bytes 786440 | tf_op jit(solution)/shard_map/ppermute | solution.py:465
  265.3 34.2 %collective-permute-start.21 = (f32[32,2048]{1,0:T(8,128)}, f32[32,2048]{1,0:T(8,128)S(1)}, u32[]{:S(2)}, u32[]{:S(2)}) collective-permute-start(f32[32,2048]{1,0:T(8,128)} %copy-done.30), channel_id=1, source_target_pairs={{0,2},{1,3},{2,0},{3,1},{4,6},{5,7},{6,4},{7,5},{8,10},{9,11},{10,... | collective-permute-start | bytes 786440 | tf_op jit(solution)/shard_map/ppermute | solution.py:465
  267.0 34.2 %collective-permute-start.22 = (f32[32,2048]{1,0:T(8,128)}, f32[32,2048]{1,0:T(8,128)S(1)}, u32[]{:S(2)}, u32[]{:S(2)}) collective-permute-start(f32[32,2048]{1,0:T(8,128)} %copy-done.29), channel_id=1, source_target_pairs={{0,3},{1,2},{2,1},{3,0},{4,7},{5,6},{6,5},{7,4},{8,11},{9,10},{10,... | collective-permute-start | bytes 786440 | tf_op jit(solution)/shard_map/ppermute | solution.py:465
  268.2 22.2 %collective-permute-start.42 = (f32[4,24,256]{2,1,0:T(8,128)S(1)}, f32[4,24,256]{2,1,0:T(8,128)S(1)}, u32[]{:S(2)}, u32[]{:S(2)}) collective-permute-start(f32[4,24,256]{2,1,0:T(8,128)S(1)} %merge.9.ends_ref), channel_id=1, source_target_pairs={{0,16},{4,20},{8,24},{12,28},{16,0},{20,4},{24,8},{28,12},{1,17},{... | collective-permute-start | bytes 294920 | tf_op jit(solution)/shard_map/ppermute | solution.py:459
  (80 other events, 666.4 us)

commit v2 on v1

--- a/solution.py
+++ b/solution.py
@@ -14,9 +14,10 @@
 step_size = 0.25
 alpha_reach = 16.0
 highest = lax.Precision.HIGHEST
-vmem_bytes = 30 * 1024 * 1024
+vmem_bytes = 50 * 1024 * 1024
 lane = 128
-chunk_eighths = (4, 3, 1)
+chunk_eighths = (6, 2)
+near_step, far_step, ends_step = 3, 4, 5
 
 
 def split_bf16(table):
@@ -50,7 +51,15 @@
         self.groups = [c // space for c in self.chunks]
         ring = list(range(0, subj, 2)) + list(range(subj - 1, 0, -2))
         self.ring = ring
-        self.place = [ring.index(j) for j in range(subj)]
+        rows = np.zeros((subj, space, 2 * subj + 2), np.int32)
+        for at, j in enumerate(ring):
+            for k in range(subj):
+                rows[j, :, 2 * k] = ring[(at - 1 - k) % subj]
+                rows[j, :, 2 * k + 1] = ring[(at + 1 + k) % subj]
+            rows[j, :, 2 * subj] = np.arange(space)
+            rows[j, :, 2 * subj + 1] = j
+        self.place_table = rows
+        self.at_space, self.at_subj = 2 * subj, 2 * subj + 1
         forward, inverse, lam = packed_np(length)
         order = np.stack(
             [
@@ -86,15 +95,48 @@
         r = 2.0 / (centre + np.sqrt(centre * centre - 4.0))
         q = r * r
         scale = (2.0 / sigma_sq) * q / (alpha_reach * alpha_reach)
-        self.r_table = np.stack(
-            [r, scale * (1 + q) / (1 - q) ** 3, scale / (1 - q) ** 2, np.log(r)]
-        ).astype(np.float32)
+        table = np.stack([r, scale * (1 + q) / (1 - q) ** 3, scale / (1 - q) ** 2, np.log(r)])
+        self.r_tables = [
+            table[:, off : off + size]
+            .reshape(4, space, g, length)
+            .transpose(1, 0, 2, 3)
+            .astype(np.float32)
+            for off, size, g in zip(self.offs, self.chunks, self.groups)
+        ]
 
 
 def split(value):
     high = value.astype(jnp.bfloat16)
     low = (value - high.astype(jnp.float32)).astype(jnp.bfloat16)
     return high, low
+
+
+def whole(shape):
+    return pl.BlockSpec(shape, lambda at, place: (0,) * len(shape))
+
+
+def call_once(kernel, name, out_shape, place, mine, args, scratch=()):
+    at_space = place.shape[0] - 2
+    picked = [
+        pl.BlockSpec(
+            (1, *m.shape[1:]),
+            lambda at, place, n=m.ndim: (place[at_space],) + (0,) * (n - 1),
+        )
+        for m in mine
+    ]
+    return pl.pallas_call(
+        kernel,
+        out_shape=out_shape,
+        grid_spec=pltpu.PrefetchScalarGridSpec(
+            num_scalar_prefetch=1,
+            grid=(1,),
+            in_specs=picked + [whole(a.shape) for a in args],
+            out_specs=jax.tree.map(lambda o: whole(o.shape), out_shape),
+            scratch_shapes=scratch,
+        ),
+        compiler_params=params(),
+        name=name,
+    )(place, *[jnp.asarray(m) for m in mine], *args)
 
 
 def params(**kw):
@@ -156,12 +198,12 @@
         transform(outs[n:])
 
 
-def force_blocks(plan, place, warped, images, jac):
+def force_blocks(plan, k, place, warped, images, jac):
     count, xl, _, length = warped.shape
     yh = plan.yl // 2
-    step_x = min(16, xl)
+    step_x = xl
     source = pl.BlockSpec(
-        (count, step_x, yh, length), lambda way, at, place: (0, at, 2 * place[way] + way, 0)
+        (count, step_x, yh, length), lambda way, at, place: (0, at, 2 * place[2 * k + way] + way, 0)
     )
     shapes = [jax.ShapeDtypeStruct((c, plan.half), jnp.float32) for c in plan.chunks] * 2
     outs = pl.pallas_call(
@@ -175,7 +217,7 @@
                 source,
                 source,
                 pl.BlockSpec((length, length), lambda way, at, place: (0, 0)),
-                pl.BlockSpec((1, length, 3 * length), lambda way, at, place: (place[2], 0, 0)),
+                pl.BlockSpec((1, length, 3 * length), lambda way, at, place: (place[plan.at_space], 0, 0)),
             ],
             out_specs=[pl.BlockSpec(s.shape, lambda way, at, place: (0, 0)) for s in shapes],
             scratch_shapes=[pltpu.VMEM((length // lane, xl * yh, lane), jnp.float32)],
@@ -192,25 +234,27 @@
     return outs[:n], outs[n:]
 
 
-def join_kernel(plan, g, right, right_local, left, left_local, *outs):
+def join_kernel(plan, g, place_ref, right, right_local, left, left_local, *outs):
     for d, out in enumerate(outs):
         rows = slice(d * g, (d + 1) * g)
         out[:, : plan.half] = right[rows] + right_local[rows]
         out[:, plan.half :] = left[rows] + left_local[rows]
 
 
-def join(plan, g, right, right_local, left, left_local):
-    return pl.pallas_call(
+def join(plan, g, place, right, right_local, left, left_local):
+    return call_once(
         functools.partial(join_kernel, plan, g),
-        out_shape=[jax.ShapeDtypeStruct((g, plan.lanes), jnp.float32)] * plan.space,
-        compiler_params=params(),
-        name="join",
-    )(right, right_local, left, left_local)
-
-
-def forward_kernel(plan, g, place_ref, w_ref, r_ref, *rest):
+        "join",
+        [jax.ShapeDtypeStruct((g, plan.lanes), jnp.float32)] * plan.space,
+        place,
+        [],
+        [right, right_local, left, left_local],
+    )
+
+
+def forward_kernel(plan, g, place_ref, r_ref, w_ref, *rest):
     pieces, f_ref, ends_ref = rest[: plan.space], rest[-2], rest[-1]
-    me = place_ref[0]
+    me = place_ref[plan.at_space]
     total = None
     for d, piece in enumerate(pieces):
         lines = jnp.concatenate(
@@ -221,7 +265,7 @@
         term = jnp.dot(both, w_ref[me ^ d], preferred_element_type=jnp.float32)
         total = term if total is None else total + term
     f_ref[...] = total
-    r = r_ref[0]
+    r = r_ref[0, 0]
     length = plan.length
 
     def line(y):
@@ -233,98 +277,51 @@
     for y in range(plan.yl):
         w = r * (w + v)
         v = line(y) + r * v
-    ends_ref[0], ends_ref[1] = v, w
+    ends_ref[:, :length], ends_ref[:, length : 2 * length] = v, w
     v, w = zero, zero
     for y in range(plan.yl - 1, -1, -1):
         v = v + line(y)
         w = r * (w + v)
         v = r * v
-    ends_ref[2], ends_ref[3] = v, w
-
-
-def forward_lines(plan, g, place, r_tab, pieces):
-    rows = plan.tiles * g
-    return pl.pallas_call(
+    ends_ref[:, 2 * length : 3 * length], ends_ref[:, 3 * length :] = v, w
+
+
+def forward_lines(plan, c, place, pieces):
+    g = plan.groups[c]
+    return call_once(
         functools.partial(forward_kernel, plan, g),
-        out_shape=[
-            jax.ShapeDtypeStruct((rows, plan.ty * plan.length), jnp.float32),
-            jax.ShapeDtypeStruct((4, g, plan.length), jnp.float32),
+        "first_forward",
+        [
+            jax.ShapeDtypeStruct((plan.tiles * g, plan.ty * plan.length), jnp.float32),
+            jax.ShapeDtypeStruct((g, 4 * plan.length), jnp.float32),
         ],
-        in_specs=[pl.BlockSpec(memory_space=pltpu.SMEM)]
-        + [pl.BlockSpec(memory_space=pltpu.VMEM)] * (2 + plan.space),
-        out_specs=[pl.BlockSpec(memory_space=pltpu.VMEM)] * 2,
-        compiler_params=params(),
-        name="first_forward",
-    )(place, jnp.asarray(plan.w_table), r_tab, *pieces)
-
-
-def combine(ends, other, right, power, span):
-    hi = [jnp.where(right, ends[i], other[i]) for i in range(4)]
-    lo = [jnp.where(right, other[i], ends[i]) for i in range(4)]
-    return (
-        hi[0] + power * lo[0],
-        hi[1] + power * (lo[1] + span * lo[0]),
-        lo[2] + power * hi[2],
-        lo[3] + power * (hi[3] + span * hi[2]),
-    )
-
-
-def merge_kernel(plan, stage, place_ref, r_ref, ends_ref, other_ref, out_ref):
-    span = float(plan.yl << stage)
-    right = (place_ref[0] >> stage) % 2 == 1
-    power = jnp.exp(span * r_ref[3])
-    ends = [ends_ref[i] for i in range(4)]
-    other = [other_ref[i] for i in range(4)]
-    for i, value in enumerate(combine(ends, other, right, power, span)):
-        out_ref[i] = value
-
-
-def merge(plan, stage, place, r_tab, ends, other):
-    return pl.pallas_call(
-        functools.partial(merge_kernel, plan, stage),
-        out_shape=jax.ShapeDtypeStruct(ends.shape, jnp.float32),
-        in_specs=[pl.BlockSpec(memory_space=pltpu.SMEM)]
-        + [pl.BlockSpec(memory_space=pltpu.VMEM)] * 3,
-        out_specs=pl.BlockSpec(memory_space=pltpu.VMEM),
-        compiler_params=params(),
-        name="merge",
-    )(place, r_tab, ends, other)
-
-
-def backward_kernel(plan, g, stages, place_ref, v_ref, r_ref, f_ref, ends_ref, *rest):
-    others, outs, u_ref = rest[:stages], rest[stages:-1], rest[-1]
-    me, block = place_ref[0], place_ref[1]
+        place,
+        [plan.r_tables[c]],
+        [jnp.asarray(plan.w_table), *pieces],
+    )
+
+
+def backward_kernel(plan, g, place_ref, r_ref, v_ref, f_ref, *rest):
+    ends_refs, outs, u_ref = rest[: plan.subj], rest[plan.subj : -1], rest[-1]
+    me, block = place_ref[plan.at_space], place_ref[plan.at_subj]
     length = plan.length
-    r, alpha, beta, log_r = r_ref[0], r_ref[1], r_ref[2], r_ref[3]
-    ends = [ends_ref[i] for i in range(4)]
+    r, alpha, beta, log_r = (r_ref[0, i] for i in range(4))
+    full = jnp.exp(float(length) * log_r)
+    once = 1.0 / (1.0 - full)
+    again = float(length) * full * once
     zero = jnp.zeros_like(r)
     carry = [zero] * 4
-    for stage in range(stages):
-        other = [others[stage][i] for i in range(4)]
-        size = 1 << stage
-        right = (block >> stage) % 2 == 1
-        inside = block % size
-        before = (inside * plan.yl).astype(jnp.float32)
-        after = ((size - 1 - inside) * plan.yl).astype(jnp.float32)
-        reach = jnp.where(right, before, after)
-        power = jnp.exp(reach * log_r)
+    for h, ref in enumerate(ends_refs):
+        source = block if h == 0 else place_ref[h - 1]
         for i in (0, 2):
-            take = jnp.where(right, 1.0, 0.0) if i == 0 else jnp.where(right, 0.0, 1.0)
-            carry[i] = carry[i] + take * (power * other[i])
-            carry[i + 1] = carry[i + 1] + take * (power * (other[i + 1] + reach * other[i]))
-        if stage == stages - 1:
-            span = float(plan.yl << stage)
-            ends = combine(ends, other, right, jnp.exp(span * log_r), span)
-    full = jnp.exp(float(length) * log_r)
-    inverse = 1.0 / (1.0 - full)
-    for i in (0, 2):
-        v = ends[i] * inverse
-        w = (ends[i + 1] + full * (float(length) * v)) * inverse
-        reach = (block if i == 0 else plan.subj - 1 - block) * plan.yl
-        reach = reach.astype(jnp.float32)
-        power = jnp.exp(reach * log_r)
-        carry[i] = carry[i] + power * v
-        carry[i + 1] = carry[i + 1] + power * (w + reach * v)
+            between = block - 1 - source if i == 0 else source - 1 - block
+            between = jnp.where(between < 0, between + plan.subj, between)
+            reach = (between * plan.yl).astype(jnp.float32)
+            power = once * jnp.exp(reach * log_r)
+            v = ref[:g, i * length : (i + 1) * length]
+            w = ref[:g, (i + 1) * length : (i + 2) * length]
+            carry[i] = carry[i] + power * v
+            carry[i + 1] = carry[i + 1] + power * (w + (reach + again) * v)
 
     def line(y):
         t, a = y // plan.ty, y % plan.ty
@@ -349,25 +346,23 @@
             out[:, t * lane : (t + 1) * lane] = back[t * g : (t + 1) * g]
 
 
-def backward_lines(plan, g, place, r_tab, f, ends, others):
-    stages = len(others)
-    return pl.pallas_call(
-        functools.partial(backward_kernel, plan, g, stages),
-        out_shape=[jax.ShapeDtypeStruct((g, plan.lanes), jnp.float32)] * plan.space,
-        in_specs=[pl.BlockSpec(memory_space=pltpu.SMEM)]
-        + [pl.BlockSpec(memory_space=pltpu.VMEM)] * (4 + stages),
-        out_specs=[pl.BlockSpec(memory_space=pltpu.VMEM)] * plan.space,
-        scratch_shapes=[pltpu.VMEM(f.shape, jnp.float32)],
-        compiler_params=params(),
-        name="second_and_back",
-    )(place, jnp.asarray(plan.v_table), r_tab, f, ends, *others)
-
-
-def finish_kernel(plan, y_step, place_ref, i_ref, velocity, *rest):
+def backward_lines(plan, c, place, f, ends):
+    g = plan.groups[c]
+    return call_once(
+        functools.partial(backward_kernel, plan, g),
+        "second_and_back",
+        [jax.ShapeDtypeStruct((g, plan.lanes), jnp.float32)] * plan.space,
+        place,
+        [plan.r_tables[c]],
+        [jnp.asarray(plan.v_table), f, *ends],
+        scratch=[pltpu.VMEM(f.shape, jnp.float32)],
+    )
+
+
+def finish_kernel(plan, y_step, fresh, place_ref, high_ref, low_ref, base, *rest):
     pieces, out, field = rest[:-2], rest[-2], rest[-1]
     length, xl = plan.length, plan.xl
-    high_table, low_table = i_ref[0, 0], i_ref[0, 1]
-    table = jnp.concatenate([high_table, high_table, low_table], axis=0)
+    table = jnp.concatenate([high_ref[0], high_ref[0], low_ref[0]], axis=0)
     for t in range(y_step // plan.ty):
         columns = jnp.concatenate([p[:, t * lane : (t + 1) * lane] for p in pieces], axis=0)
         high, low = split(columns.T)
@@ -381,91 +376,137 @@
                 ]
     for h in range(length // lane):
         cols = slice(h * lane, (h + 1) * lane)
-        vel = velocity[:, :, cols]
-        smoothed = field[h].reshape(xl, y_step, lane)
-        out[:, :, cols] = vel - step_size * (2.0 * vel - smoothed)
-
-
-def finish(plan, place, velocity, pieces):
-    xl, yl, length = velocity.shape
+        old = base[:, :, cols]
+        if fresh:
+            old = old - (2.0 * step_size) * old
+        out[:, :, cols] = old + step_size * field[h].reshape(xl, y_step, lane)
+
+
+def finish(plan, cs, place, base, fresh, pieces):
+    xl, yl, length = base.shape
     y_step = 8
     width = y_step * xl
+    rows = slice(plan.offs[cs[0]], plan.offs[cs[-1]] + plan.chunks[cs[-1]])
+    high, low = (jnp.asarray(plan.i_table[:, i, rows]) for i in range(2))
+    count = high.shape[1]
+    table = pl.BlockSpec((1, count, length), lambda at, place: (place[plan.at_space], 0, 0))
+    block = pl.BlockSpec((xl, y_step, length), lambda at, place: (0, at, 0))
     return pl.pallas_call(
-        functools.partial(finish_kernel, plan, y_step),
-        out_shape=jax.ShapeDtypeStruct(velocity.shape, jnp.float32),
+        functools.partial(finish_kernel, plan, y_step, fresh),
+        out_shape=jax.ShapeDtypeStruct(base.shape, jnp.float32),
         grid_spec=pltpu.PrefetchScalarGridSpec(
             num_scalar_prefetch=1,
             grid=(yl // y_step,),
-            in_specs=[
-                pl.BlockSpec((1, 2, length, length), lambda at, place: (place[0], 0, 0, 0)),
-                pl.BlockSpec((xl, y_step, length), lambda at, place: (0, at, 0)),
-            ]
+            in_specs=[table, table, block]
             + [pl.BlockSpec((p.shape[0], width), lambda at, place: (0, at)) for p in pieces],
-            out_specs=pl.BlockSpec((xl, y_step, length), lambda at, place: (0, at, 0)),
+            out_specs=block,
             scratch_shapes=[pltpu.VMEM((length // lane, xl * y_step, lane), jnp.float32)],
         ),
         compiler_params=params(),
         name="last_back",
-    )(place, jnp.asarray(plan.i_table), velocity, *pieces)
+    )(place, high, low, base, *pieces)
+
+
+def tie(first, second):
+    return lax.optimization_barrier((first, second))
+
+
+def over_space(plan, pieces):
+    moved = [
+        lax.ppermute(pieces[d], "space", [(i, i ^ d) for i in range(plan.space)])
+        for d in range(1, plan.space)
+    ]
+    return [pieces[0], *moved]
 
 
 def ring_body(plan, template_warped, subject_images, jacobians, velocity):
-    subj, space = plan.subj, plan.space
+    subj = plan.subj
     j, s = lax.axis_index("subj"), lax.axis_index("space")
-    ring = jnp.asarray(plan.ring, jnp.int32)
-    at = jnp.asarray(plan.place, jnp.int32)[j]
-    place = jnp.stack([s, j]).astype(jnp.int32)
+    table = plan.place_table
+    place = lax.dynamic_slice(jnp.asarray(table), (j, s, 0), (1, 1, table.shape[2])).reshape(-1)
     to_right = [(plan.ring[i], plan.ring[(i + 1) % subj]) for i in range(subj)]
     to_left = [(b, a) for a, b in to_right]
-    chunks = range(len(plan.chunks))
-    r_tabs = [
-        lax.dynamic_slice_in_dim(jnp.asarray(plan.r_table), off + s * g, g, axis=1)
-        for off, g in zip(plan.offs, plan.groups)
+
+    local = [
+        force_blocks(plan, k, place, template_warped, subject_images, jacobians)
+        for k in range(subj)
     ]
 
-    local = []
-    for k in range(subj):
-        blocks = jnp.stack([ring[(at - 1 - k) % subj], ring[(at + 1 + k) % subj], s])
-        local.append(
-            force_blocks(
-                plan, blocks.astype(jnp.int32), template_warped, subject_images, jacobians
-            )
-        )
-
-    stages = subj.bit_length() - 1
-    gate = None
-    finished = []
-    for c in chunks:
-        g = plan.groups[c]
-        right, left = local[0][0][c], local[0][1][c]
-        if gate is not None:
-            right, left, _ = lax.optimization_barrier((right, left, gate))
+    def ring(c, beside):
+        size = plan.chunks[c]
+        right, left, extra = local[0][0][c], local[0][1][c], ()
         for k in range(1, subj):
+            (right, left), extra = beside(k, (right, left))
+            if extra:
+                right = jnp.concatenate([right, extra[0]])
+                left = jnp.concatenate([left, extra[1]])
             right = lax.ppermute(right, "subj", to_right)
             left = lax.ppermute(left, "subj", to_left)
+            if extra:
+                arrived.append((right[size:], left[size:]))
             if k < subj - 1:
-                right = right + local[k][0][c]
-                left = left + local[k][1][c]
-        pieces = join(plan, g, right, local[-1][0][c], left, local[-1][1][c])
-        gate = pieces[0]
-        pieces = [pieces[0]] + [
-            lax.ppermute(pieces[d], "space", [(i, i ^ d) for i in range(space)])
-            for d in range(1, space)
-        ]
-        f, ends = forward_lines(plan, g, place, r_tabs[c], pieces)
-        others = []
-        for stage in range(stages):
-            size = 1 << stage
-            other = lax.ppermute(ends, "subj", [(i, i ^ size) for i in range(subj)])
-            others.append(other)
-            if stage < stages - 1:
-                ends = merge(plan, stage, place[1:], r_tabs[c], ends, other)
-        pieces = backward_lines(plan, g, place, r_tabs[c], f, ends, others)
-        finished += [pieces[0]] + [
-            lax.ppermute(pieces[d], "space", [(i, i ^ d) for i in range(space)])
-            for d in range(1, space)
-        ]
-    return finish(plan, place, velocity, finished)
+                right = right[:size] + local[k][0][c]
+                left = left[:size] + local[k][1][c]
+        return join(
+            plan, plan.groups[c], place, right, local[-1][0][c], left, local[-1][1][c]
+        )
+
+    def more_hops(own):
+        right, left = arrived[-1] if arrived else (own, own)
+        while len(arrived) < subj // 2:
+            right = lax.ppermute(right, "subj", to_right)
+            if len(arrived) < subj // 2 - 1:
+                left = lax.ppermute(left, "subj", to_left)
+            arrived.append((right, left))
+        flat = [own] + [e for pair in arrived for e in pair]
+        return flat[:subj]
+
+    count = len(plan.chunks)
+    base, fresh = velocity, True
+    waiting = None
+    pieces = None
+    for c in range(count):
+        arrived = []
+        held = {}
+
+        def beside(k, both):
+            if c == 0:
+                return both, ()
+            if k == 1:
+                both, held["own"] = tie(both, pieces[0])
+                moved = over_space(plan, [held["own"], *pieces[1:]])[1:]
+                held["near"], held["far"] = moved[:-1], moved[-1:]
+            if k == near_step:
+                both, held["near"] = tie(both, held["near"])
+            if k == far_step:
+                both, held["far"] = tie(both, held["far"])
+                all_pieces = [held["own"], *held["near"], *held["far"]]
+                held["lines"] = forward_lines(plan, c - 1, place, all_pieces)
+            if k == ends_step:
+                both, held["lines"] = tie(both, held["lines"])
+            if k < ends_step or len(arrived) >= subj // 2:
+                return both, ()
+            own = held["lines"][1]
+            return both, (arrived[-1] if arrived else (own, own))
+
+        new_pieces = ring(c, beside)
+        if c > 0:
+            f, own = held["lines"]
+            new_own, f = tie(new_pieces[0], f)
+            new_pieces = [new_own, *new_pieces[1:]]
+            back = backward_lines(plan, c - 1, place, f, more_hops(own))
+            finished = over_space(plan, back)
+            if c < count - 1:
+                base, fresh = finish(plan, [c - 1], place, base, fresh, finished), False
+        pieces = new_pieces
+    arrived = []
+    f, own = forward_lines(plan, count - 1, place, over_space(plan, pieces))
+    ends = more_hops(own)
+    if count > 1:
+        f, finished = tie(f, finished)
+        base, fresh = finish(plan, [count - 2], place, base, fresh, finished), False
+    back = backward_lines(plan, count - 1, place, f, ends)
+    return finish(plan, [count - 1], place, base, fresh, over_space(plan, back))
 
 
 def smoothing_symbol(first, second, third, length):
@@ -527,6 +568,7 @@
         and xl >= 16
         and lane % xl == 0
         and length // 8 // space % 8 == 0
+        and yl * xl == 8 * length
     )
     if not fits:
         return transposing_body(template_warped, subject_images, jacobians, velocity)

time: 315 us -> 250 us (0.79)
  waiting for transfers between devices: 90.9 us -> 125 us
  starting transfers between devices: 74.9 us -> 47.7 us
  local copies, waits for them, and re-layouts: 31.7 us -> 5.59 us
  Pallas kernels: 86.1 us -> 68.6 us
  other arithmetic: 18.2 us -> 1.89 us
  between operations: 11.3 us -> 0.47 us
    ppermute x69 -> x48, waiting for transfers between devices: 90.9 us -> 125 us  [the longest x14 83.3 us: ring(): left = lax.ppermute(left, 'subj', to_left)]
    ppermute x69 -> x48, starting transfers between devices: 74.9 us -> 47.7 us  [the longest x14 21.5 us: ring(): left = lax.ppermute(left, 'subj', to_left)]
    unnamed x70 -> x24, local copies, waits for them, and re-layouts: 25.9 us -> 4.82 us
    pallas_call x8, Pallas kernels: 63.4 us -> 42.6 us  [force_blocks(): pl.pallas_call(functools.partial(force_kernel, plan, step_x), out_shape=s...]
    another operation x5 -> x0, other arithmetic: 10.4 us -> none  [the longest x4 10.3 us: ring_body(): jnp.stack([ring[(at - 1 - k) % subj], ring[(at + 1 + k) % subj], s])]
    add x36 -> x24, other arithmetic: 7.77 us -> 1.67 us  [the longest x12 0.84 us: ring(): left = left[:size] + local[k][1][c]]
    dynamic_slice x5 -> x0, local copies, waits for them, and re-layouts: 5.85 us -> none  [the longest x3 2.61 us: ring_body(): lax.dynamic_slice_in_dim(jnp.asarray(plan.r_table), off + s * g, g, axis=1)]
    pallas_call x16 -> x8, Pallas kernels: 22.7 us -> 26 us  [the longest x6 16.4 us: call_once(): pl.pallas_call(kernel, out_shape=out_shape, grid_spec=pltpu.PrefetchScala...]
  transfers between devices with their start and end apart: 69 -> 48, of which waited for: 30 -> 24; matrix products, arithmetic and copies ran while one was open for 6% -> 1% of each run, Pallas kernels for 23% -> 22%
where the time goes in v2:
time: 250 us
  waiting for transfers between devices  125 us (50%)
  Pallas kernels  68.6 us (27%)
  starting transfers between devices  47.7 us (19%)
  local copies, waits for them, and re-layouts  5.59 us (2%)
    ppermute x14, waiting for transfers between devices, ring(): left = lax.ppermute(left, 'subj', to_left)  83.3 us
    pallas_call x8, Pallas kernels, force_blocks(): pl.pallas_call(functools.partial(force_kernel, plan, step_x), out_shape=s...  42.6 us
    ppermute x14, waiting for transfers between devices, ring(): right = lax.ppermute(right, 'subj', to_right)  29 us
    ppermute x14, starting transfers between devices, ring(): left = lax.ppermute(left, 'subj', to_left)  21.5 us
    pallas_call x6, Pallas kernels, call_once(): pl.pallas_call(kernel, out_shape=out_shape, grid_spec=pltpu.PrefetchScala...  16.4 us
    ppermute x14, starting transfers between devices, ring(): right = lax.ppermute(right, 'subj', to_right)  10.8 us
    ppermute x5, waiting for transfers between devices, more_hops(): right = lax.ppermute(right, 'subj', to_right)  9.91 us
    pallas_call x2, Pallas kernels, finish(): pl.pallas_call(functools.partial(finish_kernel, plan, y_step, fresh), out...  9.56 us
  transfers between devices with their start and end apart: 48, of which 24 were waited for; matrix products, arithmetic and copies ran while one was open for 1% of the time, Pallas kernels for 22%

profile of v2, /device:TPU:0, one launch (start us, length us, event | category | flops | bytes accessed | tf_op | source)
XLA Modules:
  0.0 249.6 jit_solution(13509327426037088682)
XLA Ops:
  3.0 5.3 %force.8 = (f32[192,1024]{1,0:T(8,128)S(1)}, f32[64,1024]{1,0:T(8,128)S(1)}, f32[192,1024]{1,0:T(8,128)S(1)}, f32[64,1024]{1,0:T(8,128)S(1)}) custom-call(s32[18]{0:T(128)S(1)} %dynamic-slice_bitcast_fusion.place_ref, bf16[2,64,256,256]{3,2,1,0:T(8,128)(2,1)} %warped.15, bf16[2,64,256,256]{3,2,1,0:T(8,128)(2,1)} %images.15, bf16[2,64,256,256]{3,2,1,0:T(8,128)(2,1)} %jac.15, ...), custom_call_target="tpu_custom_call" | custom-call | flops 1073741824 | bytes 8388608 | tf_op jit(solution)/shard_map/force/pallas_call | solution.py:209
  11.5 5.3 %force.9 = (f32[192,1024]{1,0:T(8,128)S(1)}, f32[64,1024]{1,0:T(8,128)S(1)}, f32[192,1024]{1,0:T(8,128)S(1)}, f32[64,1024]{1,0:T(8,128)S(1)}) custom-call(s32[18]{0:T(128)S(1)} %dynamic-slice_bitcast_fusion.place_ref, bf16[2,64,256,256]{3,2,1,0:T(8,128)(2,1)} %warped.15, bf16[2,64,256,256]{3,2,1,0:T(8,128)(2,1)} %images.15, bf16[2,64,256,256]{3,2,1,0:T(8,128)(2,1)} %jac.15, ...), custom_call_target="tpu_custom_call" | custom-call | flops 1073741824 | bytes 8388608 | tf_op jit(solution)/shard_map/force/pallas_call | solution.py:209
  16.8 12.2 %collective-permute-done.7 = f32[192,1024]{1,0:T(8,128)S(1)} collective-permute-done((f32[192,1024]{1,0:T(8,128)S(1)}, f32[192,1024]{1,0:T(8,128)S(1)}, u32[]{:S(2)}, u32[]{:S(2)}) %collective-permute-start.7) | collective-permute-done | bytes 786464 | tf_op jit(solution)/shard_map/ppermute | solution.py:444
  31.3 5.3 %force.10 = (f32[192,1024]{1,0:T(8,128)S(1)}, f32[64,1024]{1,0:T(8,128)S(1)}, f32[192,1024]{1,0:T(8,128)S(1)}, f32[64,1024]{1,0:T(8,128)S(1)}) custom-call(s32[18]{0:T(128)S(1)} %dynamic-slice_bitcast_fusion.place_ref, bf16[2,64,256,256]{3,2,1,0:T(8,128)(2,1)} %warped.15, bf16[2,64,256,256]{3,2,1,0:T(8,128)(2,1)} %images.15, bf16[2,64,256,256]{3,2,1,0:T(8,128)(2,1)} %jac.15, ...), custom_call_target="tpu_custom_call" | custom-call | flops 1073741824 | bytes 8388608 | tf_op jit(solution)/shard_map/force/pallas_call | solution.py:209
  36.7 11.2 %collective-permute-done.8 = f32[192,1024]{1,0:T(8,128)S(1)} collective-permute-done((f32[192,1024]{1,0:T(8,128)S(1)}, f32[192,1024]{1,0:T(8,128)S(1)}, u32[]{:S(2)}, u32[]{:S(2)}) %collective-permute-start.8) | collective-permute-done | bytes 786464 | tf_op jit(solution)/shard_map/ppermute | solution.py:444
  50.2 5.3 %force.11 = (f32[192,1024]{1,0:T(8,128)S(1)}, f32[64,1024]{1,0:T(8,128)S(1)}, f32[192,1024]{1,0:T(8,128)S(1)}, f32[64,1024]{1,0:T(8,128)S(1)}) custom-call(s32[18]{0:T(128)S(1)} %dynamic-slice_bitcast_fusion.place_ref, bf16[2,64,256,256]{3,2,1,0:T(8,128)(2,1)} %warped.15, bf16[2,64,256,256]{3,2,1,0:T(8,128)(2,1)} %images.15, bf16[2,64,256,256]{3,2,1,0:T(8,128)(2,1)} %jac.15, ...), custom_call_target="tpu_custom_call" | custom-call | flops 1073741824 | bytes 8388608 | tf_op jit(solution)/shard_map/force/pallas_call | solution.py:209
  55.6 10.3 %collective-permute-done.9 = f32[192,1024]{1,0:T(8,128)S(1)} collective-permute-done((f32[192,1024]{1,0:T(8,128)S(1)}, f32[192,1024]{1,0:T(8,128)S(1)}, u32[]{:S(2)}, u32[]{:S(2)}) %collective-permute-start.9) | collective-permute-done | bytes 786464 | tf_op jit(solution)/shard_map/ppermute | solution.py:444
  68.2 5.3 %force.12 = (f32[192,1024]{1,0:T(8,128)S(1)}, f32[64,1024]{1,0:T(8,128)S(1)}, f32[192,1024]{1,0:T(8,128)S(1)}, f32[64,1024]{1,0:T(8,128)S(1)}) custom-call(s32[18]{0:T(128)S(1)} %dynamic-slice_bitcast_fusion.place_ref, bf16[2,64,256,256]{3,2,1,0:T(8,128)(2,1)} %warped.15, bf16[2,64,256,256]{3,2,1,0:T(8,128)(2,1)} %images.15, bf16[2,64,256,256]{3,2,1,0:T(8,128)(2,1)} %jac.15, ...), custom_call_target="tpu_custom_call" | custom-call | flops 1073741824 | bytes 8388608 | tf_op jit(solution)/shard_map/force/pallas_call | solution.py:209
  73.5 10.0 %collective-permute-done.10 = f32[192,1024]{1,0:T(8,128)S(1)} collective-permute-done((f32[192,1024]{1,0:T(8,128)S(1)}, f32[192,1024]{1,0:T(8,128)S(1)}, u32[]{:S(2)}, u32[]{:S(2)}) %collective-permute-start.10) | collective-permute-done | bytes 786464 | tf_op jit(solution)/shard_map/ppermute | solution.py:444
  86.1 5.3 %force.13 = (f32[192,1024]{1,0:T(8,128)S(1)}, f32[64,1024]{1,0:T(8,128)S(1)}, f32[192,1024]{1,0:T(8,128)S(1)}, f32[64,1024]{1,0:T(8,128)S(1)}) custom-call(s32[18]{0:T(128)S(1)} %dynamic-slice_bitcast_fusion.place_ref, bf16[2,64,256,256]{3,2,1,0:T(8,128)(2,1)} %warped.15, bf16[2,64,256,256]{3,2,1,0:T(8,128)(2,1)} %images.15, bf16[2,64,256,256]{3,2,1,0:T(8,128)(2,1)} %jac.15, ...), custom_call_target="tpu_custom_call" | custom-call | flops 1073741824 | bytes 8388608 | tf_op jit(solution)/shard_map/force/pallas_call | solution.py:209
  91.5 9.8 %collective-permute-done.11 = f32[192,1024]{1,0:T(8,128)S(1)} collective-permute-done((f32[192,1024]{1,0:T(8,128)S(1)}, f32[192,1024]{1,0:T(8,128)S(1)}, u32[]{:S(2)}, u32[]{:S(2)}) %collective-permute-start.11) | collective-permute-done | bytes 786464 | tf_op jit(solution)/shard_map/ppermute | solution.py:444
  103.6 5.3 %force.14 = (f32[192,1024]{1,0:T(8,128)S(1)}, f32[64,1024]{1,0:T(8,128)S(1)}, f32[192,1024]{1,0:T(8,128)S(1)}, f32[64,1024]{1,0:T(8,128)S(1)}) custom-call(s32[18]{0:T(128)S(1)} %dynamic-slice_bitcast_fusion.place_ref, bf16[2,64,256,256]{3,2,1,0:T(8,128)(2,1)} %warped.15, bf16[2,64,256,256]{3,2,1,0:T(8,128)(2,1)} %images.15, bf16[2,64,256,256]{3,2,1,0:T(8,128)(2,1)} %jac.15, ...), custom_call_target="tpu_custom_call" | custom-call | flops 1073741824 | bytes 8388608 | tf_op jit(solution)/shard_map/force/pallas_call | solution.py:209
  109.0 10.0 %collective-permute-done.12 = f32[192,1024]{1,0:T(8,128)S(1)} collective-permute-done((f32[192,1024]{1,0:T(8,128)S(1)}, f32[192,1024]{1,0:T(8,128)S(1)}, u32[]{:S(2)}, u32[]{:S(2)}) %collective-permute-start.12) | collective-permute-done | bytes 786464 | tf_op jit(solution)/shard_map/ppermute | solution.py:444
  121.3 5.3 %force.15 = (f32[192,1024]{1,0:T(8,128)S(1)}, f32[64,1024]{1,0:T(8,128)S(1)}, f32[192,1024]{1,0:T(8,128)S(1)}, f32[64,1024]{1,0:T(8,128)S(1)}) custom-call(s32[18]{0:T(128)S(1)} %dynamic-slice_bitcast_fusion.place_ref, bf16[2,64,256,256]{3,2,1,0:T(8,128)(2,1)} %warped.15, bf16[2,64,256,256]{3,2,1,0:T(8,128)(2,1)} %images.15, bf16[2,64,256,256]{3,2,1,0:T(8,128)(2,1)} %jac.15, ...), custom_call_target="tpu_custom_call" | custom-call | flops 1073741824 | bytes 8388608 | tf_op jit(solution)/shard_map/force/pallas_call | solution.py:209
  127.5 7.4 %collective-permute-done.13.left = f32[192,1024]{1,0:T(8,128)S(1)} collective-permute-done((f32[192,1024]{1,0:T(8,128)S(1)}, f32[192,1024]{1,0:T(8,128)S(1)}, u32[]{:S(2)}, u32[]{:S(2)}) %collective-permute-start.13) | collective-permute-done | bytes 786464 | tf_op jit(solution)/shard_map/ppermute | solution.py:444
  145.9 4.2 %collective-permute-done.17 = f32[64,1024]{1,0:T(8,128)S(1)} collective-permute-done((f32[64,1024]{1,0:T(8,128)S(1)}, f32[64,1024]{1,0:T(8,128)S(1)}, u32[]{:S(2)}, u32[]{:S(2)}) %collective-permute-start.17) | collective-permute-done | bytes 262176 | tf_op jit(solution)/shard_map/ppermute | solution.py:444
  153.6 5.1 %collective-permute-done.21 = f32[64,1024]{1,0:T(8,128)S(1)} collective-permute-done((f32[64,1024]{1,0:T(8,128)S(1)}, f32[64,1024]{1,0:T(8,128)S(1)}, u32[]{:S(2)}, u32[]{:S(2)}) %collective-permute-start.21) | collective-permute-done | bytes 262176 | tf_op jit(solution)/shard_map/ppermute | solution.py:444
  162.2 5.0 %first_forward.2 = (f32[768,512]{1,0:T(8,128)}, f32[48,1024]{1,0:T(8,128)S(1)}) custom-call(s32[18]{0:T(128)S(1)} %dynamic-slice_bitcast_fusion.place_ref, f32[4,4,48,256]{3,2,1,0:T(8,128)S(1)} %copy-done.5, bf16[4,384,512]{2,1,0:T(8,128)(2,1)} %constant.40.clone.w_ref, f32[48,2048]{1,0:T(8,128)S(1)} %get-tuple-element.114.rest_0_, ...), custom_call_target="tpu_custom_call" | custom-call | tf_op jit(solution)/shard_map/first_forward/pallas_call | solution.py:127
  171.1 8.2 %collective-permute-done.25 = f32[112,1024]{1,0:T(8,128)S(1)} collective-permute-done((f32[112,1024]{1,0:T(8,128)S(1)}, f32[112,1024]{1,0:T(8,128)S(1)}, u32[]{:S(2)}, u32[]{:S(2)}) %collective-permute-start.25) | collective-permute-done | bytes 458784 | tf_op jit(solution)/shard_map/ppermute | solution.py:443
  182.5 8.4 %collective-permute-done.26 = f32[112,1024]{1,0:T(8,128)S(1)} collective-permute-done((f32[112,1024]{1,0:T(8,128)S(1)}, f32[112,1024]{1,0:T(8,128)S(1)}, u32[]{:S(2)}, u32[]{:S(2)}) %collective-permute-start.26) | collective-permute-done | bytes 458784 | tf_op jit(solution)/shard_map/ppermute | solution.py:443
  193.3 8.2 %collective-permute-done.27.right = f32[112,1024]{1,0:T(8,128)S(1)} collective-permute-done((f32[112,1024]{1,0:T(8,128)S(1)}, f32[112,1024]{1,0:T(8,128)S(1)}, u32[]{:S(2)}, u32[]{:S(2)}) %collective-permute-start.27) | collective-permute-done | bytes 458784 | tf_op jit(solution)/shard_map/ppermute | solution.py:443
  207.5 5.8 %second_and_back.2 = (f32[48,2048]{1,0:T(8,128)S(1)}, f32[48,2048]{1,0:T(8,128)S(1)}, f32[48,2048]{1,0:T(8,128)S(1)}, f32[48,2048]{1,0:T(8,128)S(1)}) custom-call(s32[18]{0:T(128)S(1)} %dynamic-slice_bitcast_fusion.place_ref, f32[4,4,48,256]{3,2,1,0:T(8,128)S(1)} %copy-done.5, bf16[4,1536,128]{2,1,0:T(8,128)(2,1)} %constant.42.clone.v_ref, ...), custom_call_target="tpu_custom_call" | custom-call | tf_op jit(solution)/shard_map/second_and_back/pallas_call | solution.py:127
  237.8 5.8 %last_back.2.base = f32[64,32,256]{2,1,0:T(8,128)} custom-call(s32[18]{0:T(128)S(1)} %dynamic-slice_bitcast_fusion.place_ref, bf16[4,192,256]{2,1,0:T(8,128)(2,1)S(1)} %copy-done.8, bf16[4,192,256]{2,1,0:T(8,128)(2,1)S(1)} %copy-done.9, f32[64,32,256]{2,1,0:T(8,128)} %base.1, f32[48,2048]{1,0:T(8,128)S(1)} %get-tuple-element.141.rest_0_, ...), custom_call_target="tpu_custom_call" | custom-call | tf_op jit(solution)/shard_map/last_back/pallas_call | solution.py:394
  245.8 3.8 %last_back.3 = f32[64,32,256]{2,1,0:T(8,128)} custom-call(s32[18]{0:T(128)S(1)} %dynamic-slice_bitcast_fusion.place_ref, bf16[4,64,256]{2,1,0:T(8,128)(2,1)S(1)} %copy-done.10, bf16[4,64,256]{2,1,0:T(8,128)(2,1)S(1)} %copy-done.11, f32[64,32,256]{2,1,0:T(8,128)S(1)} %copy-done.2, f32[16,2048]{1,0:T(8,128)S(1)} %get-tuple-element.147.rest_0_, ...), custom_call_target="tpu_custom_call" | custom-call | tf_op jit(solution)/shard_map/last_back/pallas_call | solution.py:394
  (148 shorter events, 81.1 us)
Async XLA Ops:
  8.3 20.6 %collective-permute-start.7 = (f32[192,1024]{1,0:T(8,128)S(1)}, f32[192,1024]{1,0:T(8,128)S(1)}, u32[]{:S(2)}, u32[]{:S(2)}) collective-permute-start(f32[192,1024]{1,0:T(8,128)S(1)} %get-tuple-element.88), channel_id=1, source_target_pairs={{8,0},{16,8},{24,16},{28,24},{20,28},{12,20},{4,12},{0,4},{9,1},{1... | collective-permute-start | bytes 2359304 | tf_op jit(solution)/shard_map/ppermute | solution.py:444
  11.3 19.4 %collective-permute-start = (f32[192,1024]{1,0:T(8,128)S(1)}, f32[192,1024]{1,0:T(8,128)S(1)}, u32[]{:S(2)}, u32[]{:S(2)}) collective-permute-start(f32[192,1024]{1,0:T(8,128)S(1)} %get-tuple-element.80), channel_id=1, source_target_pairs={{0,8},{8,16},{16,24},{24,28},{28,20},{20,12},{12,4},{4,0},{1,9},{9... | collective-permute-start | bytes 2359304 | tf_op jit(solution)/shard_map/ppermute | solution.py:443
  29.1 18.8 %collective-permute-start.8 = (f32[192,1024]{1,0:T(8,128)S(1)}, f32[192,1024]{1,0:T(8,128)S(1)}, u32[]{:S(2)}, u32[]{:S(2)}) collective-permute-start(f32[192,1024]{1,0:T(8,128)S(1)} %add.86), channel_id=1, source_target_pairs={{8,0},{16,8},{24,16},{28,24},{20,28},{12,20},{4,12},{0,4},{9,1},{1... | collective-permute-start | bytes 2359304 | tf_op jit(solution)/shard_map/ppermute | solution.py:444
  30.9 18.4 %collective-permute-start.1 = (f32[192,1024]{1,0:T(8,128)S(1)}, f32[192,1024]{1,0:T(8,128)S(1)}, u32[]{:S(2)}, u32[]{:S(2)}) collective-permute-start(f32[192,1024]{1,0:T(8,128)S(1)} %add.80), channel_id=1, source_target_pairs={{0,8},{8,16},{16,24},{24,28},{28,20},{20,12},{12,4},{4,0},{1,9},{9... | collective-permute-start | bytes 2359304 | tf_op jit(solution)/shard_map/ppermute | solution.py:443
  48.0 17.9 %collective-permute-start.9 = (f32[192,1024]{1,0:T(8,128)S(1)}, f32[192,1024]{1,0:T(8,128)S(1)}, u32[]{:S(2)}, u32[]{:S(2)}) collective-permute-start(f32[192,1024]{1,0:T(8,128)S(1)} %add.87), channel_id=1, source_target_pairs={{8,0},{16,8},{24,16},{28,24},{20,28},{12,20},{4,12},{0,4},{9,1},{1... | collective-permute-start | bytes 2359304 | tf_op jit(solution)/shard_map/ppermute | solution.py:444
  49.4 17.6 %collective-permute-start.2 = (f32[192,1024]{1,0:T(8,128)S(1)}, f32[192,1024]{1,0:T(8,128)S(1)}, u32[]{:S(2)}, u32[]{:S(2)}) collective-permute-start(f32[192,1024]{1,0:T(8,128)S(1)} %add.81), channel_id=1, source_target_pairs={{0,8},{8,16},{16,24},{24,28},{28,20},{20,12},{12,4},{4,0},{1,9},{9... | collective-permute-start | bytes 2359304 | tf_op jit(solution)/shard_map/ppermute | solution.py:443
  66.0 17.6 %collective-permute-start.10 = (f32[192,1024]{1,0:T(8,128)S(1)}, f32[192,1024]{1,0:T(8,128)S(1)}, u32[]{:S(2)}, u32[]{:S(2)}) collective-permute-start(f32[192,1024]{1,0:T(8,128)S(1)} %add.88), channel_id=1, source_target_pairs={{8,0},{16,8},{24,16},{28,24},{20,28},{12,20},{4,12},{0,4},{9,1},{1... | collective-permute-start | bytes 2359304 | tf_op jit(solution)/shard_map/ppermute | solution.py:444
  67.1 17.6 %collective-permute-start.3 = (f32[192,1024]{1,0:T(8,128)S(1)}, f32[192,1024]{1,0:T(8,128)S(1)}, u32[]{:S(2)}, u32[]{:S(2)}) collective-permute-start(f32[192,1024]{1,0:T(8,128)S(1)} %add.82), channel_id=1, source_target_pairs={{0,8},{8,16},{16,24},{24,28},{28,20},{20,12},{12,4},{4,0},{1,9},{9... | collective-permute-start | bytes 2359304 | tf_op jit(solution)/shard_map/ppermute | solution.py:443
  83.7 17.6 %collective-permute-start.11 = (f32[192,1024]{1,0:T(8,128)S(1)}, f32[192,1024]{1,0:T(8,128)S(1)}, u32[]{:S(2)}, u32[]{:S(2)}) collective-permute-start(f32[192,1024]{1,0:T(8,128)S(1)} %add.89), channel_id=1, source_target_pairs={{8,0},{16,8},{24,16},{28,24},{20,28},{12,20},{4,12},{0,4},{9,1},{1... | collective-permute-start | bytes 2359304 | tf_op jit(solution)/shard_map/ppermute | solution.py:444
  84.8 17.6 %collective-permute-start.4 = (f32[192,1024]{1,0:T(8,128)S(1)}, f32[192,1024]{1,0:T(8,128)S(1)}, u32[]{:S(2)}, u32[]{:S(2)}) collective-permute-start(f32[192,1024]{1,0:T(8,128)S(1)} %add.83), channel_id=1, source_target_pairs={{0,8},{8,16},{16,24},{24,28},{28,20},{20,12},{12,4},{4,0},{1,9},{9... | collective-permute-start | bytes 2359304 | tf_op jit(solution)/shard_map/ppermute | solution.py:443
  101.4 17.6 %collective-permute-start.12 = (f32[192,1024]{1,0:T(8,128)S(1)}, f32[192,1024]{1,0:T(8,128)S(1)}, u32[]{:S(2)}, u32[]{:S(2)}) collective-permute-start(f32[192,1024]{1,0:T(8,128)S(1)} %add.90), channel_id=1, source_target_pairs={{8,0},{16,8},{24,16},{28,24},{20,28},{12,20},{4,12},{0,4},{9,1},{1... | collective-permute-start | bytes 2359304 | tf_op jit(solution)/shard_map/ppermute | solution.py:444
  102.5 17.6 %collective-permute-start.5 = (f32[192,1024]{1,0:T(8,128)S(1)}, f32[192,1024]{1,0:T(8,128)S(1)}, u32[]{:S(2)}, u32[]{:S(2)}) collective-permute-start(f32[192,1024]{1,0:T(8,128)S(1)} %add.84), channel_id=1, source_target_pairs={{0,8},{8,16},{16,24},{24,28},{28,20},{20,12},{12,4},{4,0},{1,9},{9... | collective-permute-start | bytes 2359304 | tf_op jit(solution)/shard_map/ppermute | solution.py:443
  119.1 15.9 %collective-permute-start.13 = (f32[192,1024]{1,0:T(8,128)S(1)}, f32[192,1024]{1,0:T(8,128)S(1)}, u32[]{:S(2)}, u32[]{:S(2)}) collective-permute-start(f32[192,1024]{1,0:T(8,128)S(1)} %add.91), channel_id=1, source_target_pairs={{8,0},{16,8},{24,16},{28,24},{20,28},{12,20},{4,12},{0,4},{9,1},{1... | collective-permute-start | bytes 2359304 | tf_op jit(solution)/shard_map/ppermute | solution.py:444
  120.3 14.7 %collective-permute-start.6 = (f32[192,1024]{1,0:T(8,128)S(1)}, f32[192,1024]{1,0:T(8,128)S(1)}, u32[]{:S(2)}, u32[]{:S(2)}) collective-permute-start(f32[192,1024]{1,0:T(8,128)S(1)} %add.85), channel_id=1, source_target_pairs={{0,8},{8,16},{16,24},{24,28},{28,20},{20,12},{12,4},{4,0},{1,9},{9... | collective-permute-start | bytes 2359304 | tf_op jit(solution)/shard_map/ppermute | solution.py:443
  139.0 12.4 %collective-permute-start.18 = (f32[48,2048]{1,0:T(8,128)S(1)}, f32[48,2048]{1,0:T(8,128)S(1)}, u32[]{:S(2)}, u32[]{:S(2)}) collective-permute-start(f32[48,2048]{1,0:T(8,128)S(1)} %get-tuple-element.103), channel_id=1, source_target_pairs={{0,1},{1,0},{2,3},{3,2},{4,5},{5,4},{6,7},{7,6},{8,9},{9,8},{10,11... | collective-permute-start | bytes 1179656 | tf_op jit(solution)/shard_map/ppermute | solution.py:416
  139.0 12.4 %collective-permute-start.19 = (f32[48,2048]{1,0:T(8,128)S(1)}, f32[48,2048]{1,0:T(8,128)S(1)}, u32[]{:S(2)}, u32[]{:S(2)}) collective-permute-start(f32[48,2048]{1,0:T(8,128)S(1)} %get-tuple-element.104), channel_id=1, source_target_pairs={{0,2},{1,3},{2,0},{3,1},{4,6},{5,7},{6,4},{7,5},{8,10},{9,11},{10,... | collective-permute-start | bytes 1179656 | tf_op jit(solution)/shard_map/ppermute | solution.py:416
  145.9 14.2 %collective-permute-start.22 = (f32[48,2048]{1,0:T(8,128)S(1)}, f32[48,2048]{1,0:T(8,128)S(1)}, u32[]{:S(2)}, u32[]{:S(2)}) collective-permute-start(f32[48,2048]{1,0:T(8,128)S(1)} %get-tuple-element.109), channel_id=1, source_target_pairs={{0,3},{1,2},{2,1},{3,0},{4,7},{5,6},{6,5},{7,4},{8,11},{9,10},{10,... | collective-permute-start | bytes 1179656 | tf_op jit(solution)/shard_map/ppermute | solution.py:416
  169.2 11.9 %collective-permute-start.28 = (f32[112,1024]{1,0:T(8,128)S(1)}, f32[112,1024]{1,0:T(8,128)S(1)}, u32[]{:S(2)}, u32[]{:S(2)}) collective-permute-start(f32[112,1024]{1,0:T(8,128)S(1)} %get-tuple-element.151), channel_id=1, source_target_pairs={{8,0},{16,8},{24,16},{28,24},{20,28},{12,20},{4,12},{0,4},{9,1},{1... | collective-permute-start | bytes 1376264 | tf_op jit(solution)/shard_map/ppermute | solution.py:444
  179.4 11.6 %collective-permute-start.26 = (f32[112,1024]{1,0:T(8,128)S(1)}, f32[112,1024]{1,0:T(8,128)S(1)}, u32[]{:S(2)}, u32[]{:S(2)}) collective-permute-start(f32[112,1024]{1,0:T(8,128)S(1)} %pad_maximum_fusion.2), channel_id=1, source_target_pairs={{0,8},{8,16},{16,24},{24,28},{28,20},{20,12},{12,4},{4,0},{1,9},{9... | collective-permute-start | bytes 1376264 | tf_op jit(solution)/shard_map/ppermute | solution.py:443
  203.4 12.0 %collective-permute-start.31 = (f32[16,2048]{1,0:T(8,128)S(1)}, f32[16,2048]{1,0:T(8,128)S(1)}, u32[]{:S(2)}, u32[]{:S(2)}) collective-permute-start(f32[16,2048]{1,0:T(8,128)S(1)} %get-tuple-element.132), channel_id=1, source_target_pairs={{0,1},{1,0},{2,3},{3,2},{4,5},{5,4},{6,7},{7,6},{8,9},{9,8},{10,11... | collective-permute-start | bytes 393224 | tf_op jit(solution)/shard_map/ppermute | solution.py:416
  203.4 12.0 %collective-permute-start.32 = (f32[16,2048]{1,0:T(8,128)S(1)}, f32[16,2048]{1,0:T(8,128)S(1)}, u32[]{:S(2)}, u32[]{:S(2)}) collective-permute-start(f32[16,2048]{1,0:T(8,128)S(1)} %get-tuple-element.133), channel_id=1, source_target_pairs={{0,2},{1,3},{2,0},{3,1},{4,6},{5,7},{6,4},{7,5},{8,10},{9,11},{10,... | collective-permute-start | bytes 393224 | tf_op jit(solution)/shard_map/ppermute | solution.py:416
  213.3 17.2 %collective-permute-start.35 = (f32[48,2048]{1,0:T(8,128)S(1)}, f32[48,2048]{1,0:T(8,128)S(1)}, u32[]{:S(2)}, u32[]{:S(2)}) collective-permute-start(f32[48,2048]{1,0:T(8,128)S(1)} %get-tuple-element.138), channel_id=1, source_target_pairs={{0,1},{1,0},{2,3},{3,2},{4,5},{5,4},{6,7},{7,6},{8,9},{9,8},{10,11... | collective-permute-start | bytes 1179656 | tf_op jit(solution)/shard_map/ppermute | solution.py:416
  213.4 17.1 %collective-permute-start.36 = (f32[48,2048]{1,0:T(8,128)S(1)}, f32[48,2048]{1,0:T(8,128)S(1)}, u32[]{:S(2)}, u32[]{:S(2)}) collective-permute-start(f32[48,2048]{1,0:T(8,128)S(1)} %get-tuple-element.139), channel_id=1, source_target_pairs={{0,2},{1,3},{2,0},{3,1},{4,6},{5,7},{6,4},{7,5},{8,10},{9,11},{10,... | collective-permute-start | bytes 1179656 | tf_op jit(solution)/shard_map/ppermute | solution.py:416
  215.3 17.7 %collective-permute-start.37 = (f32[48,2048]{1,0:T(8,128)S(1)}, f32[48,2048]{1,0:T(8,128)S(1)}, u32[]{:S(2)}, u32[]{:S(2)}) collective-permute-start(f32[48,2048]{1,0:T(8,128)S(1)} %get-tuple-element.140), channel_id=1, source_target_pairs={{0,3},{1,2},{2,1},{3,0},{4,7},{5,6},{6,5},{7,4},{8,11},{9,10},{10,... | collective-permute-start | bytes 1179656 | tf_op jit(solution)/shard_map/ppermute | solution.py:416
  (36 other events, 290.5 us)

commit v3 on v2

v3 whole, which is shorter than its diff:
```python
import functools
import math

import jax
import jax.numpy as jnp
import ml_dtypes
import numpy as np
from jax import lax
from jax.experimental import pallas as pl
from jax.experimental.pallas import tpu as pltpu
from jax.sharding import PartitionSpec as P

sigma_sq = 0.05
step_size = 0.25
alpha_reach = 16.0
highest = lax.Precision.HIGHEST
vmem_bytes = 50 * 1024 * 1024
lane = 128
early_eighths = 6
near_step, far_step, ends_step = 3, 4, 5


def split_bf16(table):
    high = table.astype(ml_dtypes.bfloat16)
    low = (table - high.astype(np.float64)).astype(ml_dtypes.bfloat16)
    return high, low


def packed_np(length):
    half = length // 2
    index = np.arange(length)
    freq = np.where(index <= half, index, index - half)
    angle = (index[:, None] * freq[None, :] % length) * (2.0 * math.pi / length)
    forward = np.where(index[None, :] <= half, np.cos(angle), np.sin(angle))
    weight = np.where((index == 0) | (index == half), 1.0, 2.0) / length
    lam = 2.0 - 2.0 * np.cos(freq * (2.0 * math.pi / length))
    return forward, (forward * weight[None, :]).T, lam


class Plan:
    def __init__(self, length, rows_x, subj, space):
        self.length, self.xl, self.subj, self.space = length, rows_x, subj, space
        self.yl = length // subj
        self.lanes = self.yl * self.xl
        self.half = self.lanes // 2
        self.ty = lane // self.xl if self.xl < lane else 1
        self.tiles = self.lanes // lane
        early = length * early_eighths // 8
        self.early, self.late = early, length - early
        self.chunks = [self.early, self.late]
        self.offs = [0, early]
        self.g, self.gl = self.early // space, self.late // subj
        ring = list(range(0, subj, 2)) + list(range(subj - 1, 0, -2))
        self.ring = ring
        rows = np.zeros((subj, space, 2 * subj + 2), np.int32)
        for at, j in enumerate(ring):
            for k in range(subj):
                rows[j, :, 2 * k] = ring[(at - 1 - k) % subj]
                rows[j, :, 2 * k + 1] = ring[(at + 1 + k) % subj]
            rows[j, :, 2 * subj] = np.arange(space)
            rows[j, :, 2 * subj + 1] = j
        self.place_table = rows
        self.at_space, self.at_subj = 2 * subj, 2 * subj + 1
        forward, inverse, lam = packed_np(length)
        high, low = split_bf16(forward.T)
        self.t_table = np.concatenate([high, high, low], axis=1)
        high, low = split_bf16(inverse)
        self.i_table = np.stack([high, low])
        lines = length // self.ty
        high, low = split_bf16(forward.reshape(lines, self.ty * length))
        self.y_table = np.concatenate([high, high, low], axis=0)
        wide = inverse.T.reshape(lines, self.ty, length).transpose(1, 0, 2)
        high, low = split_bf16(wide.reshape(length, length))
        self.g_table = np.concatenate([high, high, low], axis=1)
        eye = np.eye(self.ty)
        blocks = forward.reshape(space, self.xl, length)
        wide = np.einsum("ab,sxw->saxbw", eye, blocks).reshape(space, lane, self.ty * length)
        high, low = split_bf16(wide)
        self.w_table = np.concatenate([high, high, low], axis=1)
        blocks = inverse.reshape(length, space, self.xl)
        wide = np.einsum("ab,wsx->sawbx", eye, blocks).reshape(space, self.ty * length, lane)
        high, low = split_bf16(wide)
        self.v_table = np.concatenate([high, high, low], axis=1)
        index = np.arange(length)
        slope = np.zeros((length, length))
        slope[(index + 1) % length, index] += 0.5
        slope[(index - 1) % length, index] -= 0.5
        slope = slope.astype(ml_dtypes.bfloat16)
        self.d_table = np.concatenate([slope, self.t_table], axis=1)
        centre = (1.0 + alpha_reach * (lam[:, None] + lam[None, :])) / alpha_reach + 2.0
        r = 2.0 / (centre + np.sqrt(centre * centre - 4.0))
        q = r * r
        scale = (2.0 / sigma_sq) * q / (alpha_reach * alpha_reach)
        table = np.stack([r, scale * (1 + q) / (1 - q) ** 3, scale / (1 - q) ** 2, np.log(r)])
        table = table.astype(np.float32)
        early_rows = table[:, :early].reshape(4, space, self.g, length)
        self.r_early = early_rows.transpose(1, 0, 2, 3)
        late_rows = table[:, early:].reshape(4, subj, self.gl, length)
        self.r_late = late_rows.transpose(1, 0, 2, 3)


def split(value):
    high = value.astype(jnp.bfloat16)
    low = (value - high.astype(jnp.float32)).astype(jnp.bfloat16)
    return high, low


def call_once(kernel, name, out_shape, place, args, scratch=()):
    vmem = pl.BlockSpec(memory_space=pltpu.VMEM)
    return pl.pallas_call(
        kernel,
        out_shape=out_shape,
        in_specs=[pl.BlockSpec(memory_space=pltpu.SMEM)] + [vmem] * len(args),
        out_specs=jax.tree.map(lambda _: vmem, out_shape),
        scratch_shapes=scratch,
        compiler_params=params(),
        name=name,
    )(place, *[jnp.asarray(a) for a in args])


def params(**kw):
    return pltpu.CompilerParams(vmem_limit_bytes=vmem_bytes, **kw)


def force_kernel(plan, place_ref, warped, images, jac, table, *rest):
    outs, field = rest[:-1], rest[-1]
    me = place_ref[plan.at_space]
    n = len(plan.chunks)
    way = pl.program_id(0)
    yh = plan.yl // 2
    count = warped.shape[0]
    length = plan.length
    rows = plan.xl * yh

    total = None
    for b in range(count):
        w = warped[b].reshape(rows, length)
        slope = jnp.dot(w, table[:, :length], preferred_element_type=jnp.float32)
        diff = images[b].reshape(rows, length).astype(jnp.float32) - w.astype(jnp.float32)
        term = jac[b].reshape(rows, length).astype(jnp.float32) * diff * slope
        total = term if total is None else total + term
    field[...] = jnp.swapaxes(total.reshape(plan.xl, yh, length), 0, 1)

    def transform(refs):
        per = max(1, 256 // plan.xl)
        for y0 in range(0, yh, per):
            lines = field[y0 : y0 + per].reshape(per * plan.xl, length)
            high, low = split(lines)
            both = jnp.concatenate([high, low, high], axis=1)
            out = lax.dot_general(
                table[:, length:], both, (((1,), (1,)), ((), ())), preferred_element_type=jnp.float32
            )
            cols = slice(y0 * plan.xl, (y0 + per) * plan.xl)
            for d in range(plan.space):
                rows = pl.ds(pl.multiple_of((me ^ d) * plan.g, 8), plan.g)
                refs[0][rows, cols] = out[d * plan.g : (d + 1) * plan.g]
            refs[1][:, cols] = out[plan.early :]

    @pl.when(way == 0)
    def _():
        transform(outs[:n])

    @pl.when(way == 1)
    def _():
        transform(outs[n:])


def force_blocks(plan, k, place, warped, images, jac):
    count, xl, _, length = warped.shape
    yh = plan.yl // 2
    source = pl.BlockSpec(
        (count, xl, yh, length), lambda way, place: (0, 0, 2 * place[2 * k + way] + way, 0)
    )
    shapes = [jax.ShapeDtypeStruct((c, plan.half), jnp.float32) for c in plan.chunks] * 2
    outs = pl.pallas_call(
        functools.partial(force_kernel, plan),
        out_shape=shapes,
        grid_spec=pltpu.PrefetchScalarGridSpec(
            num_scalar_prefetch=1,
            grid=(2,),
            in_specs=[
                source,
                source,
                source,
                pl.BlockSpec((length, 4 * length), lambda way, place: (0, 0)),
            ],
            out_specs=[pl.BlockSpec(s.shape, lambda way, place: (0, 0)) for s in shapes],
            scratch_shapes=[pltpu.VMEM((yh, xl, length), jnp.float32)],
        ),
        compiler_params=params(),
        cost_estimate=pl.CostEstimate(
            flops=16 * xl * yh * length * length,
            bytes_accessed=12 * count * xl * yh * length + 8 * xl * yh * length,
            transcendentals=0,
        ),
        name="force",
    )(place, warped, images, jac, jnp.asarray(plan.d_table))
    n = len(plan.chunks)
    return outs[:n], outs[n:]


def join_kernel(plan, place_ref, right_local, left_local, right, left, *outs):
    for d, out in enumerate(outs):
        rows = slice(d * plan.g, (d + 1) * plan.g)
        out[:, : plan.half] = right[rows] + right_local[rows]
        out[:, plan.half :] = left[rows] + left_local[rows]


def join(plan, place, *args):
    return call_once(
        functools.partial(join_kernel, plan),
        "join",
        [jax.ShapeDtypeStruct((plan.g, plan.lanes), jnp.float32)] * plan.space,
        place,
        args,
    )


def regroup_kernel(plan, place_ref, *rest):
    sources, outs = rest[:-2], rest[-2:]
    for n, source in enumerate(sources):
        at = 2 * place_ref[n] + n % 2
        to = pl.ds(pl.multiple_of(at % plan.subj * plan.gl, 8), plan.gl)

        def put(way):
            for m in range(plan.subj):
                target = place_ref[2 * m + way]
                rows = pl.ds(pl.multiple_of(target * plan.gl, 8), plan.gl)
                outs[way][m, to, :] = source[rows, :]

        for way in range(2):
            pl.when(at // plan.subj == way)(functools.partial(put, way))


def regroup(plan, place, sources):
    shape = (plan.subj, plan.late, plan.half)
    return call_once(
        functools.partial(regroup_kernel, plan),
        "regroup",
        [jax.ShapeDtypeStruct(shape, jnp.float32)] * 2,
        place,
        sources,
    )


def forward_kernel(plan, place_ref, r_ref, w_ref, *rest):
    g = plan.g
    pieces, f_ref, ends_ref = rest[: plan.space], rest[-2], rest[-1]
    me = place_ref[plan.at_space]
    total = None
    for d, piece in enumerate(pieces):
        lines = jnp.concatenate(
            [piece[:, t * lane : (t + 1) * lane] for t in range(plan.tiles)], axis=0
        )
        high, low = split(lines)
        both = jnp.concatenate([high, low, high], axis=1)
        term = jnp.dot(both, w_ref[me ^ d], preferred_element_type=jnp.float32)
        total = term if total is None else total + term
    f_ref[...] = total
    r = r_ref[me, 0]
    length = plan.length

    def line(y):
        t, a = y // plan.ty, y % plan.ty
        return f_ref[t * g : (t + 1) * g, a * length : (a + 1) * length]

    zero = jnp.zeros_like(r)
    v, w = zero, zero
    for y in range(plan.yl):
        w = r * (w + v)
        v = line(y) + r * v
    ends_ref[:, :length], ends_ref[:, length : 2 * length] = v, w
    v, w = zero, zero
    for y in range(plan.yl - 1, -1, -1):
        v = v + line(y)
        w = r * (w + v)
        v = r * v
    ends_ref[:, 2 * length : 3 * length], ends_ref[:, 3 * length :] = v, w


def forward_lines(plan, place, pieces):
    return call_once(
        functools.partial(forward_kernel, plan),
        "first_forward",
        [
            jax.ShapeDtypeStruct((plan.tiles * plan.g, plan.ty * plan.length), jnp.float32),
            jax.ShapeDtypeStruct((plan.g, 4 * plan.length), jnp.float32),
        ],
        place,
        [plan.r_early, plan.w_table, *pieces],
    )


def enter(log_r, length, size, blocks, block, sources):
    full = jnp.exp(float(length) * log_r)
    once = 1.0 / (1.0 - full)
    again = float(length) * full * once
    carry = [jnp.zeros_like(log_r)] * 4
    g = log_r.shape[0]
    for source, ref in sources:
        for i in (0, 2):
            between = block - 1 - source if i == 0 else source - 1 - block
            between = jnp.where(between < 0, between + blocks, between)
            reach = (between * size).astype(jnp.float32)
            power = once * jnp.exp(reach * log_r)
            v = ref[:g, i * length : (i + 1) * length]
            w = ref[:g, (i + 1) * length : (i + 2) * length]
            carry[i] = carry[i] + power * v
            carry[i + 1] = carry[i + 1] + power * (w + (reach + again) * v)
    return carry


def backward_kernel(plan, place_ref, r_ref, v_ref, f_ref, *rest):
    ends_refs, outs, u_ref = rest[: plan.subj], rest[plan.subj : -1], rest[-1]
    me, block = place_ref[plan.at_space], place_ref[plan.at_subj]
    g, length = plan.g, plan.length
    r, alpha, beta, log_r = (r_ref[me, i] for i in range(4))
    sources = [(block if h == 0 else place_ref[h - 1], ref) for h, ref in enumerate(ends_refs)]
    carry = enter(log_r, length, plan.yl, plan.subj, block, sources)

    def line(y):
        t, a = y // plan.ty, y % plan.ty
        return (slice(t * g, (t + 1) * g), slice(a * length, (a + 1) * length))

    v, w = carry[0], carry[1]
    for y in range(plan.yl):
        w = r * (w + v)
        v = f_ref[line(y)] + r * v
        u_ref[line(y)] = alpha * v + beta * w
    v, w = carry[2], carry[3]
    for y in range(plan.yl - 1, -1, -1):
        u_ref[line(y)] = u_ref[line(y)] + (alpha * v + beta * w)
        v = v + f_ref[line(y)]
        w = r * (w + v)
        v = r * v
    high, low = split(u_ref[...])
    both = jnp.concatenate([high, low, high], axis=1)
    top = plan.space // 2
    tables = jnp.concatenate([v_ref[me ^ d] for d in range(plan.space)], axis=1)
    all_back = jnp.dot(both, tables, preferred_element_type=jnp.float32)
    for d in range(plan.space):
        out = outs[min(d, top)]
        first = max(d - top, 0) * g
        back = all_back[:, d * lane : (d + 1) * lane]
        for t in range(plan.tiles):
            out[first : first + g, t * lane : (t + 1) * lane] = back[t * g : (t + 1) * g]


def backward_lines(plan, place, f, ends):
    top = plan.space // 2
    counts = [plan.g] * top + [plan.g * top]
    return call_once(
        functools.partial(backward_kernel, plan),
        "second_and_back",
        [jax.ShapeDtypeStruct((c, plan.lanes), jnp.float32) for c in counts],
        place,
        [plan.r_early, plan.v_table, f, *ends],
        scratch=[pltpu.VMEM(f.shape, jnp.float32)],
    )


def late_forward_kernel(plan, place_ref, r_ref, y_ref, *rest):
    *arrived, f_ref, ends_ref, z_ref = rest
    length, gl, xl, ty = plan.length, plan.gl, plan.xl, plan.ty
    lines = length // ty
    tiles = plan.half // lane
    for way in range(2):
        local, ref = arrived[way], arrived[2 + way]
        for b in range(plan.subj):
            rows = slice(b * gl, (b + 1) * gl)
            for t in range(tiles):
                cols = slice(t * lane, (t + 1) * lane)
                to = ((way * plan.subj + b) * tiles + t) * gl
                z_ref[to : to + gl, :] = ref[rows, cols] + local[0, rows, cols]
    turned = jnp.concatenate([z_ref[pl.ds(p, lines, stride=gl), :].T for p in range(gl)], axis=0)
    high, low = split(turned)
    both = jnp.concatenate([high, low, high], axis=1)
    out = jnp.dot(both, y_ref[...], preferred_element_type=jnp.float32)
    for p in range(gl):
        value = None
        for a in range(ty):
            rows = slice(p * lane + a * xl, p * lane + (a + 1) * xl)
            term = out[rows, a * length : (a + 1) * length]
            value = term if value is None else value + term
        for h in range(length // lane):
            f_ref[h, pl.ds(p, xl, stride=gl), :] = value[:, h * lane : (h + 1) * lane]
    r = r_ref[place_ref[plan.at_subj], 0]

    def line(x):
        rows = slice(x * gl, (x + 1) * gl)
        return jnp.concatenate([f_ref[h, rows, :] for h in range(length // lane)], axis=1)

    zero = jnp.zeros_like(r)
    v, w = zero, zero
    for x in range(xl):
        w = r * (w + v)
        v = line(x) + r * v
    ends_ref[:, :length], ends_ref[:, length : 2 * length] = v, w
    v, w = zero, zero
    for x in range(xl - 1, -1, -1):
        v = v + line(x)
        w = r * (w + v)
        v = r * v
    ends_ref[:, 2 * length : 3 * length], ends_ref[:, 3 * length :] = v, w


def late_forward(plan, place, *args):
    return call_once(
        functools.partial(late_forward_kernel, plan),
        "second_forward",
        [
            jax.ShapeDtypeStruct((plan.length // lane, plan.xl * plan.gl, lane), jnp.float32),
            jax.ShapeDtypeStruct((plan.gl, 4 * plan.length), jnp.float32),
        ],
        place,
        [plan.r_late, plan.y_table, *args],
        scratch=[pltpu.VMEM((plan.length // plan.ty * plan.gl, lane), jnp.float32)],
    )


def late_backward_kernel(plan, place_ref, r_ref, g_ref, f_ref, *rest):
    ends_refs = rest[: plan.space]
    out_ref, u_ref, y_ref = rest[plan.space :]
    me = place_ref[plan.at_space]
    length, gl, xl, ty = plan.length, plan.gl, plan.xl, plan.ty
    lines, halves = length // ty, length // lane
    r, alpha, beta, log_r = (r_ref[place_ref[plan.at_subj], i] for i in range(4))
    sources = [(me ^ d, ref) for d, ref in enumerate(ends_refs)]
    carry = enter(log_r, length, xl, plan.space, me, sources)

    def line(ref, x):
        rows = slice(x * gl, (x + 1) * gl)
        return jnp.concatenate([ref[h, rows, :] for h in range(halves)], axis=1)

    def keep(x, value):
        for h in range(halves):
            u_ref[h, x * gl : (x + 1) * gl, :] = value[:, h * lane : (h + 1) * lane]

    v, w = carry[0], carry[1]
    for x in range(xl):
        w = r * (w + v)
        v = line(f_ref, x) + r * v
        keep(x, alpha * v + beta * w)
    v, w = carry[2], carry[3]
    for x in range(xl - 1, -1, -1):
        keep(x, line(u_ref, x) + (alpha * v + beta * w))
        v = v + line(f_ref, x)
        w = r * (w + v)
        v = r * v
    rows = jnp.concatenate(
        [
            jnp.concatenate(
                [u_ref[h, pl.ds(p, xl, stride=gl), :] for h in range(halves)], axis=1
            )
            for p in range(gl)
        ],
        axis=0,
    )
    high, low = split(rows)
    both = jnp.concatenate([high, low, high], axis=1)
    out = lax.dot_general(
        g_ref[...], both, (((1,), (1,)), ((), ())), preferred_element_type=jnp.float32
    )
    place_of = lax.broadcasted_iota(jnp.int32, (lines, lane), 1) // xl
    for p in range(gl):
        tile, spot = p // ty, p % ty
        value = None
        for a in range(ty):
            part = out[a * lines : (a + 1) * lines, tile * lane : (tile + 1) * lane]
            if a != spot:
                part = pltpu.roll(part, (a - spot) % ty * xl, 1)
            value = part if value is None else jnp.where(place_of == a, part, value)
        y_ref[pl.ds(p, lines, stride=gl), :] = value
    for j in range(plan.subj):
        for t in range(plan.tiles):
            start = (j * plan.tiles + t) * gl
            out_ref[j, :, t * lane : (t + 1) * lane] = y_ref[start : start + gl, :]


def late_backward(plan, place, f, ends):
    return call_once(
        functools.partial(late_backward_kernel, plan),
        "first_and_back",
        jax.ShapeDtypeStruct((plan.subj, plan.gl, plan.lanes), jnp.float32),
        place,
        [plan.r_late, plan.g_table, f, *ends],
        scratch=[
            pltpu.VMEM(f.shape, jnp.float32),
            pltpu.VMEM((plan.length // plan.ty * plan.gl, lane), jnp.float32),
        ],
    )


def finish_kernel(plan, y_step, place_ref, i_ref, velocity, *rest):
    pieces, out = rest[:-1], rest[-1]
    length, xl = plan.length, plan.xl
    me = place_ref[plan.at_space]
    starts = [pl.multiple_of((me ^ d) * plan.g, 8) for d in range(plan.space)]
    high, low = (
        jnp.concatenate(
            [i_ref[i, pl.ds(start, plan.g), :] for start in starts] + [i_ref[i, plan.early :, :]],
            axis=0,
        )
        for i in range(2)
    )
    table = jnp.concatenate([high, high, low], axis=0)
    lines = []
    for t in range(y_step // plan.ty):
        columns = jnp.concatenate([p[:, t * lane : (t + 1) * lane] for p in pieces], axis=0)
        high, low = split(columns.T)
        both = jnp.concatenate([high, low, high], axis=1)
        lines.append(jnp.dot(both, table, preferred_element_type=jnp.float32))
        if len(lines) * plan.ty == 8:
            y = (t + 1) * plan.ty - 8
            block = jnp.concatenate(lines, axis=0).reshape(8, xl, length)
            smoothed = jnp.swapaxes(block, 0, 1)
            vel = velocity[:, y : y + 8, :]
            out[:, y : y + 8, :] = vel - step_size * (2.0 * vel - smoothed)
            lines = []


def finish(plan, place, velocity, pieces):
    xl, yl, length = velocity.shape
    y_step = 16
    width = y_step * xl
    block = pl.BlockSpec((xl, y_step, length), lambda at, place: (0, at, 0))
    return pl.pallas_call(
        functools.partial(finish_kernel, plan, y_step),
        out_shape=jax.ShapeDtypeStruct(velocity.shape, jnp.float32),
        grid_spec=pltpu.PrefetchScalarGridSpec(
            num_scalar_prefetch=1,
            grid=(yl // y_step,),
            in_specs=[
                pl.BlockSpec((2, length, length), lambda at, place: (0, 0, 0)),
                block,
            ]
            + [pl.BlockSpec((p.shape[0], width), lambda at, place: (0, at)) for p in pieces],
            out_specs=block,
        ),
        compiler_params=params(),
        name="last_back",
    )(place, jnp.asarray(plan.i_table), velocity, *pieces)


def tie(first, second):
    return lax.optimization_barrier((first, second))


def over_one(plan, part, d):
    if d == 0:
        return part
    return lax.ppermute(part, "space", [(i, i ^ d) for i in range(plan.space)])


def over_space(plan, pieces):
    return [over_one(plan, piece, d) for d, piece in enumerate(pieces)]


def ring_body(plan, template_warped, subject_images, jacobians, velocity):
    subj, space, half = plan.subj, plan.space, plan.subj // 2
    j, s = lax.axis_index("subj"), lax.axis_index("space")
    table = plan.place_table
    place = lax.dynamic_slice(jnp.asarray(table), (j, s, 0), (1, 1, table.shape[2])).reshape(-1)
    to_right = [(plan.ring[i], plan.ring[(i + 1) % subj]) for i in range(subj)]
    to_left = [(b, a) for a, b in to_right]

    def go_round(both):
        return lax.ppermute(both[0], "subj", to_right), lax.ppermute(both[1], "subj", to_left)

    local = [
        force_blocks(plan, k, place, template_warped, subject_images, jacobians)
        for k in range(subj)
    ]

    both = local[0][0][0], local[0][1][0]
    for k in range(1, subj):
        both = go_round(both)
        if k < subj - 1:
            both = tuple(b + local[k][way][0] for way, b in enumerate(both))
    pieces = join(plan, place, local[-1][0][0], local[-1][1][0], *both)
    late = regroup(plan, place, [local[k][way][1] for k in range(subj) for way in range(2)])

    top = space // 2
    both, own = tie((late[0][0], late[1][0]), pieces[0])
    pieces = [own, *pieces[1:]]
    far = lax.ppermute(
        jnp.concatenate(pieces[top:]), "space", [(i, i ^ top) for i in range(space)]
    )
    moved = over_space(plan, pieces[:top])
    arrived = []
    for k in range(1, subj):
        if k == near_step:
            both, moved = tie(both, moved)
        if k == far_step:
            both, far = tie(both, far)
            far = [far[d * plan.g : (d + 1) * plan.g] for d in range(top)]
            f, ends = forward_lines(plan, place, [*moved, *over_space(plan, far)])
        if k == ends_step:
            both, (f, ends) = tie(both, (f, ends))
        if k >= ends_step and len(arrived) < half:
            extra = arrived[-1] if arrived else (ends, ends)
            both = tuple(jnp.concatenate([b, e]) for b, e in zip(both, extra))
        both = go_round(both)
        if both[0].shape[0] > plan.late:
            arrived.append(tuple(b[plan.late :] for b in both))
        if k < subj - 1:
            both = tuple(b[: plan.late] + late[way][k] for way, b in enumerate(both))
    while len(arrived) < half:
        arrived.append(go_round(arrived[-1] if arrived else (ends, ends)))
    all_ends = [ends] + [e for pair in arrived for e in pair]

    f_late, ends_late = late_forward(
        plan, place, late[0][subj - 1 :], late[1][subj - 1 :], *both
    )
    others = [over_one(plan, ends_late, d) for d in range(space)]
    f, others = tie(f, others)
    *back, far = backward_lines(plan, place, f, all_ends[:subj])
    far = lax.ppermute(far, "space", [(i, i ^ top) for i in range(space)])
    back = over_space(plan, back)
    f_late, back = tie(f_late, back)
    back_late = late_backward(plan, place, f_late, others)
    back_late = lax.all_to_all(back_late, "subj", 0, 0)
    back_late = back_late.reshape(plan.late, plan.lanes)
    far = [far[d * plan.g : (d + 1) * plan.g] for d in range(top)]
    back += over_space(plan, far)
    return finish(plan, place, velocity, [*back, back_late])


def smoothing_symbol(first, second, third, length):
    def damping(freq):
        turns = (freq % length).astype(jnp.float32)
        return 2.0 - 2.0 * jnp.cos(turns * (2.0 * math.pi / length))

    total = damping(first) + damping(second) + damping(third)
    return 1.0 / (1.0 + alpha_reach * total) ** 2


def transposing_body(template_warped, subject_images, jacobians, velocity):
    length = template_warped.shape[3]
    half = length // 2
    warped = template_warped.astype(jnp.float32)
    slope = (jnp.roll(warped, -1, axis=3) - jnp.roll(warped, 1, axis=3)) * 0.5
    partial_value = jnp.sum(
        jacobians.astype(jnp.float32) * (subject_images.astype(jnp.float32) - warped) * slope,
        axis=0,
    )
    forward, inverse, _ = packed_np(length)
    forward, inverse = forward.astype(np.float32), inverse.astype(np.float32)
    packed = jnp.einsum("xyz,zp->xpy", partial_value, forward, precision=highest)
    packed = lax.psum_scatter(packed, "subj", scatter_dimension=1, tiled=True)
    packed = packed * (2.0 / sigma_sq)
    spectra = jnp.einsum("xpy,yk->kpx", packed, forward, precision=highest)
    lines = lax.all_to_all(spectra, "space", split_axis=0, concat_axis=2, tiled=True)
    freq_lines = jnp.einsum("kpx,xw->kpw", lines, forward, precision=highest)

    def true_freq(index):
        return jnp.where(index <= half, index, index - half)

    def mine(axis, size):
        return true_freq(lax.axis_index(axis) * size + jnp.arange(size, dtype=jnp.int32))

    symbol = smoothing_symbol(
        mine("space", lines.shape[0])[:, None, None],
        mine("subj", lines.shape[1])[None, :, None],
        true_freq(jnp.arange(length, dtype=jnp.int32))[None, None, :],
        length,
    )
    back_lines = jnp.einsum("kpw,wx->xpk", freq_lines * symbol, inverse, precision=highest)
    columns = lax.all_to_all(back_lines, "space", split_axis=0, concat_axis=2, tiled=True)
    real_field = jnp.einsum("xpk,ky->xpy", columns, inverse, precision=highest)
    depth_lines = lax.all_to_all(real_field, "subj", split_axis=2, concat_axis=1, tiled=True)
    smoothed = jnp.einsum("xpy,pz->xyz", depth_lines, inverse, precision=highest)
    return velocity - step_size * (2.0 * velocity - smoothed)


def body(subj, space, template_warped, subject_images, jacobians, velocity):
    _, xl, _, length = template_warped.shape
    yl = velocity.shape[1]
    power_of_two = subj & (subj - 1) == 0 and space & (space - 1) == 0
    fits = (
        subj > 1
        and power_of_two
        and length % lane == 0
        and yl % 32 == 0
        and xl >= 16
        and lane % xl == 0
        and 2 * xl == lane
        and early_eighths * length // 8 % (8 * space) == 0
        and (8 - early_eighths) * length // 8 % (8 * subj) == 0
        and yl * xl == 8 * length
    )
    if not fits:
        return transposing_body(template_warped, subject_images, jacobians, velocity)
    plan = Plan(length, xl, subj, space)
    return ring_body(plan, template_warped, subject_images, jacobians, velocity)


def solution(mesh):
    return jax.shard_map(
        functools.partial(body, mesh.shape["subj"], mesh.shape["space"]),
        mesh=mesh,
        in_specs=(
            P("subj", "space", None, None),
            P("subj", "space", None, None),
            P("subj", "space", None, None),
            P("space", "subj", None),
        ),
        out_specs=P("space", "subj", None),
        check_vma=False,
    )
```

time: 250 us -> 245 us (0.980)
  waiting for transfers between devices: 125 us -> 133 us
  starting transfers between devices: 47.7 us -> 39.9 us
  Pallas kernels: 68.6 us -> 64.2 us
    ppermute x48 -> x38, starting transfers between devices: 47.7 us -> 36.4 us  [the longest x14 20.6 us: go_round(): lax.ppermute(both[1], 'subj', to_left)]
    ppermute x48 -> x38, waiting for transfers between devices: 125 us -> 132 us  [the longest x14 83 us: go_round(): lax.ppermute(both[1], 'subj', to_left)]
    pallas_call x16 -> x15, Pallas kernels: 68.6 us -> 64.2 us  [the longest x8 42.3 us: force_blocks(): pl.pallas_call(functools.partial(force_kernel, plan), out_shape=shapes, g...]
    all_to_all x0 -> x1, starting transfers between devices: none -> 3.49 us  [ring_body(): back_late = lax.all_to_all(back_late, 'subj', 0, 0)]
    unnamed x24 -> x20, local copies, waits for them, and re-layouts: 4.82 us -> 1.77 us
  transfers between devices with their start and end apart: 48 -> 39, of which waited for: 24 -> 25; matrix products, arithmetic and copies ran while one was open for 1% -> 2% of each run, Pallas kernels for 22% -> 18%
where the time goes in v3:
time: 245 us
  waiting for transfers between devices  133 us (54%)
  Pallas kernels  64.2 us (26%)
  starting transfers between devices  39.9 us (16%)
  local copies, waits for them, and re-layouts  5.2 us (2%)
    ppermute x14, waiting for transfers between devices, go_round(): lax.ppermute(both[1], 'subj', to_left)  83 us
    pallas_call x8, Pallas kernels, force_blocks(): pl.pallas_call(functools.partial(force_kernel, plan), out_shape=shapes, g...  42.3 us
    ppermute x15, waiting for transfers between devices, go_round(): lax.ppermute(both[0], 'subj', to_right)  31.5 us
    ppermute x14, starting transfers between devices, go_round(): lax.ppermute(both[1], 'subj', to_left)  20.6 us
    pallas_call x6, Pallas kernels, call_once(): pl.pallas_call(kernel, out_shape=out_shape, in_specs=[pl.BlockSpec(memory...  17.3 us
    ppermute x15, starting transfers between devices, go_round(): lax.ppermute(both[0], 'subj', to_right)  11.5 us
    ppermute x1, waiting for transfers between devices, ring_body(): far = lax.ppermute(far, 'space', [(i, i ^ top) for i in range(space)])  11.1 us
    ppermute x7, waiting for transfers between devices, over_one(): return lax.ppermute(part, 'space', [(i, i ^ d) for i in range(plan.space)])  6.23 us
  transfers between devices with their start and end apart: 39, of which 25 were waited for; matrix products, arithmetic and copies ran while one was open for 2% of the time, Pallas kernels for 18%

profile of v3, /device:TPU:0, one launch (start us, length us, event | category | flops | bytes accessed | tf_op | source)
XLA Modules:
  0.0 244.5 jit_solution(15187311540194904131)
XLA Ops:
  1.7 5.3 %force.8 = (f32[192,1024]{1,0:T(8,128)S(1)}, f32[64,1024]{1,0:T(8,128)S(1)}, f32[192,1024]{1,0:T(8,128)S(1)}, f32[64,1024]{1,0:T(8,128)S(1)}) custom-call(s32[18]{0:T(128)S(1)} %dynamic-slice_bitcast_fusion.place_ref, bf16[2,64,256,256]{3,2,1,0:T(8,128)(2,1)} %warped.15, bf16[2,64,256,256]{3,2,1,0:T(8,128)(2,1)} %images.15, bf16[2,64,256,256]{3,2,1,0:T(8,128)(2,1)} %jac.15, ...), custom_call_target="tpu_custom_call" | custom-call | flops 1073741824 | bytes 8388608 | tf_op jit(solution)/shard_map/force/pallas_call | solution.py:175
  10.2 5.3 %force.9 = (f32[192,1024]{1,0:T(8,128)S(1)}, f32[64,1024]{1,0:T(8,128)S(1)}, f32[192,1024]{1,0:T(8,128)S(1)}, f32[64,1024]{1,0:T(8,128)S(1)}) custom-call(s32[18]{0:T(128)S(1)} %dynamic-slice_bitcast_fusion.place_ref, bf16[2,64,256,256]{3,2,1,0:T(8,128)(2,1)} %warped.15, bf16[2,64,256,256]{3,2,1,0:T(8,128)(2,1)} %images.15, bf16[2,64,256,256]{3,2,1,0:T(8,128)(2,1)} %jac.15, ...), custom_call_target="tpu_custom_call" | custom-call | flops 1073741824 | bytes 8388608 | tf_op jit(solution)/shard_map/force/pallas_call | solution.py:175
  15.5 12.2 %collective-permute-done.7 = f32[192,1024]{1,0:T(8,128)S(1)} collective-permute-done((f32[192,1024]{1,0:T(8,128)S(1)}, f32[192,1024]{1,0:T(8,128)S(1)}, u32[]{:S(2)}, u32[]{:S(2)}) %collective-permute-start.7) | collective-permute-done | bytes 786464 | tf_op jit(solution)/shard_map/ppermute | solution.py:568
  30.0 5.3 %force.10 = (f32[192,1024]{1,0:T(8,128)S(1)}, f32[64,1024]{1,0:T(8,128)S(1)}, f32[192,1024]{1,0:T(8,128)S(1)}, f32[64,1024]{1,0:T(8,128)S(1)}) custom-call(s32[18]{0:T(128)S(1)} %dynamic-slice_bitcast_fusion.place_ref, bf16[2,64,256,256]{3,2,1,0:T(8,128)(2,1)} %warped.15, bf16[2,64,256,256]{3,2,1,0:T(8,128)(2,1)} %images.15, bf16[2,64,256,256]{3,2,1,0:T(8,128)(2,1)} %jac.15, ...), custom_call_target="tpu_custom_call" | custom-call | flops 1073741824 | bytes 8388608 | tf_op jit(solution)/shard_map/force/pallas_call | solution.py:175
  35.3 11.2 %collective-permute-done.8 = f32[192,1024]{1,0:T(8,128)S(1)} collective-permute-done((f32[192,1024]{1,0:T(8,128)S(1)}, f32[192,1024]{1,0:T(8,128)S(1)}, u32[]{:S(2)}, u32[]{:S(2)}) %collective-permute-start.8) | collective-permute-done | bytes 786464 | tf_op jit(solution)/shard_map/ppermute | solution.py:568
  48.9 5.3 %force.11 = (f32[192,1024]{1,0:T(8,128)S(1)}, f32[64,1024]{1,0:T(8,128)S(1)}, f32[192,1024]{1,0:T(8,128)S(1)}, f32[64,1024]{1,0:T(8,128)S(1)}) custom-call(s32[18]{0:T(128)S(1)} %dynamic-slice_bitcast_fusion.place_ref, bf16[2,64,256,256]{3,2,1,0:T(8,128)(2,1)} %warped.15, bf16[2,64,256,256]{3,2,1,0:T(8,128)(2,1)} %images.15, bf16[2,64,256,256]{3,2,1,0:T(8,128)(2,1)} %jac.15, ...), custom_call_target="tpu_custom_call" | custom-call | flops 1073741824 | bytes 8388608 | tf_op jit(solution)/shard_map/force/pallas_call | solution.py:175
  54.2 10.3 %collective-permute-done.9 = f32[192,1024]{1,0:T(8,128)S(1)} collective-permute-done((f32[192,1024]{1,0:T(8,128)S(1)}, f32[192,1024]{1,0:T(8,128)S(1)}, u32[]{:S(2)}, u32[]{:S(2)}) %collective-permute-start.9) | collective-permute-done | bytes 786464 | tf_op jit(solution)/shard_map/ppermute | solution.py:568
  66.8 5.3 %force.12 = (f32[192,1024]{1,0:T(8,128)S(1)}, f32[64,1024]{1,0:T(8,128)S(1)}, f32[192,1024]{1,0:T(8,128)S(1)}, f32[64,1024]{1,0:T(8,128)S(1)}) custom-call(s32[18]{0:T(128)S(1)} %dynamic-slice_bitcast_fusion.place_ref, bf16[2,64,256,256]{3,2,1,0:T(8,128)(2,1)} %warped.15, bf16[2,64,256,256]{3,2,1,0:T(8,128)(2,1)} %images.15, bf16[2,64,256,256]{3,2,1,0:T(8,128)(2,1)} %jac.15, ...), custom_call_target="tpu_custom_call" | custom-call | flops 1073741824 | bytes 8388608 | tf_op jit(solution)/shard_map/force/pallas_call | solution.py:175
  72.1 10.1 %collective-permute-done.10 = f32[192,1024]{1,0:T(8,128)S(1)} collective-permute-done((f32[192,1024]{1,0:T(8,128)S(1)}, f32[192,1024]{1,0:T(8,128)S(1)}, u32[]{:S(2)}, u32[]{:S(2)}) %collective-permute-start.10) | collective-permute-done | bytes 786464 | tf_op jit(solution)/shard_map/ppermute | solution.py:568
  84.7 5.3 %force.13 = (f32[192,1024]{1,0:T(8,128)S(1)}, f32[64,1024]{1,0:T(8,128)S(1)}, f32[192,1024]{1,0:T(8,128)S(1)}, f32[64,1024]{1,0:T(8,128)S(1)}) custom-call(s32[18]{0:T(128)S(1)} %dynamic-slice_bitcast_fusion.place_ref, bf16[2,64,256,256]{3,2,1,0:T(8,128)(2,1)} %warped.15, bf16[2,64,256,256]{3,2,1,0:T(8,128)(2,1)} %images.15, bf16[2,64,256,256]{3,2,1,0:T(8,128)(2,1)} %jac.15, ...), custom_call_target="tpu_custom_call" | custom-call | flops 1073741824 | bytes 8388608 | tf_op jit(solution)/shard_map/force/pallas_call | solution.py:175
  90.0 9.9 %collective-permute-done.11 = f32[192,1024]{1,0:T(8,128)S(1)} collective-permute-done((f32[192,1024]{1,0:T(8,128)S(1)}, f32[192,1024]{1,0:T(8,128)S(1)}, u32[]{:S(2)}, u32[]{:S(2)}) %collective-permute-start.11) | collective-permute-done | bytes 786464 | tf_op jit(solution)/shard_map/ppermute | solution.py:568
  102.3 5.3 %force.14 = (f32[192,1024]{1,0:T(8,128)S(1)}, f32[64,1024]{1,0:T(8,128)S(1)}, f32[192,1024]{1,0:T(8,128)S(1)}, f32[64,1024]{1,0:T(8,128)S(1)}) custom-call(s32[18]{0:T(128)S(1)} %dynamic-slice_bitcast_fusion.place_ref, bf16[2,64,256,256]{3,2,1,0:T(8,128)(2,1)} %warped.15, bf16[2,64,256,256]{3,2,1,0:T(8,128)(2,1)} %images.15, bf16[2,64,256,256]{3,2,1,0:T(8,128)(2,1)} %jac.15, ...), custom_call_target="tpu_custom_call" | custom-call | flops 1073741824 | bytes 8388608 | tf_op jit(solution)/shard_map/force/pallas_call | solution.py:175
  107.5 10.0 %collective-permute-done.12 = f32[192,1024]{1,0:T(8,128)S(1)} collective-permute-done((f32[192,1024]{1,0:T(8,128)S(1)}, f32[192,1024]{1,0:T(8,128)S(1)}, u32[]{:S(2)}, u32[]{:S(2)}) %collective-permute-start.12) | collective-permute-done | bytes 786464 | tf_op jit(solution)/shard_map/ppermute | solution.py:568
  120.0 5.3 %force.15 = (f32[192,1024]{1,0:T(8,128)S(1)}, f32[64,1024]{1,0:T(8,128)S(1)}, f32[192,1024]{1,0:T(8,128)S(1)}, f32[64,1024]{1,0:T(8,128)S(1)}) custom-call(s32[18]{0:T(128)S(1)} %dynamic-slice_bitcast_fusion.place_ref, bf16[2,64,256,256]{3,2,1,0:T(8,128)(2,1)} %warped.15, bf16[2,64,256,256]{3,2,1,0:T(8,128)(2,1)} %images.15, bf16[2,64,256,256]{3,2,1,0:T(8,128)(2,1)} %jac.15, ...), custom_call_target="tpu_custom_call" | custom-call | flops 1073741824 | bytes 8388608 | tf_op jit(solution)/shard_map/force/pallas_call | solution.py:175
  137.6 5.4 %collective-permute-done.16 = f32[64,1024]{1,0:T(8,128)S(1)} collective-permute-done((f32[64,1024]{1,0:T(8,128)S(1)}, f32[64,1024]{1,0:T(8,128)S(1)}, u32[]{:S(2)}, u32[]{:S(2)}) %collective-permute-start.16) | collective-permute-done | bytes 262176 | tf_op jit(solution)/shard_map/ppermute | solution.py:568
  152.8 4.3 %collective-permute-done.20 = f32[64,1024]{1,0:T(8,128)S(1)} collective-permute-done((f32[64,1024]{1,0:T(8,128)S(1)}, f32[64,1024]{1,0:T(8,128)S(1)}, u32[]{:S(2)}, u32[]{:S(2)}) %collective-permute-start.20) | collective-permute-done | bytes 262176 | tf_op jit(solution)/shard_map/ppermute | solution.py:568
  161.0 4.2 %collective-permute-done.23 = f32[64,1024]{1,0:T(8,128)S(1)} collective-permute-done((f32[64,1024]{1,0:T(8,128)S(1)}, f32[64,1024]{1,0:T(8,128)S(1)}, u32[]{:S(2)}, u32[]{:S(2)}) %collective-permute-start.23) | collective-permute-done | bytes 262176 | tf_op jit(solution)/shard_map/ppermute | solution.py:568
  166.9 4.5 %first_forward.1 = (f32[768,512]{1,0:T(8,128)}, f32[48,1024]{1,0:T(8,128)S(1)}) custom-call(s32[18]{0:T(128)S(1)} %dynamic-slice_bitcast_fusion.place_ref, f32[4,4,48,256]{3,2,1,0:T(8,128)S(1)} %copy-done.1, bf16[4,384,512]{2,1,0:T(8,128)(2,1)} %constant.36.clone.w_ref, f32[48,2048]{1,0:T(8,128)S(1)} %get-tuple-element.117.rest_0_, ...), custom_call_target="tpu_custom_call" | custom-call | tf_op jit(solution)/shard_map/first_forward/pallas_call | solution.py:110
  173.5 8.4 %collective-permute-done.25 = f32[112,1024]{1,0:T(8,128)S(1)} collective-permute-done((f32[112,1024]{1,0:T(8,128)S(1)}, f32[112,1024]{1,0:T(8,128)S(1)}, u32[]{:S(2)}, u32[]{:S(2)}) %collective-permute-start.25) | collective-permute-done | bytes 458784 | tf_op jit(solution)/shard_map/ppermute | solution.py:568
  184.3 9.3 %collective-permute-done.26 = f32[112,1024]{1,0:T(8,128)S(1)} collective-permute-done((f32[112,1024]{1,0:T(8,128)S(1)}, f32[112,1024]{1,0:T(8,128)S(1)}, u32[]{:S(2)}, u32[]{:S(2)}) %collective-permute-start.26) | collective-permute-done | bytes 458784 | tf_op jit(solution)/shard_map/ppermute | solution.py:568
  196.0 8.4 %collective-permute-done.27.rest_2_ = f32[112,1024]{1,0:T(8,128)S(1)} collective-permute-done((f32[112,1024]{1,0:T(8,128)S(1)}, f32[112,1024]{1,0:T(8,128)S(1)}, u32[]{:S(2)}, u32[]{:S(2)}) %collective-permute-start.27) | collective-permute-done | bytes 458784 | tf_op jit(solution)/shard_map/ppermute | solution.py:568
  212.2 4.1 %second_and_back.1 = (f32[48,2048]{1,0:T(8,128)S(1)}, f32[48,2048]{1,0:T(8,128)S(1)}, f32[96,2048]{1,0:T(8,128)S(1)}) custom-call(s32[18]{0:T(128)S(1)} %dynamic-slice_bitcast_fusion.place_ref, f32[4,4,48,256]{3,2,1,0:T(8,128)S(1)} %copy-done.1, bf16[4,1536,128]{2,1,0:T(8,128)(2,1)} %constant.39.clone.v_ref, f32[768,512]{1,0:T(8,128)} %get-tuple-element.128.f_ref, ...), custom_call_target="tpu_custom_call" | custom-call | tf_op jit(solution)/shard_map/second_and_back/pallas_call | solution.py:110
  224.9 11.1 %collective-permute-done.36 = f32[96,2048]{1,0:T(8,128)} collective-permute-done((f32[96,2048]{1,0:T(8,128)S(1)}, f32[96,2048]{1,0:T(8,128)}, u32[]{:S(2)}, u32[]{:S(2)}) %collective-permute-start.36) | collective-permute-done | bytes 786464 | tf_op jit(solution)/shard_map/ppermute | solution.py:618
  239.9 4.6 %last_back.1 = f32[64,32,256]{2,1,0:T(8,128)} custom-call(s32[18]{0:T(128)S(1)} %dynamic-slice_bitcast_fusion.place_ref, bf16[2,256,256]{2,1,0:T(8,128)(2,1)S(1)} %copy-done.6, f32[64,32,256]{2,1,0:T(8,128)} %velocity.1, f32[48,2048]{1,0:T(8,128)S(1)} %get-tuple-element.131.rest_0_, f32[48,2048]{1,0:T(8,128)S(1)} %collective-permute-done.35.rest_1_, ...), custom_call_target="tpu_custom_call" | custom-call | tf_op jit(solution)/shard_map/last_back/pallas_call | solution.py:527
  (129 shorter events, 73.7 us)
Async XLA Ops:
  7.0 20.6 %collective-permute-start.7 = (f32[192,1024]{1,0:T(8,128)S(1)}, f32[192,1024]{1,0:T(8,128)S(1)}, u32[]{:S(2)}, u32[]{:S(2)}) collective-permute-start(f32[192,1024]{1,0:T(8,128)S(1)} %get-tuple-element.99), channel_id=1, source_target_pairs={{8,0},{16,8},{24,16},{28,24},{20,28},{12,20},{4,12},{0,4},{9,1},{1... | collective-permute-start | bytes 2359304 | tf_op jit(solution)/shard_map/ppermute | solution.py:568
  10.0 19.5 %collective-permute-start = (f32[192,1024]{1,0:T(8,128)S(1)}, f32[192,1024]{1,0:T(8,128)S(1)}, u32[]{:S(2)}, u32[]{:S(2)}) collective-permute-start(f32[192,1024]{1,0:T(8,128)S(1)} %get-tuple-element.92), channel_id=1, source_target_pairs={{0,8},{8,16},{16,24},{24,28},{28,20},{20,12},{12,4},{4,0},{1,9},{9... | collective-permute-start | bytes 2359304 | tf_op jit(solution)/shard_map/ppermute | solution.py:568
  27.8 18.8 %collective-permute-start.8 = (f32[192,1024]{1,0:T(8,128)S(1)}, f32[192,1024]{1,0:T(8,128)S(1)}, u32[]{:S(2)}, u32[]{:S(2)}) collective-permute-start(f32[192,1024]{1,0:T(8,128)S(1)} %add.86), channel_id=1, source_target_pairs={{8,0},{16,8},{24,16},{28,24},{20,28},{12,20},{4,12},{0,4},{9,1},{1... | collective-permute-start | bytes 2359304 | tf_op jit(solution)/shard_map/ppermute | solution.py:568
  29.6 18.5 %collective-permute-start.1 = (f32[192,1024]{1,0:T(8,128)S(1)}, f32[192,1024]{1,0:T(8,128)S(1)}, u32[]{:S(2)}, u32[]{:S(2)}) collective-permute-start(f32[192,1024]{1,0:T(8,128)S(1)} %add.80), channel_id=1, source_target_pairs={{0,8},{8,16},{16,24},{24,28},{28,20},{20,12},{12,4},{4,0},{1,9},{9... | collective-permute-start | bytes 2359304 | tf_op jit(solution)/shard_map/ppermute | solution.py:568
  46.6 17.8 %collective-permute-start.9 = (f32[192,1024]{1,0:T(8,128)S(1)}, f32[192,1024]{1,0:T(8,128)S(1)}, u32[]{:S(2)}, u32[]{:S(2)}) collective-permute-start(f32[192,1024]{1,0:T(8,128)S(1)} %add.87), channel_id=1, source_target_pairs={{8,0},{16,8},{24,16},{28,24},{20,28},{12,20},{4,12},{0,4},{9,1},{1... | collective-permute-start | bytes 2359304 | tf_op jit(solution)/shard_map/ppermute | solution.py:568
  48.2 17.6 %collective-permute-start.2 = (f32[192,1024]{1,0:T(8,128)S(1)}, f32[192,1024]{1,0:T(8,128)S(1)}, u32[]{:S(2)}, u32[]{:S(2)}) collective-permute-start(f32[192,1024]{1,0:T(8,128)S(1)} %add.81), channel_id=1, source_target_pairs={{0,8},{8,16},{16,24},{24,28},{28,20},{20,12},{12,4},{4,0},{1,9},{9... | collective-permute-start | bytes 2359304 | tf_op jit(solution)/shard_map/ppermute | solution.py:568
  64.6 17.6 %collective-permute-start.10 = (f32[192,1024]{1,0:T(8,128)S(1)}, f32[192,1024]{1,0:T(8,128)S(1)}, u32[]{:S(2)}, u32[]{:S(2)}) collective-permute-start(f32[192,1024]{1,0:T(8,128)S(1)} %add.88), channel_id=1, source_target_pairs={{8,0},{16,8},{24,16},{28,24},{20,28},{12,20},{4,12},{0,4},{9,1},{1... | collective-permute-start | bytes 2359304 | tf_op jit(solution)/shard_map/ppermute | solution.py:568
  65.9 17.6 %collective-permute-start.3 = (f32[192,1024]{1,0:T(8,128)S(1)}, f32[192,1024]{1,0:T(8,128)S(1)}, u32[]{:S(2)}, u32[]{:S(2)}) collective-permute-start(f32[192,1024]{1,0:T(8,128)S(1)} %add.82), channel_id=1, source_target_pairs={{0,8},{8,16},{16,24},{24,28},{28,20},{20,12},{12,4},{4,0},{1,9},{9... | collective-permute-start | bytes 2359304 | tf_op jit(solution)/shard_map/ppermute | solution.py:568
  82.3 17.6 %collective-permute-start.11 = (f32[192,1024]{1,0:T(8,128)S(1)}, f32[192,1024]{1,0:T(8,128)S(1)}, u32[]{:S(2)}, u32[]{:S(2)}) collective-permute-start(f32[192,1024]{1,0:T(8,128)S(1)} %add.89), channel_id=1, source_target_pairs={{8,0},{16,8},{24,16},{28,24},{20,28},{12,20},{4,12},{0,4},{9,1},{1... | collective-permute-start | bytes 2359304 | tf_op jit(solution)/shard_map/ppermute | solution.py:568
  83.6 17.6 %collective-permute-start.4 = (f32[192,1024]{1,0:T(8,128)S(1)}, f32[192,1024]{1,0:T(8,128)S(1)}, u32[]{:S(2)}, u32[]{:S(2)}) collective-permute-start(f32[192,1024]{1,0:T(8,128)S(1)} %add.83), channel_id=1, source_target_pairs={{0,8},{8,16},{16,24},{24,28},{28,20},{20,12},{12,4},{4,0},{1,9},{9... | collective-permute-start | bytes 2359304 | tf_op jit(solution)/shard_map/ppermute | solution.py:568
  100.0 17.6 %collective-permute-start.12 = (f32[192,1024]{1,0:T(8,128)S(1)}, f32[192,1024]{1,0:T(8,128)S(1)}, u32[]{:S(2)}, u32[]{:S(2)}) collective-permute-start(f32[192,1024]{1,0:T(8,128)S(1)} %add.90), channel_id=1, source_target_pairs={{8,0},{16,8},{24,16},{28,24},{20,28},{12,20},{4,12},{0,4},{9,1},{1... | collective-permute-start | bytes 2359304 | tf_op jit(solution)/shard_map/ppermute | solution.py:568
  101.3 17.6 %collective-permute-start.5 = (f32[192,1024]{1,0:T(8,128)S(1)}, f32[192,1024]{1,0:T(8,128)S(1)}, u32[]{:S(2)}, u32[]{:S(2)}) collective-permute-start(f32[192,1024]{1,0:T(8,128)S(1)} %add.84), channel_id=1, source_target_pairs={{0,8},{8,16},{16,24},{24,28},{28,20},{20,12},{12,4},{4,0},{1,9},{9... | collective-permute-start | bytes 2359304 | tf_op jit(solution)/shard_map/ppermute | solution.py:568
  117.7 15.5 %collective-permute-start.13 = (f32[192,1024]{1,0:T(8,128)S(1)}, f32[192,1024]{1,0:T(8,128)S(1)}, u32[]{:S(2)}, u32[]{:S(2)}) collective-permute-start(f32[192,1024]{1,0:T(8,128)S(1)} %add.91), channel_id=1, source_target_pairs={{8,0},{16,8},{24,16},{28,24},{20,28},{12,20},{4,12},{0,4},{9,1},{1... | collective-permute-start | bytes 2359304 | tf_op jit(solution)/shard_map/ppermute | solution.py:568
  119.0 15.1 %collective-permute-start.6 = (f32[192,1024]{1,0:T(8,128)S(1)}, f32[192,1024]{1,0:T(8,128)S(1)}, u32[]{:S(2)}, u32[]{:S(2)}) collective-permute-start(f32[192,1024]{1,0:T(8,128)S(1)} %add.85), channel_id=1, source_target_pairs={{0,8},{8,16},{16,24},{24,28},{28,20},{20,12},{12,4},{4,0},{1,9},{9... | collective-permute-start | bytes 2359304 | tf_op jit(solution)/shard_map/ppermute | solution.py:568
  145.3 13.5 %collective-permute-start.21 = (f32[96,2048]{1,0:T(8,128)S(1)}, f32[96,2048]{1,0:T(8,128)S(1)}, u32[]{:S(2)}, u32[]{:S(2)}) collective-permute-start(f32[96,2048]{1,0:T(8,128)S(1)} %pad_maximum_fusion), channel_id=1, source_target_pairs={{0,2},{1,3},{2,0},{3,1},{4,6},{5,7},{6,4},{7,5},{8,10},{9,11},{10,... | collective-permute-start | bytes 2359304 | tf_op jit(solution)/shard_map/ppermute | solution.py:586
  171.4 10.5 %collective-permute-start.25 = (f32[112,1024]{1,0:T(8,128)S(1)}, f32[112,1024]{1,0:T(8,128)S(1)}, u32[]{:S(2)}, u32[]{:S(2)}) collective-permute-start(f32[112,1024]{1,0:T(8,128)S(1)} %get-tuple-element.148), channel_id=1, source_target_pairs={{0,8},{8,16},{16,24},{24,28},{28,20},{20,12},{12,4},{4,0},{1,9},{9... | collective-permute-start | bytes 1376264 | tf_op jit(solution)/shard_map/ppermute | solution.py:568
  171.9 11.0 %collective-permute-start.28 = (f32[112,1024]{1,0:T(8,128)S(1)}, f32[112,1024]{1,0:T(8,128)S(1)}, u32[]{:S(2)}, u32[]{:S(2)}) collective-permute-start(f32[112,1024]{1,0:T(8,128)S(1)} %get-tuple-element.147), channel_id=1, source_target_pairs={{8,0},{16,8},{24,16},{28,24},{20,28},{12,20},{4,12},{0,4},{9,1},{1... | collective-permute-start | bytes 1376264 | tf_op jit(solution)/shard_map/ppermute | solution.py:568
  182.0 11.6 %collective-permute-start.26 = (f32[112,1024]{1,0:T(8,128)S(1)}, f32[112,1024]{1,0:T(8,128)S(1)}, u32[]{:S(2)}, u32[]{:S(2)}) collective-permute-start(f32[112,1024]{1,0:T(8,128)S(1)} %pad_maximum_fusion.3), channel_id=1, source_target_pairs={{0,8},{8,16},{16,24},{24,28},{28,20},{20,12},{12,4},{4,0},{1,9},{9... | collective-permute-start | bytes 1376264 | tf_op jit(solution)/shard_map/ppermute | solution.py:568
  183.0 12.2 %collective-permute-start.29 = (f32[112,1024]{1,0:T(8,128)S(1)}, f32[112,1024]{1,0:T(8,128)S(1)}, u32[]{:S(2)}, u32[]{:S(2)}) collective-permute-start(f32[112,1024]{1,0:T(8,128)S(1)} %pad_maximum_fusion.5), channel_id=1, source_target_pairs={{8,0},{16,8},{24,16},{28,24},{20,28},{12,20},{4,12},{0,4},{9,1},{1... | collective-permute-start | bytes 1376264 | tf_op jit(solution)/shard_map/ppermute | solution.py:568
  193.7 10.6 %collective-permute-start.27 = (f32[112,1024]{1,0:T(8,128)S(1)}, f32[112,1024]{1,0:T(8,128)S(1)}, u32[]{:S(2)}, u32[]{:S(2)}) collective-permute-start(f32[112,1024]{1,0:T(8,128)S(1)} %pad_maximum_fusion.4), channel_id=1, source_target_pairs={{0,8},{8,16},{16,24},{24,28},{28,20},{20,12},{12,4},{4,0},{1,9},{9... | collective-permute-start | bytes 1376264 | tf_op jit(solution)/shard_map/ppermute | solution.py:568
  195.3 10.6 %collective-permute-start.30 = (f32[112,1024]{1,0:T(8,128)S(1)}, f32[112,1024]{1,0:T(8,128)S(1)}, u32[]{:S(2)}, u32[]{:S(2)}) collective-permute-start(f32[112,1024]{1,0:T(8,128)S(1)} %pad_maximum_fusion.6), channel_id=1, source_target_pairs={{8,0},{16,8},{24,16},{28,24},{20,28},{12,20},{4,12},{0,4},{9,1},{1... | collective-permute-start | bytes 1376264 | tf_op jit(solution)/shard_map/ppermute | solution.py:568
  204.4 7.8 %collective-permute-start.34 = (f32[48,1024]{1,0:T(8,128)S(1)}, f32[48,1024]{1,0:T(8,128)S(1)}, u32[]{:S(2)}, u32[]{:S(2)}) collective-permute-start(f32[48,1024]{1,0:T(8,128)S(1)} %slice.128.rest_5_), channel_id=1, source_target_pairs={{0,8},{8,16},{16,24},{24,28},{28,20},{20,12},{12,4},{4,0},{1,9},{9... | collective-permute-start | bytes 589832 | tf_op jit(solution)/shard_map/ppermute | solution.py:568
  216.3 19.8 %collective-permute-start.36 = (f32[96,2048]{1,0:T(8,128)S(1)}, f32[96,2048]{1,0:T(8,128)}, u32[]{:S(2)}, u32[]{:S(2)}) collective-permute-start(f32[96,2048]{1,0:T(8,128)S(1)} %get-tuple-element.133), channel_id=1, source_target_pairs={{0,2},{1,3},{2,0},{3,1},{4,6},{5,7},{6,4},{7,5},{8,10},{9,11},{10,... | collective-permute-start | bytes 2359304 | tf_op jit(solution)/shard_map/ppermute | solution.py:618
  221.4 18.5 %all-to-all-start = ((f32[8,8,2048]{2,1,0:T(8,128)}), f32[8,8,2048]{2,1,0:T(8,128)S(1)}, u32[]{:S(2)}, u32[]{:S(2)}) async-start(f32[8,8,2048]{2,1,0:T(8,128)} %first_and_back.1), calls=%async_computation | async-start | bytes 1048576 | tf_op jit(solution)/shard_map/all_to_all | solution.py:622
  (25 other events, 170.1 us)

commit v4 on v3

--- a/solution.py
+++ b/solution.py
@@ -17,6 +17,7 @@
 vmem_bytes = 50 * 1024 * 1024
 lane = 128
 early_eighths = 6
+early_parts = 2
 near_step, far_step, ends_step = 3, 4, 5
 
 
@@ -48,7 +49,7 @@
         early = length * early_eighths // 8
         self.early, self.late = early, length - early
         self.chunks = [self.early, self.late]
-        self.offs = [0, early]
+        self.part = early // early_parts
         self.g, self.gl = self.early // space, self.late // subj
         ring = list(range(0, subj, 2)) + list(range(subj - 1, 0, -2))
         self.ring = ring
@@ -125,7 +126,7 @@
 def force_kernel(plan, place_ref, warped, images, jac, table, *rest):
     outs, field = rest[:-1], rest[-1]
     me = place_ref[plan.at_space]
-    n = len(plan.chunks)
+    n = len(outs) // 2
     way = pl.program_id(0)
     yh = plan.yl // 2
     count = warped.shape[0]
@@ -142,19 +143,22 @@
     field[...] = jnp.swapaxes(total.reshape(plan.xl, yh, length), 0, 1)
 
     def transform(refs):
+        starts = [pl.multiple_of((me ^ d) * plan.g, 16) for d in range(plan.space)]
+        rows_of = [table[pl.ds(start, plan.g), length:] for start in starts]
+        ordered = jnp.concatenate([*rows_of, table[plan.early :, length:]], axis=0)
         per = max(1, 256 // plan.xl)
         for y0 in range(0, yh, per):
             lines = field[y0 : y0 + per].reshape(per * plan.xl, length)
             high, low = split(lines)
             both = jnp.concatenate([high, low, high], axis=1)
             out = lax.dot_general(
-                table[:, length:], both, (((1,), (1,)), ((), ())), preferred_element_type=jnp.float32
+                ordered, both, (((1,), (1,)), ((), ())), preferred_element_type=jnp.float32
             )
             cols = slice(y0 * plan.xl, (y0 + per) * plan.xl)
-            for d in range(plan.space):
-                rows = pl.ds(pl.multiple_of((me ^ d) * plan.g, 8), plan.g)
-                refs[0][rows, cols] = out[d * plan.g : (d + 1) * plan.g]
-            refs[1][:, cols] = out[plan.early :]
+            first = 0
+            for ref in refs:
+                ref[:, cols] = out[first : first + ref.shape[0]]
+                first += ref.shape[0]
 
     @pl.when(way == 0)
     def _():
@@ -171,7 +175,8 @@
     source = pl.BlockSpec(
         (count, xl, yh, length), lambda way, place: (0, 0, 2 * place[2 * k + way] + way, 0)
     )
-    shapes = [jax.ShapeDtypeStruct((c, plan.half), jnp.float32) for c in plan.chunks] * 2
+    sizes = [plan.part] * early_parts + [plan.late]
+    shapes = [jax.ShapeDtypeStruct((c, plan.half), jnp.float32) for c in sizes] * 2
     outs = pl.pallas_call(
         functools.partial(force_kernel, plan),
         out_shape=shapes,
@@ -195,18 +200,22 @@
         ),
         name="force",
     )(place, warped, images, jac, jnp.asarray(plan.d_table))
-    n = len(plan.chunks)
+    n = len(sizes)
     return outs[:n], outs[n:]
 
 
-def join_kernel(plan, place_ref, right_local, left_local, right, left, *outs):
+def join_kernel(plan, place_ref, *rest):
+    arrived, outs = rest[: -plan.space], rest[-plan.space :]
+    per = plan.part // plan.g
     for d, out in enumerate(outs):
-        rows = slice(d * plan.g, (d + 1) * plan.g)
-        out[:, : plan.half] = right[rows] + right_local[rows]
-        out[:, plan.half :] = left[rows] + left_local[rows]
-
-
-def join(plan, place, *args):
+        part, at = d // per, d % per * plan.g
+        for way in range(2):
+            mine, came = arrived[(2 * part + way) * 2 : (2 * part + way) * 2 + 2]
+            cols = slice(way * plan.half, (way + 1) * plan.half)
+            out[:, cols] = mine[at : at + plan.g] + came[at : at + plan.g]
+
+
+def join(plan, place, args):
     return call_once(
         functools.partial(join_kernel, plan),
         "join",
@@ -572,13 +581,19 @@
         for k in range(subj)
     ]
 
-    both = local[0][0][0], local[0][1][0]
+    parts = range(early_parts)
+    streams = [(local[0][0][p], local[0][1][p]) for p in parts]
     for k in range(1, subj):
-        both = go_round(both)
+        streams = [go_round(both) for both in streams]
         if k < subj - 1:
-            both = tuple(b + local[k][way][0] for way, b in enumerate(both))
-    pieces = join(plan, place, local[-1][0][0], local[-1][1][0], *both)
-    late = regroup(plan, place, [local[k][way][1] for k in range(subj) for way in range(2)])
+            streams = [
+                tuple(b + local[k][way][p] for way, b in enumerate(both))
+                for p, both in enumerate(streams)
+            ]
+    pieces = join(
+        plan, place, [a for p in parts for way in range(2) for a in (local[-1][way][p], streams[p][way])]
+    )
+    late = regroup(plan, place, [local[k][way][-1] for k in range(subj) for way in range(2)])
 
     top = space // 2
     both, own = tie((late[0][0], late[1][0]), pieces[0])
@@ -595,14 +610,14 @@
             both, far = tie(both, far)
             far = [far[d * plan.g : (d + 1) * plan.g] for d in range(top)]
             f, ends = forward_lines(plan, place, [*moved, *over_space(plan, far)])
-        if k == ends_step:
-            both, (f, ends) = tie(both, (f, ends))
         if k >= ends_step and len(arrived) < half:
             extra = arrived[-1] if arrived else (ends, ends)
             both = tuple(jnp.concatenate([b, e]) for b, e in zip(both, extra))
         both = go_round(both)
         if both[0].shape[0] > plan.late:
             arrived.append(tuple(b[plan.late :] for b in both))
+        if k == far_step:
+            both, (f, ends) = tie(both, (f, ends))
         if k < subj - 1:
             both = tuple(b[: plan.late] + late[way][k] for way, b in enumerate(both))
     while len(arrived) < half:
@@ -615,10 +630,11 @@
     others = [over_one(plan, ends_late, d) for d in range(space)]
     f, others = tie(f, others)
     *back, far = backward_lines(plan, place, f, all_ends[:subj])
+    f_late, back[0] = tie(f_late, back[0])
     far = lax.ppermute(far, "space", [(i, i ^ top) for i in range(space)])
     back = over_space(plan, back)
-    f_late, back = tie(f_late, back)
     back_late = late_backward(plan, place, f_late, others)
+    back_late, back = tie(back_late, back)
     back_late = lax.all_to_all(back_late, "subj", 0, 0)
     back_late = back_late.reshape(plan.late, plan.lanes)
     far = [far[d * plan.g : (d + 1) * plan.g] for d in range(top)]
@@ -685,6 +701,8 @@
         and xl >= 16
         and lane % xl == 0
         and 2 * xl == lane
+        and early_eighths * length // 8 % (16 * space) == 0
+        and space % early_parts == 0
         and early_eighths * length // 8 % (8 * space) == 0
         and (8 - early_eighths) * length // 8 % (8 * subj) == 0
         and yl * xl == 8 * length

time: 245 us -> 241 us (0.984)
  waiting for transfers between devices: 133 us -> 113 us
  starting transfers between devices: 39.9 us -> 56.6 us
    ppermute x14 -> x21, waiting for transfers between devices: 83 us -> 60.3 us  [go_round(): lax.ppermute(both[1], 'subj', to_left)]
    ppermute x14 -> x21, starting transfers between devices: 20.6 us -> 41.1 us  [go_round(): lax.ppermute(both[1], 'subj', to_left)]
    ppermute x15 -> x22, starting transfers between devices: 11.5 us -> 5.94 us  [go_round(): lax.ppermute(both[0], 'subj', to_right)]
    ppermute x15 -> x22, waiting for transfers between devices: 31.5 us -> 36.2 us  [go_round(): lax.ppermute(both[0], 'subj', to_right)]
  transfers between devices with their start and end apart: 39 -> 53, of which waited for: 25 -> 29; matrix products, arithmetic and copies ran while one was open for 2% -> 1% of each run, Pallas kernels for 18% -> 20%
where the time goes in v4:
time: 241 us
  waiting for transfers between devices  113 us (47%)
  Pallas kernels  64 us (27%)
  starting transfers between devices  56.6 us (23%)
  local copies, waits for them, and re-layouts  4.63 us (2%)
    ppermute x21, waiting for transfers between devices, go_round(): lax.ppermute(both[1], 'subj', to_left)  60.3 us
    pallas_call x8, Pallas kernels, force_blocks(): pl.pallas_call(functools.partial(force_kernel, plan), out_shape=shapes, g...  42.2 us
    ppermute x21, starting transfers between devices, go_round(): lax.ppermute(both[1], 'subj', to_left)  41.1 us
    ppermute x22, waiting for transfers between devices, go_round(): lax.ppermute(both[0], 'subj', to_right)  36.2 us
    pallas_call x6, Pallas kernels, call_once(): pl.pallas_call(kernel, out_shape=out_shape, in_specs=[pl.BlockSpec(memory...  17.2 us
    ppermute x1, waiting for transfers between devices, ring_body(): far = lax.ppermute(far, 'space', [(i, i ^ top) for i in range(space)])  11.9 us
    ppermute x22, starting transfers between devices, go_round(): lax.ppermute(both[0], 'subj', to_right)  5.94 us
  transfers between devices with their start and end apart: 53, of which 29 were waited for; matrix products, arithmetic and copies ran while one was open for 1% of the time, Pallas kernels for 20%

profile of v4, /device:TPU:0, one launch (start us, length us, event | category | flops | bytes accessed | tf_op | source)
XLA Modules:
  0.0 240.8 jit_solution(7451602258369814805)
XLA Ops:
  1.7 5.3 %force.8 = (f32[96,1024]{1,0:T(8,128)S(1)}, f32[96,1024]{1,0:T(8,128)S(1)}, f32[64,1024]{1,0:T(8,128)S(1)}, f32[96,1024]{1,0:T(8,128)S(1)}, f32[96,1024]{1,0:T(8,128)S(1)}, /*index=5*/f32[64,1024]{1,0:T(8,128)S(1)}) custom-call(s32[18]{0:T(128)S(1)} %dynamic-slice_bitcast_fusion.place_ref, bf16[2,64,256,256]{3,2,1,0:T(8,128)(2,1)} %warped.15, ...), custom_call_target="tpu_custom_call" | custom-call | flops 1073741824 | bytes 8388608 | tf_op jit(solution)/shard_map/force/pallas_call | solution.py:180
  12.2 5.3 %force.9 = (f32[96,1024]{1,0:T(8,128)S(1)}, f32[96,1024]{1,0:T(8,128)S(1)}, f32[64,1024]{1,0:T(8,128)S(1)}, f32[96,1024]{1,0:T(8,128)S(1)}, f32[96,1024]{1,0:T(8,128)S(1)}, /*index=5*/f32[64,1024]{1,0:T(8,128)S(1)}) custom-call(s32[18]{0:T(128)S(1)} %dynamic-slice_bitcast_fusion.place_ref, bf16[2,64,256,256]{3,2,1,0:T(8,128)(2,1)} %warped.15, ...), custom_call_target="tpu_custom_call" | custom-call | flops 1073741824 | bytes 8388608 | tf_op jit(solution)/shard_map/force/pallas_call | solution.py:180
  22.3 6.1 %collective-permute-done.21 = f32[96,1024]{1,0:T(8,128)S(1)} collective-permute-done((f32[96,1024]{1,0:T(8,128)S(1)}, f32[96,1024]{1,0:T(8,128)S(1)}, u32[]{:S(2)}, u32[]{:S(2)}) %collective-permute-start.21) | collective-permute-done | bytes 393248 | tf_op jit(solution)/shard_map/ppermute | solution.py:577
  30.8 5.3 %force.10 = (f32[96,1024]{1,0:T(8,128)S(1)}, f32[96,1024]{1,0:T(8,128)S(1)}, f32[64,1024]{1,0:T(8,128)S(1)}, f32[96,1024]{1,0:T(8,128)S(1)}, f32[96,1024]{1,0:T(8,128)S(1)}, /*index=5*/f32[64,1024]{1,0:T(8,128)S(1)}) custom-call(s32[18]{0:T(128)S(1)} %dynamic-slice_bitcast_fusion.place_ref, bf16[2,64,256,256]{3,2,1,0:T(8,128)(2,1)} %warped.15, ...), custom_call_target="tpu_custom_call" | custom-call | flops 1073741824 | bytes 8388608 | tf_op jit(solution)/shard_map/force/pallas_call | solution.py:180
  39.2 6.1 %collective-permute-done.22 = f32[96,1024]{1,0:T(8,128)S(1)} collective-permute-done((f32[96,1024]{1,0:T(8,128)S(1)}, f32[96,1024]{1,0:T(8,128)S(1)}, u32[]{:S(2)}, u32[]{:S(2)}) %collective-permute-start.22) | collective-permute-done | bytes 393248 | tf_op jit(solution)/shard_map/ppermute | solution.py:577
  47.6 5.3 %force.11 = (f32[96,1024]{1,0:T(8,128)S(1)}, f32[96,1024]{1,0:T(8,128)S(1)}, f32[64,1024]{1,0:T(8,128)S(1)}, f32[96,1024]{1,0:T(8,128)S(1)}, f32[96,1024]{1,0:T(8,128)S(1)}, /*index=5*/f32[64,1024]{1,0:T(8,128)S(1)}) custom-call(s32[18]{0:T(128)S(1)} %dynamic-slice_bitcast_fusion.place_ref, bf16[2,64,256,256]{3,2,1,0:T(8,128)(2,1)} %warped.15, ...), custom_call_target="tpu_custom_call" | custom-call | flops 1073741824 | bytes 8388608 | tf_op jit(solution)/shard_map/force/pallas_call | solution.py:180
  56.0 6.1 %collective-permute-done.23 = f32[96,1024]{1,0:T(8,128)S(1)} collective-permute-done((f32[96,1024]{1,0:T(8,128)S(1)}, f32[96,1024]{1,0:T(8,128)S(1)}, u32[]{:S(2)}, u32[]{:S(2)}) %collective-permute-start.23) | collective-permute-done | bytes 393248 | tf_op jit(solution)/shard_map/ppermute | solution.py:577
  64.5 5.3 %force.12 = (f32[96,1024]{1,0:T(8,128)S(1)}, f32[96,1024]{1,0:T(8,128)S(1)}, f32[64,1024]{1,0:T(8,128)S(1)}, f32[96,1024]{1,0:T(8,128)S(1)}, f32[96,1024]{1,0:T(8,128)S(1)}, /*index=5*/f32[64,1024]{1,0:T(8,128)S(1)}) custom-call(s32[18]{0:T(128)S(1)} %dynamic-slice_bitcast_fusion.place_ref, bf16[2,64,256,256]{3,2,1,0:T(8,128)(2,1)} %warped.15, ...), custom_call_target="tpu_custom_call" | custom-call | flops 1073741824 | bytes 8388608 | tf_op jit(solution)/shard_map/force/pallas_call | solution.py:180
  72.9 6.1 %collective-permute-done.24 = f32[96,1024]{1,0:T(8,128)S(1)} collective-permute-done((f32[96,1024]{1,0:T(8,128)S(1)}, f32[96,1024]{1,0:T(8,128)S(1)}, u32[]{:S(2)}, u32[]{:S(2)}) %collective-permute-start.24) | collective-permute-done | bytes 393248 | tf_op jit(solution)/shard_map/ppermute | solution.py:577
  81.5 5.3 %force.13 = (f32[96,1024]{1,0:T(8,128)S(1)}, f32[96,1024]{1,0:T(8,128)S(1)}, f32[64,1024]{1,0:T(8,128)S(1)}, f32[96,1024]{1,0:T(8,128)S(1)}, f32[96,1024]{1,0:T(8,128)S(1)}, /*index=5*/f32[64,1024]{1,0:T(8,128)S(1)}) custom-call(s32[18]{0:T(128)S(1)} %dynamic-slice_bitcast_fusion.place_ref, bf16[2,64,256,256]{3,2,1,0:T(8,128)(2,1)} %warped.15, ...), custom_call_target="tpu_custom_call" | custom-call | flops 1073741824 | bytes 8388608 | tf_op jit(solution)/shard_map/force/pallas_call | solution.py:180
  89.7 6.1 %collective-permute-done.25 = f32[96,1024]{1,0:T(8,128)S(1)} collective-permute-done((f32[96,1024]{1,0:T(8,128)S(1)}, f32[96,1024]{1,0:T(8,128)S(1)}, u32[]{:S(2)}, u32[]{:S(2)}) %collective-permute-start.25) | collective-permute-done | bytes 393248 | tf_op jit(solution)/shard_map/ppermute | solution.py:577
  98.2 5.3 %force.14 = (f32[96,1024]{1,0:T(8,128)S(1)}, f32[96,1024]{1,0:T(8,128)S(1)}, f32[64,1024]{1,0:T(8,128)S(1)}, f32[96,1024]{1,0:T(8,128)S(1)}, f32[96,1024]{1,0:T(8,128)S(1)}, /*index=5*/f32[64,1024]{1,0:T(8,128)S(1)}) custom-call(s32[18]{0:T(128)S(1)} %dynamic-slice_bitcast_fusion.place_ref, bf16[2,64,256,256]{3,2,1,0:T(8,128)(2,1)} %warped.15, ...), custom_call_target="tpu_custom_call" | custom-call | flops 1073741824 | bytes 8388608 | tf_op jit(solution)/shard_map/force/pallas_call | solution.py:180
  103.4 5.3 %force.15 = (f32[96,1024]{1,0:T(8,128)S(1)}, f32[96,1024]{1,0:T(8,128)S(1)}, f32[64,1024]{1,0:T(8,128)S(1)}, f32[96,1024]{1,0:T(8,128)S(1)}, f32[96,1024]{1,0:T(8,128)S(1)}, /*index=5*/f32[64,1024]{1,0:T(8,128)S(1)}) custom-call(s32[18]{0:T(128)S(1)} %dynamic-slice_bitcast_fusion.place_ref, bf16[2,64,256,256]{3,2,1,0:T(8,128)(2,1)} %warped.15, ...), custom_call_target="tpu_custom_call" | custom-call | flops 1073741824 | bytes 8388608 | tf_op jit(solution)/shard_map/force/pallas_call | solution.py:180
  118.4 7.6 %collective-permute-done.13.rest_3_ = f32[96,1024]{1,0:T(8,128)S(1)} collective-permute-done((f32[96,1024]{1,0:T(8,128)S(1)}, f32[96,1024]{1,0:T(8,128)S(1)}, u32[]{:S(2)}, u32[]{:S(2)}) %collective-permute-start.13) | collective-permute-done | bytes 393248 | tf_op jit(solution)/shard_map/ppermute | solution.py:577
  135.7 6.5 %collective-permute-done.30 = f32[64,1024]{1,0:T(8,128)S(1)} collective-permute-done((f32[64,1024]{1,0:T(8,128)S(1)}, f32[64,1024]{1,0:T(8,128)S(1)}, u32[]{:S(2)}, u32[]{:S(2)}) %collective-permute-start.30) | collective-permute-done | bytes 262176 | tf_op jit(solution)/shard_map/ppermute | solution.py:577
  152.8 4.3 %collective-permute-done.34 = f32[64,1024]{1,0:T(8,128)S(1)} collective-permute-done((f32[64,1024]{1,0:T(8,128)S(1)}, f32[64,1024]{1,0:T(8,128)S(1)}, u32[]{:S(2)}, u32[]{:S(2)}) %collective-permute-start.34) | collective-permute-done | bytes 262176 | tf_op jit(solution)/shard_map/ppermute | solution.py:577
  161.1 4.4 %first_forward.1 = (f32[768,512]{1,0:T(8,128)}, f32[48,1024]{1,0:T(8,128)S(1)}) custom-call(s32[18]{0:T(128)S(1)} %dynamic-slice_bitcast_fusion.place_ref, f32[4,4,48,256]{3,2,1,0:T(8,128)S(1)} %copy-done.1, bf16[4,384,512]{2,1,0:T(8,128)(2,1)} %constant.36.clone.w_ref, f32[48,2048]{1,0:T(8,128)S(1)} %get-tuple-element.151.rest_0_, ...), custom_call_target="tpu_custom_call" | custom-call | tf_op jit(solution)/shard_map/first_forward/pallas_call | solution.py:111
  170.1 10.0 %collective-permute-done.39 = f32[112,1024]{1,0:T(8,128)S(1)} collective-permute-done((f32[112,1024]{1,0:T(8,128)S(1)}, f32[112,1024]{1,0:T(8,128)S(1)}, u32[]{:S(2)}, u32[]{:S(2)}) %collective-permute-start.39) | collective-permute-done | bytes 458784 | tf_op jit(solution)/shard_map/ppermute | solution.py:577
  182.3 8.9 %collective-permute-done.40 = f32[112,1024]{1,0:T(8,128)S(1)} collective-permute-done((f32[112,1024]{1,0:T(8,128)S(1)}, f32[112,1024]{1,0:T(8,128)S(1)}, u32[]{:S(2)}, u32[]{:S(2)}) %collective-permute-start.40) | collective-permute-done | bytes 458784 | tf_op jit(solution)/shard_map/ppermute | solution.py:577
  193.6 8.2 %collective-permute-done.41.rest_2_ = f32[112,1024]{1,0:T(8,128)S(1)} collective-permute-done((f32[112,1024]{1,0:T(8,128)S(1)}, f32[112,1024]{1,0:T(8,128)S(1)}, u32[]{:S(2)}, u32[]{:S(2)}) %collective-permute-start.41) | collective-permute-done | bytes 458784 | tf_op jit(solution)/shard_map/ppermute | solution.py:577
  209.0 4.1 %second_and_back.1 = (f32[48,2048]{1,0:T(8,128)S(1)}, f32[48,2048]{1,0:T(8,128)S(1)}, f32[96,2048]{1,0:T(8,128)S(1)}) custom-call(s32[18]{0:T(128)S(1)} %dynamic-slice_bitcast_fusion.place_ref, f32[4,4,48,256]{3,2,1,0:T(8,128)S(1)} %copy-done.1, bf16[4,1536,128]{2,1,0:T(8,128)(2,1)} %constant.39.clone.v_ref, f32[768,512]{1,0:T(8,128)} %get-tuple-element.162.f_ref, ...), custom_call_target="tpu_custom_call" | custom-call | tf_op jit(solution)/shard_map/second_and_back/pallas_call | solution.py:111
  216.4 4.6 %all-to-all-start = ((f32[8,8,2048]{2,1,0:T(8,128)}), f32[8,8,2048]{2,1,0:T(8,128)S(1)}, u32[]{:S(2)}, u32[]{:S(2)}) async-start(f32[8,8,2048]{2,1,0:T(8,128)} %first_and_back.1), calls=%async_computation | async-start | bytes 1048576 | tf_op jit(solution)/shard_map/all_to_all | solution.py:638
  221.0 11.9 %collective-permute-done.50 = f32[96,2048]{1,0:T(8,128)} collective-permute-done((f32[96,2048]{1,0:T(8,128)S(1)}, f32[96,2048]{1,0:T(8,128)}, u32[]{:S(2)}, u32[]{:S(2)}) %collective-permute-start.50) | collective-permute-done | bytes 786464 | tf_op jit(solution)/shard_map/ppermute | solution.py:634
  236.2 4.6 %last_back.1 = f32[64,32,256]{2,1,0:T(8,128)} custom-call(s32[18]{0:T(128)S(1)} %dynamic-slice_bitcast_fusion.place_ref, bf16[2,256,256]{2,1,0:T(8,128)(2,1)S(1)} %copy-done.7, f32[64,32,256]{2,1,0:T(8,128)} %velocity.1, f32[48,2048]{1,0:T(8,128)S(1)} %get-tuple-element.171.rest_0_, f32[48,2048]{1,0:T(8,128)S(1)} %collective-permute-done.49.rest_1_, ...), custom_call_target="tpu_custom_call" | custom-call | tf_op jit(solution)/shard_map/last_back/pallas_call | solution.py:536
  (171 shorter events, 92.3 us)
Async XLA Ops:
  10.2 18.3 %collective-permute-start.21 = (f32[96,1024]{1,0:T(8,128)S(1)}, f32[96,1024]{1,0:T(8,128)S(1)}, u32[]{:S(2)}, u32[]{:S(2)}) collective-permute-start(f32[96,1024]{1,0:T(8,128)S(1)} %get-tuple-element.133), channel_id=1, source_target_pairs={{8,0},{16,8},{24,16},{28,24},{20,28},{12,20},{4,12},{0,4},{9,1},{1... | collective-permute-start | bytes 1179656 | tf_op jit(solution)/shard_map/ppermute | solution.py:577
  12.0 18.5 %collective-permute-start = (f32[96,1024]{1,0:T(8,128)S(1)}, f32[96,1024]{1,0:T(8,128)S(1)}, u32[]{:S(2)}, u32[]{:S(2)}) collective-permute-start(f32[96,1024]{1,0:T(8,128)S(1)} %get-tuple-element.109), channel_id=1, source_target_pairs={{0,8},{8,16},{16,24},{24,28},{28,20},{20,12},{12,4},{4,0},{1,9},{9... | collective-permute-start | bytes 1179656 | tf_op jit(solution)/shard_map/ppermute | solution.py:577
  20.1 16.8 %collective-permute-start.8 = (f32[96,1024]{1,0:T(8,128)S(1)}, f32[96,1024]{1,0:T(8,128)S(1)}, u32[]{:S(2)}, u32[]{:S(2)}) collective-permute-start(f32[96,1024]{1,0:T(8,128)S(1)} %add.122), channel_id=1, source_target_pairs={{8,0},{16,8},{24,16},{28,24},{20,28},{12,20},{4,12},{0,4},{9,1},{1... | collective-permute-start | bytes 1179656 | tf_op jit(solution)/shard_map/ppermute | solution.py:577
  22.2 16.8 %collective-permute-start.15 = (f32[96,1024]{1,0:T(8,128)S(1)}, f32[96,1024]{1,0:T(8,128)S(1)}, u32[]{:S(2)}, u32[]{:S(2)}) collective-permute-start(f32[96,1024]{1,0:T(8,128)S(1)} %add.128), channel_id=1, source_target_pairs={{0,8},{8,16},{16,24},{24,28},{28,20},{20,12},{12,4},{4,0},{1,9},{9... | collective-permute-start | bytes 1179656 | tf_op jit(solution)/shard_map/ppermute | solution.py:577
  28.5 16.8 %collective-permute-start.22 = (f32[96,1024]{1,0:T(8,128)S(1)}, f32[96,1024]{1,0:T(8,128)S(1)}, u32[]{:S(2)}, u32[]{:S(2)}) collective-permute-start(f32[96,1024]{1,0:T(8,128)S(1)} %add.134), channel_id=1, source_target_pairs={{8,0},{16,8},{24,16},{28,24},{20,28},{12,20},{4,12},{0,4},{9,1},{1... | collective-permute-start | bytes 1179656 | tf_op jit(solution)/shard_map/ppermute | solution.py:577
  30.6 16.8 %collective-permute-start.1 = (f32[96,1024]{1,0:T(8,128)S(1)}, f32[96,1024]{1,0:T(8,128)S(1)}, u32[]{:S(2)}, u32[]{:S(2)}) collective-permute-start(f32[96,1024]{1,0:T(8,128)S(1)} %add.116), channel_id=1, source_target_pairs={{0,8},{8,16},{16,24},{24,28},{28,20},{20,12},{12,4},{4,0},{1,9},{9... | collective-permute-start | bytes 1179656 | tf_op jit(solution)/shard_map/ppermute | solution.py:577
  36.9 16.8 %collective-permute-start.9 = (f32[96,1024]{1,0:T(8,128)S(1)}, f32[96,1024]{1,0:T(8,128)S(1)}, u32[]{:S(2)}, u32[]{:S(2)}) collective-permute-start(f32[96,1024]{1,0:T(8,128)S(1)} %add.123), channel_id=1, source_target_pairs={{8,0},{16,8},{24,16},{28,24},{20,28},{12,20},{4,12},{0,4},{9,1},{1... | collective-permute-start | bytes 1179656 | tf_op jit(solution)/shard_map/ppermute | solution.py:577
  39.0 16.8 %collective-permute-start.16 = (f32[96,1024]{1,0:T(8,128)S(1)}, f32[96,1024]{1,0:T(8,128)S(1)}, u32[]{:S(2)}, u32[]{:S(2)}) collective-permute-start(f32[96,1024]{1,0:T(8,128)S(1)} %add.129), channel_id=1, source_target_pairs={{0,8},{8,16},{16,24},{24,28},{28,20},{20,12},{12,4},{4,0},{1,9},{9... | collective-permute-start | bytes 1179656 | tf_op jit(solution)/shard_map/ppermute | solution.py:577
  45.4 16.8 %collective-permute-start.23 = (f32[96,1024]{1,0:T(8,128)S(1)}, f32[96,1024]{1,0:T(8,128)S(1)}, u32[]{:S(2)}, u32[]{:S(2)}) collective-permute-start(f32[96,1024]{1,0:T(8,128)S(1)} %add.135), channel_id=1, source_target_pairs={{8,0},{16,8},{24,16},{28,24},{20,28},{12,20},{4,12},{0,4},{9,1},{1... | collective-permute-start | bytes 1179656 | tf_op jit(solution)/shard_map/ppermute | solution.py:577
  47.5 16.8 %collective-permute-start.2 = (f32[96,1024]{1,0:T(8,128)S(1)}, f32[96,1024]{1,0:T(8,128)S(1)}, u32[]{:S(2)}, u32[]{:S(2)}) collective-permute-start(f32[96,1024]{1,0:T(8,128)S(1)} %add.117), channel_id=1, source_target_pairs={{0,8},{8,16},{16,24},{24,28},{28,20},{20,12},{12,4},{4,0},{1,9},{9... | collective-permute-start | bytes 1179656 | tf_op jit(solution)/shard_map/ppermute | solution.py:577
  53.8 16.8 %collective-permute-start.10 = (f32[96,1024]{1,0:T(8,128)S(1)}, f32[96,1024]{1,0:T(8,128)S(1)}, u32[]{:S(2)}, u32[]{:S(2)}) collective-permute-start(f32[96,1024]{1,0:T(8,128)S(1)} %add.124), channel_id=1, source_target_pairs={{8,0},{16,8},{24,16},{28,24},{20,28},{12,20},{4,12},{0,4},{9,1},{1... | collective-permute-start | bytes 1179656 | tf_op jit(solution)/shard_map/ppermute | solution.py:577
  55.9 16.8 %collective-permute-start.17 = (f32[96,1024]{1,0:T(8,128)S(1)}, f32[96,1024]{1,0:T(8,128)S(1)}, u32[]{:S(2)}, u32[]{:S(2)}) collective-permute-start(f32[96,1024]{1,0:T(8,128)S(1)} %add.130), channel_id=1, source_target_pairs={{0,8},{8,16},{16,24},{24,28},{28,20},{20,12},{12,4},{4,0},{1,9},{9... | collective-permute-start | bytes 1179656 | tf_op jit(solution)/shard_map/ppermute | solution.py:577
  62.2 16.8 %collective-permute-start.24 = (f32[96,1024]{1,0:T(8,128)S(1)}, f32[96,1024]{1,0:T(8,128)S(1)}, u32[]{:S(2)}, u32[]{:S(2)}) collective-permute-start(f32[96,1024]{1,0:T(8,128)S(1)} %add.136), channel_id=1, source_target_pairs={{8,0},{16,8},{24,16},{28,24},{20,28},{12,20},{4,12},{0,4},{9,1},{1... | collective-permute-start | bytes 1179656 | tf_op jit(solution)/shard_map/ppermute | solution.py:577
  64.3 16.8 %collective-permute-start.3 = (f32[96,1024]{1,0:T(8,128)S(1)}, f32[96,1024]{1,0:T(8,128)S(1)}, u32[]{:S(2)}, u32[]{:S(2)}) collective-permute-start(f32[96,1024]{1,0:T(8,128)S(1)} %add.118), channel_id=1, source_target_pairs={{0,8},{8,16},{16,24},{24,28},{28,20},{20,12},{12,4},{4,0},{1,9},{9... | collective-permute-start | bytes 1179656 | tf_op jit(solution)/shard_map/ppermute | solution.py:577
  70.7 16.8 %collective-permute-start.11 = (f32[96,1024]{1,0:T(8,128)S(1)}, f32[96,1024]{1,0:T(8,128)S(1)}, u32[]{:S(2)}, u32[]{:S(2)}) collective-permute-start(f32[96,1024]{1,0:T(8,128)S(1)} %add.125), channel_id=1, source_target_pairs={{8,0},{16,8},{24,16},{28,24},{20,28},{12,20},{4,12},{0,4},{9,1},{1... | collective-permute-start | bytes 1179656 | tf_op jit(solution)/shard_map/ppermute | solution.py:577
  72.7 16.8 %collective-permute-start.18 = (f32[96,1024]{1,0:T(8,128)S(1)}, f32[96,1024]{1,0:T(8,128)S(1)}, u32[]{:S(2)}, u32[]{:S(2)}) collective-permute-start(f32[96,1024]{1,0:T(8,128)S(1)} %add.131), channel_id=1, source_target_pairs={{0,8},{8,16},{16,24},{24,28},{28,20},{20,12},{12,4},{4,0},{1,9},{9... | collective-permute-start | bytes 1179656 | tf_op jit(solution)/shard_map/ppermute | solution.py:577
  79.1 16.8 %collective-permute-start.25 = (f32[96,1024]{1,0:T(8,128)S(1)}, f32[96,1024]{1,0:T(8,128)S(1)}, u32[]{:S(2)}, u32[]{:S(2)}) collective-permute-start(f32[96,1024]{1,0:T(8,128)S(1)} %add.137), channel_id=1, source_target_pairs={{8,0},{16,8},{24,16},{28,24},{20,28},{12,20},{4,12},{0,4},{9,1},{1... | collective-permute-start | bytes 1179656 | tf_op jit(solution)/shard_map/ppermute | solution.py:577
  81.2 16.8 %collective-permute-start.4 = (f32[96,1024]{1,0:T(8,128)S(1)}, f32[96,1024]{1,0:T(8,128)S(1)}, u32[]{:S(2)}, u32[]{:S(2)}) collective-permute-start(f32[96,1024]{1,0:T(8,128)S(1)} %add.119), channel_id=1, source_target_pairs={{0,8},{8,16},{16,24},{24,28},{28,20},{20,12},{12,4},{4,0},{1,9},{9... | collective-permute-start | bytes 1179656 | tf_op jit(solution)/shard_map/ppermute | solution.py:577
  87.5 26.3 %collective-permute-start.12 = (f32[96,1024]{1,0:T(8,128)S(1)}, f32[96,1024]{1,0:T(8,128)S(1)}, u32[]{:S(2)}, u32[]{:S(2)}) collective-permute-start(f32[96,1024]{1,0:T(8,128)S(1)} %add.126), channel_id=1, source_target_pairs={{8,0},{16,8},{24,16},{28,24},{20,28},{12,20},{4,12},{0,4},{9,1},{1... | collective-permute-start | bytes 1179656 | tf_op jit(solution)/shard_map/ppermute | solution.py:577
  89.6 26.3 %collective-permute-start.19 = (f32[96,1024]{1,0:T(8,128)S(1)}, f32[96,1024]{1,0:T(8,128)S(1)}, u32[]{:S(2)}, u32[]{:S(2)}) collective-permute-start(f32[96,1024]{1,0:T(8,128)S(1)} %add.132), channel_id=1, source_target_pairs={{0,8},{8,16},{16,24},{24,28},{28,20},{20,12},{12,4},{4,0},{1,9},{9... | collective-permute-start | bytes 1179656 | tf_op jit(solution)/shard_map/ppermute | solution.py:577
  95.9 20.1 %collective-permute-start.26 = (f32[96,1024]{1,0:T(8,128)S(1)}, f32[96,1024]{1,0:T(8,128)S(1)}, u32[]{:S(2)}, u32[]{:S(2)}) collective-permute-start(f32[96,1024]{1,0:T(8,128)S(1)} %add.138), channel_id=1, source_target_pairs={{8,0},{16,8},{24,16},{28,24},{20,28},{12,20},{4,12},{0,4},{9,1},{1... | collective-permute-start | bytes 1179656 | tf_op jit(solution)/shard_map/ppermute | solution.py:577
  98.0 20.1 %collective-permute-start.5 = (f32[96,1024]{1,0:T(8,128)S(1)}, f32[96,1024]{1,0:T(8,128)S(1)}, u32[]{:S(2)}, u32[]{:S(2)}) collective-permute-start(f32[96,1024]{1,0:T(8,128)S(1)} %add.120), channel_id=1, source_target_pairs={{0,8},{8,16},{16,24},{24,28},{28,20},{20,12},{12,4},{4,0},{1,9},{9... | collective-permute-start | bytes 1179656 | tf_op jit(solution)/shard_map/ppermute | solution.py:577
  213.1 19.8 %collective-permute-start.50 = (f32[96,2048]{1,0:T(8,128)S(1)}, f32[96,2048]{1,0:T(8,128)}, u32[]{:S(2)}, u32[]{:S(2)}) collective-permute-start(f32[96,2048]{1,0:T(8,128)S(1)} %get-tuple-element.173), channel_id=1, source_target_pairs={{0,2},{1,3},{2,0},{3,1},{4,6},{5,7},{6,4},{7,5},{8,10},{9,11},{10,... | collective-permute-start | bytes 2359304 | tf_op jit(solution)/shard_map/ppermute | solution.py:634
  216.4 19.7 %all-to-all-start = ((f32[8,8,2048]{2,1,0:T(8,128)}), f32[8,8,2048]{2,1,0:T(8,128)S(1)}, u32[]{:S(2)}, u32[]{:S(2)}) async-start(f32[8,8,2048]{2,1,0:T(8,128)} %first_and_back.1), calls=%async_computation | async-start | bytes 1048576 | tf_op jit(solution)/shard_map/all_to_all | solution.py:638
  (40 other events, 323.5 us)

commit v5 on v4

--- a/solution.py
+++ b/solution.py
@@ -590,14 +590,13 @@
                 tuple(b + local[k][way][p] for way, b in enumerate(both))
                 for p, both in enumerate(streams)
             ]
+    late = regroup(plan, place, [local[k][way][-1] for k in range(subj) for way in range(2)])
+    both, streams = tie((late[0][0], late[1][0]), streams)
     pieces = join(
         plan, place, [a for p in parts for way in range(2) for a in (local[-1][way][p], streams[p][way])]
     )
-    late = regroup(plan, place, [local[k][way][-1] for k in range(subj) for way in range(2)])
 
     top = space // 2
-    both, own = tie((late[0][0], late[1][0]), pieces[0])
-    pieces = [own, *pieces[1:]]
     far = lax.ppermute(
         jnp.concatenate(pieces[top:]), "space", [(i, i ^ top) for i in range(space)]
     )
@@ -607,9 +606,9 @@
         if k == near_step:
             both, moved = tie(both, moved)
         if k == far_step:
+            far = over_space(plan, [far[d * plan.g : (d + 1) * plan.g] for d in range(top)])
             both, far = tie(both, far)
-            far = [far[d * plan.g : (d + 1) * plan.g] for d in range(top)]
-            f, ends = forward_lines(plan, place, [*moved, *over_space(plan, far)])
+            f, ends = forward_lines(plan, place, [*moved, *far])
         if k >= ends_step and len(arrived) < half:
             extra = arrived[-1] if arrived else (ends, ends)
             both = tuple(jnp.concatenate([b, e]) for b, e in zip(both, extra))

time: 241 us -> 241 us (level)
    ppermute x22, waiting for transfers between devices: 36.2 us -> 88 us  [go_round(): lax.ppermute(both[0], 'subj', to_right)]
    ppermute x21, waiting for transfers between devices: 60.3 us -> 9.42 us  [go_round(): lax.ppermute(both[1], 'subj', to_left)]
    ppermute x22, starting transfers between devices: 5.94 us -> 41 us  [go_round(): lax.ppermute(both[0], 'subj', to_right)]
    ppermute x21, starting transfers between devices: 41.1 us -> 7 us  [go_round(): lax.ppermute(both[1], 'subj', to_left)]
  transfers between devices with their start and end apart: 53 -> 53, of which waited for: 29 -> 28; matrix products, arithmetic and copies ran while one was open for 1% -> 1% of each run, Pallas kernels for 20% -> 21%
where the time goes in v5:
time: 241 us
  waiting for transfers between devices  114 us (47%)
  Pallas kernels  64.1 us (27%)
  starting transfers between devices  56.7 us (24%)
  local copies, waits for them, and re-layouts  3.86 us (2%)
    ppermute x22, waiting for transfers between devices, go_round(): lax.ppermute(both[0], 'subj', to_right)  88 us
    pallas_call x8, Pallas kernels, force_blocks(): pl.pallas_call(functools.partial(force_kernel, plan), out_shape=shapes, g...  42.3 us
    ppermute x22, starting transfers between devices, go_round(): lax.ppermute(both[0], 'subj', to_right)  41 us
    pallas_call x6, Pallas kernels, call_once(): pl.pallas_call(kernel, out_shape=out_shape, in_specs=[pl.BlockSpec(memory...  17.2 us
    ppermute x1, waiting for transfers between devices, ring_body(): far = lax.ppermute(far, 'space', [(i, i ^ top) for i in range(space)])  12.5 us
    ppermute x21, waiting for transfers between devices, go_round(): lax.ppermute(both[1], 'subj', to_left)  9.42 us
    ppermute x21, starting transfers between devices, go_round(): lax.ppermute(both[1], 'subj', to_left)  7 us
  transfers between devices with their start and end apart: 53, of which 28 were waited for; matrix products, arithmetic and copies ran while one was open for 1% of the time, Pallas kernels for 21%

profile of v5, /device:TPU:0, one launch (start us, length us, event | category | flops | bytes accessed | tf_op | source)
XLA Modules:
  0.0 240.7 jit_solution(723439574499146160)
XLA Ops:
  1.7 5.3 %force.8 = (f32[96,1024]{1,0:T(8,128)S(1)}, f32[96,1024]{1,0:T(8,128)S(1)}, f32[64,1024]{1,0:T(8,128)S(1)}, f32[96,1024]{1,0:T(8,128)S(1)}, f32[96,1024]{1,0:T(8,128)S(1)}, /*index=5*/f32[64,1024]{1,0:T(8,128)S(1)}) custom-call(s32[18]{0:T(128)S(1)} %dynamic-slice_bitcast_fusion.place_ref, bf16[2,64,256,256]{3,2,1,0:T(8,128)(2,1)} %warped.15, ...), custom_call_target="tpu_custom_call" | custom-call | flops 1073741824 | bytes 8388608 | tf_op jit(solution)/shard_map/force/pallas_call | solution.py:180
  12.1 5.3 %force.9 = (f32[96,1024]{1,0:T(8,128)S(1)}, f32[96,1024]{1,0:T(8,128)S(1)}, f32[64,1024]{1,0:T(8,128)S(1)}, f32[96,1024]{1,0:T(8,128)S(1)}, f32[96,1024]{1,0:T(8,128)S(1)}, /*index=5*/f32[64,1024]{1,0:T(8,128)S(1)}) custom-call(s32[18]{0:T(128)S(1)} %dynamic-slice_bitcast_fusion.place_ref, bf16[2,64,256,256]{3,2,1,0:T(8,128)(2,1)} %warped.15, ...), custom_call_target="tpu_custom_call" | custom-call | flops 1073741824 | bytes 8388608 | tf_op jit(solution)/shard_map/force/pallas_call | solution.py:180
  22.3 6.1 %collective-permute-done.14 = f32[96,1024]{1,0:T(8,128)S(1)} collective-permute-done((f32[96,1024]{1,0:T(8,128)S(1)}, f32[96,1024]{1,0:T(8,128)S(1)}, u32[]{:S(2)}, u32[]{:S(2)}) %collective-permute-start.14) | collective-permute-done | bytes 393248 | tf_op jit(solution)/shard_map/ppermute | solution.py:577
  30.7 5.3 %force.10 = (f32[96,1024]{1,0:T(8,128)S(1)}, f32[96,1024]{1,0:T(8,128)S(1)}, f32[64,1024]{1,0:T(8,128)S(1)}, f32[96,1024]{1,0:T(8,128)S(1)}, f32[96,1024]{1,0:T(8,128)S(1)}, /*index=5*/f32[64,1024]{1,0:T(8,128)S(1)}) custom-call(s32[18]{0:T(128)S(1)} %dynamic-slice_bitcast_fusion.place_ref, bf16[2,64,256,256]{3,2,1,0:T(8,128)(2,1)} %warped.15, ...), custom_call_target="tpu_custom_call" | custom-call | flops 1073741824 | bytes 8388608 | tf_op jit(solution)/shard_map/force/pallas_call | solution.py:180
  39.2 6.1 %collective-permute-done.15 = f32[96,1024]{1,0:T(8,128)S(1)} collective-permute-done((f32[96,1024]{1,0:T(8,128)S(1)}, f32[96,1024]{1,0:T(8,128)S(1)}, u32[]{:S(2)}, u32[]{:S(2)}) %collective-permute-start.15) | collective-permute-done | bytes 393248 | tf_op jit(solution)/shard_map/ppermute | solution.py:577
  47.6 5.3 %force.11 = (f32[96,1024]{1,0:T(8,128)S(1)}, f32[96,1024]{1,0:T(8,128)S(1)}, f32[64,1024]{1,0:T(8,128)S(1)}, f32[96,1024]{1,0:T(8,128)S(1)}, f32[96,1024]{1,0:T(8,128)S(1)}, /*index=5*/f32[64,1024]{1,0:T(8,128)S(1)}) custom-call(s32[18]{0:T(128)S(1)} %dynamic-slice_bitcast_fusion.place_ref, bf16[2,64,256,256]{3,2,1,0:T(8,128)(2,1)} %warped.15, ...), custom_call_target="tpu_custom_call" | custom-call | flops 1073741824 | bytes 8388608 | tf_op jit(solution)/shard_map/force/pallas_call | solution.py:180
  56.0 6.1 %collective-permute-done.16 = f32[96,1024]{1,0:T(8,128)S(1)} collective-permute-done((f32[96,1024]{1,0:T(8,128)S(1)}, f32[96,1024]{1,0:T(8,128)S(1)}, u32[]{:S(2)}, u32[]{:S(2)}) %collective-permute-start.16) | collective-permute-done | bytes 393248 | tf_op jit(solution)/shard_map/ppermute | solution.py:577
  64.5 5.3 %force.12 = (f32[96,1024]{1,0:T(8,128)S(1)}, f32[96,1024]{1,0:T(8,128)S(1)}, f32[64,1024]{1,0:T(8,128)S(1)}, f32[96,1024]{1,0:T(8,128)S(1)}, f32[96,1024]{1,0:T(8,128)S(1)}, /*index=5*/f32[64,1024]{1,0:T(8,128)S(1)}) custom-call(s32[18]{0:T(128)S(1)} %dynamic-slice_bitcast_fusion.place_ref, bf16[2,64,256,256]{3,2,1,0:T(8,128)(2,1)} %warped.15, ...), custom_call_target="tpu_custom_call" | custom-call | flops 1073741824 | bytes 8388608 | tf_op jit(solution)/shard_map/force/pallas_call | solution.py:180
  72.9 6.1 %collective-permute-done.17 = f32[96,1024]{1,0:T(8,128)S(1)} collective-permute-done((f32[96,1024]{1,0:T(8,128)S(1)}, f32[96,1024]{1,0:T(8,128)S(1)}, u32[]{:S(2)}, u32[]{:S(2)}) %collective-permute-start.17) | collective-permute-done | bytes 393248 | tf_op jit(solution)/shard_map/ppermute | solution.py:577
  81.5 5.3 %force.13 = (f32[96,1024]{1,0:T(8,128)S(1)}, f32[96,1024]{1,0:T(8,128)S(1)}, f32[64,1024]{1,0:T(8,128)S(1)}, f32[96,1024]{1,0:T(8,128)S(1)}, f32[96,1024]{1,0:T(8,128)S(1)}, /*index=5*/f32[64,1024]{1,0:T(8,128)S(1)}) custom-call(s32[18]{0:T(128)S(1)} %dynamic-slice_bitcast_fusion.place_ref, bf16[2,64,256,256]{3,2,1,0:T(8,128)(2,1)} %warped.15, ...), custom_call_target="tpu_custom_call" | custom-call | flops 1073741824 | bytes 8388608 | tf_op jit(solution)/shard_map/force/pallas_call | solution.py:180
  89.7 6.1 %collective-permute-done.18 = f32[96,1024]{1,0:T(8,128)S(1)} collective-permute-done((f32[96,1024]{1,0:T(8,128)S(1)}, f32[96,1024]{1,0:T(8,128)S(1)}, u32[]{:S(2)}, u32[]{:S(2)}) %collective-permute-start.18) | collective-permute-done | bytes 393248 | tf_op jit(solution)/shard_map/ppermute | solution.py:577
  98.2 5.3 %force.15 = (f32[96,1024]{1,0:T(8,128)S(1)}, f32[96,1024]{1,0:T(8,128)S(1)}, f32[64,1024]{1,0:T(8,128)S(1)}, f32[96,1024]{1,0:T(8,128)S(1)}, f32[96,1024]{1,0:T(8,128)S(1)}, /*index=5*/f32[64,1024]{1,0:T(8,128)S(1)}) custom-call(s32[18]{0:T(128)S(1)} %dynamic-slice_bitcast_fusion.place_ref, bf16[2,64,256,256]{3,2,1,0:T(8,128)(2,1)} %warped.15, ...), custom_call_target="tpu_custom_call" | custom-call | flops 1073741824 | bytes 8388608 | tf_op jit(solution)/shard_map/force/pallas_call | solution.py:180
  104.2 5.3 %force.14 = (f32[96,1024]{1,0:T(8,128)S(1)}, f32[96,1024]{1,0:T(8,128)S(1)}, f32[64,1024]{1,0:T(8,128)S(1)}, f32[96,1024]{1,0:T(8,128)S(1)}, f32[96,1024]{1,0:T(8,128)S(1)}, /*index=5*/f32[64,1024]{1,0:T(8,128)S(1)}) custom-call(s32[18]{0:T(128)S(1)} %dynamic-slice_bitcast_fusion.place_ref, bf16[2,64,256,256]{3,2,1,0:T(8,128)(2,1)} %warped.15, ...), custom_call_target="tpu_custom_call" | custom-call | flops 1073741824 | bytes 8388608 | tf_op jit(solution)/shard_map/force/pallas_call | solution.py:180
  117.7 7.6 %collective-permute-done.6.rest_1_ = f32[96,1024]{1,0:T(8,128)S(1)} collective-permute-done((f32[96,1024]{1,0:T(8,128)S(1)}, f32[96,1024]{1,0:T(8,128)S(1)}, u32[]{:S(2)}, u32[]{:S(2)}) %collective-permute-start.6) | collective-permute-done | bytes 393248 | tf_op jit(solution)/shard_map/ppermute | solution.py:577
  136.6 3.9 %collective-permute-done.28 = f32[64,1024]{1,0:T(8,128)S(1)} collective-permute-done((f32[64,1024]{1,0:T(8,128)S(1)}, f32[64,1024]{1,0:T(8,128)S(1)}, u32[]{:S(2)}, u32[]{:S(2)}) %collective-permute-start.28) | collective-permute-done | bytes 262176 | tf_op jit(solution)/shard_map/ppermute | solution.py:577
  142.7 4.2 %collective-permute-done.29 = f32[64,1024]{1,0:T(8,128)S(1)} collective-permute-done((f32[64,1024]{1,0:T(8,128)S(1)}, f32[64,1024]{1,0:T(8,128)S(1)}, u32[]{:S(2)}, u32[]{:S(2)}) %collective-permute-start.29) | collective-permute-done | bytes 262176 | tf_op jit(solution)/shard_map/ppermute | solution.py:577
  151.0 4.2 %collective-permute-done.33 = f32[64,1024]{1,0:T(8,128)S(1)} collective-permute-done((f32[64,1024]{1,0:T(8,128)S(1)}, f32[64,1024]{1,0:T(8,128)S(1)}, u32[]{:S(2)}, u32[]{:S(2)}) %collective-permute-start.33) | collective-permute-done | bytes 262176 | tf_op jit(solution)/shard_map/ppermute | solution.py:577
  159.3 4.4 %first_forward.1 = (f32[768,512]{1,0:T(8,128)}, f32[48,1024]{1,0:T(8,128)S(1)}) custom-call(s32[18]{0:T(128)S(1)} %dynamic-slice_bitcast_fusion.place_ref, f32[4,4,48,256]{3,2,1,0:T(8,128)S(1)} %copy-done.1, bf16[4,384,512]{2,1,0:T(8,128)(2,1)} %constant.36.clone.w_ref, f32[48,2048]{1,0:T(8,128)S(1)} %get-tuple-element.158.rest_0_, ...), custom_call_target="tpu_custom_call" | custom-call | tf_op jit(solution)/shard_map/first_forward/pallas_call | solution.py:111
  169.0 10.9 %collective-permute-done.39 = f32[112,1024]{1,0:T(8,128)S(1)} collective-permute-done((f32[112,1024]{1,0:T(8,128)S(1)}, f32[112,1024]{1,0:T(8,128)S(1)}, u32[]{:S(2)}, u32[]{:S(2)}) %collective-permute-start.39) | collective-permute-done | bytes 458784 | tf_op jit(solution)/shard_map/ppermute | solution.py:577
  182.2 10.6 %collective-permute-done.40 = f32[112,1024]{1,0:T(8,128)S(1)} collective-permute-done((f32[112,1024]{1,0:T(8,128)S(1)}, f32[112,1024]{1,0:T(8,128)S(1)}, u32[]{:S(2)}, u32[]{:S(2)}) %collective-permute-start.40) | collective-permute-done | bytes 458784 | tf_op jit(solution)/shard_map/ppermute | solution.py:577
  195.2 7.1 %collective-permute-done.41.rest_2_ = f32[112,1024]{1,0:T(8,128)S(1)} collective-permute-done((f32[112,1024]{1,0:T(8,128)S(1)}, f32[112,1024]{1,0:T(8,128)S(1)}, u32[]{:S(2)}, u32[]{:S(2)}) %collective-permute-start.41) | collective-permute-done | bytes 458784 | tf_op jit(solution)/shard_map/ppermute | solution.py:577
  209.2 4.1 %second_and_back.1 = (f32[48,2048]{1,0:T(8,128)S(1)}, f32[48,2048]{1,0:T(8,128)S(1)}, f32[96,2048]{1,0:T(8,128)S(1)}) custom-call(s32[18]{0:T(128)S(1)} %dynamic-slice_bitcast_fusion.place_ref, f32[4,4,48,256]{3,2,1,0:T(8,128)S(1)} %copy-done.1, bf16[4,1536,128]{2,1,0:T(8,128)(2,1)} %constant.39.clone.v_ref, f32[768,512]{1,0:T(8,128)} %get-tuple-element.170.f_ref, ...), custom_call_target="tpu_custom_call" | custom-call | tf_op jit(solution)/shard_map/second_and_back/pallas_call | solution.py:111
  220.6 12.5 %collective-permute-done.50 = f32[96,2048]{1,0:T(8,128)} collective-permute-done((f32[96,2048]{1,0:T(8,128)S(1)}, f32[96,2048]{1,0:T(8,128)}, u32[]{:S(2)}, u32[]{:S(2)}) %collective-permute-start.50) | collective-permute-done | bytes 786464 | tf_op jit(solution)/shard_map/ppermute | solution.py:633
  236.1 4.6 %last_back.1 = f32[64,32,256]{2,1,0:T(8,128)} custom-call(s32[18]{0:T(128)S(1)} %dynamic-slice_bitcast_fusion.place_ref, bf16[2,256,256]{2,1,0:T(8,128)(2,1)S(1)} %copy-done.7, f32[64,32,256]{2,1,0:T(8,128)} %velocity.1, f32[48,2048]{1,0:T(8,128)S(1)} %get-tuple-element.179.rest_0_, f32[48,2048]{1,0:T(8,128)S(1)} %collective-permute-done.49.rest_1_, ...), custom_call_target="tpu_custom_call" | custom-call | tf_op jit(solution)/shard_map/last_back/pallas_call | solution.py:536
  (171 shorter events, 93.4 us)
Async XLA Ops:
  10.1 18.3 %collective-permute-start.14 = (f32[96,1024]{1,0:T(8,128)S(1)}, f32[96,1024]{1,0:T(8,128)S(1)}, u32[]{:S(2)}, u32[]{:S(2)}) collective-permute-start(f32[96,1024]{1,0:T(8,128)S(1)} %get-tuple-element.126), channel_id=1, source_target_pairs={{0,8},{8,16},{16,24},{24,28},{28,20},{20,12},{12,4},{4,0},{1,9},{9... | collective-permute-start | bytes 1179656 | tf_op jit(solution)/shard_map/ppermute | solution.py:577
  12.1 18.5 %collective-permute-start.21 = (f32[96,1024]{1,0:T(8,128)S(1)}, f32[96,1024]{1,0:T(8,128)S(1)}, u32[]{:S(2)}, u32[]{:S(2)}) collective-permute-start(f32[96,1024]{1,0:T(8,128)S(1)} %get-tuple-element.133), channel_id=1, source_target_pairs={{8,0},{16,8},{24,16},{28,24},{20,28},{12,20},{4,12},{0,4},{9,1},{1... | collective-permute-start | bytes 1179656 | tf_op jit(solution)/shard_map/ppermute | solution.py:577
  20.0 16.8 %collective-permute-start.1 = (f32[96,1024]{1,0:T(8,128)S(1)}, f32[96,1024]{1,0:T(8,128)S(1)}, u32[]{:S(2)}, u32[]{:S(2)}) collective-permute-start(f32[96,1024]{1,0:T(8,128)S(1)} %add.116), channel_id=1, source_target_pairs={{0,8},{8,16},{16,24},{24,28},{28,20},{20,12},{12,4},{4,0},{1,9},{9... | collective-permute-start | bytes 1179656 | tf_op jit(solution)/shard_map/ppermute | solution.py:577
  22.3 16.8 %collective-permute-start.8 = (f32[96,1024]{1,0:T(8,128)S(1)}, f32[96,1024]{1,0:T(8,128)S(1)}, u32[]{:S(2)}, u32[]{:S(2)}) collective-permute-start(f32[96,1024]{1,0:T(8,128)S(1)} %add.122), channel_id=1, source_target_pairs={{8,0},{16,8},{24,16},{28,24},{20,28},{12,20},{4,12},{0,4},{9,1},{1... | collective-permute-start | bytes 1179656 | tf_op jit(solution)/shard_map/ppermute | solution.py:577
  28.4 16.8 %collective-permute-start.15 = (f32[96,1024]{1,0:T(8,128)S(1)}, f32[96,1024]{1,0:T(8,128)S(1)}, u32[]{:S(2)}, u32[]{:S(2)}) collective-permute-start(f32[96,1024]{1,0:T(8,128)S(1)} %add.128), channel_id=1, source_target_pairs={{0,8},{8,16},{16,24},{24,28},{28,20},{20,12},{12,4},{4,0},{1,9},{9... | collective-permute-start | bytes 1179656 | tf_op jit(solution)/shard_map/ppermute | solution.py:577
  30.7 16.8 %collective-permute-start.22 = (f32[96,1024]{1,0:T(8,128)S(1)}, f32[96,1024]{1,0:T(8,128)S(1)}, u32[]{:S(2)}, u32[]{:S(2)}) collective-permute-start(f32[96,1024]{1,0:T(8,128)S(1)} %add.134), channel_id=1, source_target_pairs={{8,0},{16,8},{24,16},{28,24},{20,28},{12,20},{4,12},{0,4},{9,1},{1... | collective-permute-start | bytes 1179656 | tf_op jit(solution)/shard_map/ppermute | solution.py:577
  36.9 16.8 %collective-permute-start.2 = (f32[96,1024]{1,0:T(8,128)S(1)}, f32[96,1024]{1,0:T(8,128)S(1)}, u32[]{:S(2)}, u32[]{:S(2)}) collective-permute-start(f32[96,1024]{1,0:T(8,128)S(1)} %add.117), channel_id=1, source_target_pairs={{0,8},{8,16},{16,24},{24,28},{28,20},{20,12},{12,4},{4,0},{1,9},{9... | collective-permute-start | bytes 1179656 | tf_op jit(solution)/shard_map/ppermute | solution.py:577
  39.1 16.8 %collective-permute-start.9 = (f32[96,1024]{1,0:T(8,128)S(1)}, f32[96,1024]{1,0:T(8,128)S(1)}, u32[]{:S(2)}, u32[]{:S(2)}) collective-permute-start(f32[96,1024]{1,0:T(8,128)S(1)} %add.123), channel_id=1, source_target_pairs={{8,0},{16,8},{24,16},{28,24},{20,28},{12,20},{4,12},{0,4},{9,1},{1... | collective-permute-start | bytes 1179656 | tf_op jit(solution)/shard_map/ppermute | solution.py:577
  45.3 16.8 %collective-permute-start.16 = (f32[96,1024]{1,0:T(8,128)S(1)}, f32[96,1024]{1,0:T(8,128)S(1)}, u32[]{:S(2)}, u32[]{:S(2)}) collective-permute-start(f32[96,1024]{1,0:T(8,128)S(1)} %add.129), channel_id=1, source_target_pairs={{0,8},{8,16},{16,24},{24,28},{28,20},{20,12},{12,4},{4,0},{1,9},{9... | collective-permute-start | bytes 1179656 | tf_op jit(solution)/shard_map/ppermute | solution.py:577
  47.5 16.8 %collective-permute-start.23 = (f32[96,1024]{1,0:T(8,128)S(1)}, f32[96,1024]{1,0:T(8,128)S(1)}, u32[]{:S(2)}, u32[]{:S(2)}) collective-permute-start(f32[96,1024]{1,0:T(8,128)S(1)} %add.135), channel_id=1, source_target_pairs={{8,0},{16,8},{24,16},{28,24},{20,28},{12,20},{4,12},{0,4},{9,1},{1... | collective-permute-start | bytes 1179656 | tf_op jit(solution)/shard_map/ppermute | solution.py:577
  53.7 16.8 %collective-permute-start.3 = (f32[96,1024]{1,0:T(8,128)S(1)}, f32[96,1024]{1,0:T(8,128)S(1)}, u32[]{:S(2)}, u32[]{:S(2)}) collective-permute-start(f32[96,1024]{1,0:T(8,128)S(1)} %add.118), channel_id=1, source_target_pairs={{0,8},{8,16},{16,24},{24,28},{28,20},{20,12},{12,4},{4,0},{1,9},{9... | collective-permute-start | bytes 1179656 | tf_op jit(solution)/shard_map/ppermute | solution.py:577
  56.0 16.8 %collective-permute-start.10 = (f32[96,1024]{1,0:T(8,128)S(1)}, f32[96,1024]{1,0:T(8,128)S(1)}, u32[]{:S(2)}, u32[]{:S(2)}) collective-permute-start(f32[96,1024]{1,0:T(8,128)S(1)} %add.124), channel_id=1, source_target_pairs={{8,0},{16,8},{24,16},{28,24},{20,28},{12,20},{4,12},{0,4},{9,1},{1... | collective-permute-start | bytes 1179656 | tf_op jit(solution)/shard_map/ppermute | solution.py:577
  62.1 16.8 %collective-permute-start.17 = (f32[96,1024]{1,0:T(8,128)S(1)}, f32[96,1024]{1,0:T(8,128)S(1)}, u32[]{:S(2)}, u32[]{:S(2)}) collective-permute-start(f32[96,1024]{1,0:T(8,128)S(1)} %add.130), channel_id=1, source_target_pairs={{0,8},{8,16},{16,24},{24,28},{28,20},{20,12},{12,4},{4,0},{1,9},{9... | collective-permute-start | bytes 1179656 | tf_op jit(solution)/shard_map/ppermute | solution.py:577
  64.4 16.8 %collective-permute-start.24 = (f32[96,1024]{1,0:T(8,128)S(1)}, f32[96,1024]{1,0:T(8,128)S(1)}, u32[]{:S(2)}, u32[]{:S(2)}) collective-permute-start(f32[96,1024]{1,0:T(8,128)S(1)} %add.136), channel_id=1, source_target_pairs={{8,0},{16,8},{24,16},{28,24},{20,28},{12,20},{4,12},{0,4},{9,1},{1... | collective-permute-start | bytes 1179656 | tf_op jit(solution)/shard_map/ppermute | solution.py:577
  70.6 16.8 %collective-permute-start.4 = (f32[96,1024]{1,0:T(8,128)S(1)}, f32[96,1024]{1,0:T(8,128)S(1)}, u32[]{:S(2)}, u32[]{:S(2)}) collective-permute-start(f32[96,1024]{1,0:T(8,128)S(1)} %add.119), channel_id=1, source_target_pairs={{0,8},{8,16},{16,24},{24,28},{28,20},{20,12},{12,4},{4,0},{1,9},{9... | collective-permute-start | bytes 1179656 | tf_op jit(solution)/shard_map/ppermute | solution.py:577
  72.8 16.8 %collective-permute-start.11 = (f32[96,1024]{1,0:T(8,128)S(1)}, f32[96,1024]{1,0:T(8,128)S(1)}, u32[]{:S(2)}, u32[]{:S(2)}) collective-permute-start(f32[96,1024]{1,0:T(8,128)S(1)} %add.125), channel_id=1, source_target_pairs={{8,0},{16,8},{24,16},{28,24},{20,28},{12,20},{4,12},{0,4},{9,1},{1... | collective-permute-start | bytes 1179656 | tf_op jit(solution)/shard_map/ppermute | solution.py:577
  79.0 16.8 %collective-permute-start.18 = (f32[96,1024]{1,0:T(8,128)S(1)}, f32[96,1024]{1,0:T(8,128)S(1)}, u32[]{:S(2)}, u32[]{:S(2)}) collective-permute-start(f32[96,1024]{1,0:T(8,128)S(1)} %add.131), channel_id=1, source_target_pairs={{0,8},{8,16},{16,24},{24,28},{28,20},{20,12},{12,4},{4,0},{1,9},{9... | collective-permute-start | bytes 1179656 | tf_op jit(solution)/shard_map/ppermute | solution.py:577
  81.2 16.8 %collective-permute-start.25 = (f32[96,1024]{1,0:T(8,128)S(1)}, f32[96,1024]{1,0:T(8,128)S(1)}, u32[]{:S(2)}, u32[]{:S(2)}) collective-permute-start(f32[96,1024]{1,0:T(8,128)S(1)} %add.137), channel_id=1, source_target_pairs={{8,0},{16,8},{24,16},{28,24},{20,28},{12,20},{4,12},{0,4},{9,1},{1... | collective-permute-start | bytes 1179656 | tf_op jit(solution)/shard_map/ppermute | solution.py:577
  87.4 25.7 %collective-permute-start.5 = (f32[96,1024]{1,0:T(8,128)S(1)}, f32[96,1024]{1,0:T(8,128)S(1)}, u32[]{:S(2)}, u32[]{:S(2)}) collective-permute-start(f32[96,1024]{1,0:T(8,128)S(1)} %add.120), channel_id=1, source_target_pairs={{0,8},{8,16},{16,24},{24,28},{28,20},{20,12},{12,4},{4,0},{1,9},{9... | collective-permute-start | bytes 1179656 | tf_op jit(solution)/shard_map/ppermute | solution.py:577
  89.7 25.5 %collective-permute-start.12 = (f32[96,1024]{1,0:T(8,128)S(1)}, f32[96,1024]{1,0:T(8,128)S(1)}, u32[]{:S(2)}, u32[]{:S(2)}) collective-permute-start(f32[96,1024]{1,0:T(8,128)S(1)} %add.126), channel_id=1, source_target_pairs={{8,0},{16,8},{24,16},{28,24},{20,28},{12,20},{4,12},{0,4},{9,1},{1... | collective-permute-start | bytes 1179656 | tf_op jit(solution)/shard_map/ppermute | solution.py:577
  95.8 19.5 %collective-permute-start.19 = (f32[96,1024]{1,0:T(8,128)S(1)}, f32[96,1024]{1,0:T(8,128)S(1)}, u32[]{:S(2)}, u32[]{:S(2)}) collective-permute-start(f32[96,1024]{1,0:T(8,128)S(1)} %add.132), channel_id=1, source_target_pairs={{0,8},{8,16},{16,24},{24,28},{28,20},{20,12},{12,4},{4,0},{1,9},{9... | collective-permute-start | bytes 1179656 | tf_op jit(solution)/shard_map/ppermute | solution.py:577
  98.1 19.3 %collective-permute-start.26 = (f32[96,1024]{1,0:T(8,128)S(1)}, f32[96,1024]{1,0:T(8,128)S(1)}, u32[]{:S(2)}, u32[]{:S(2)}) collective-permute-start(f32[96,1024]{1,0:T(8,128)S(1)} %add.138), channel_id=1, source_target_pairs={{8,0},{16,8},{24,16},{28,24},{20,28},{12,20},{4,12},{0,4},{9,1},{1... | collective-permute-start | bytes 1179656 | tf_op jit(solution)/shard_map/ppermute | solution.py:577
  213.3 19.8 %collective-permute-start.50 = (f32[96,2048]{1,0:T(8,128)S(1)}, f32[96,2048]{1,0:T(8,128)}, u32[]{:S(2)}, u32[]{:S(2)}) collective-permute-start(f32[96,2048]{1,0:T(8,128)S(1)} %get-tuple-element.181), channel_id=1, source_target_pairs={{0,2},{1,3},{2,0},{3,1},{4,6},{5,7},{6,4},{7,5},{8,10},{9,11},{10,... | collective-permute-start | bytes 2359304 | tf_op jit(solution)/shard_map/ppermute | solution.py:633
  217.1 19.0 %all-to-all-start = ((f32[8,8,2048]{2,1,0:T(8,128)}), f32[8,8,2048]{2,1,0:T(8,128)S(1)}, u32[]{:S(2)}, u32[]{:S(2)}) async-start(f32[8,8,2048]{2,1,0:T(8,128)} %first_and_back.1), calls=%async_computation | async-start | bytes 1048576 | tf_op jit(solution)/shard_map/all_to_all | solution.py:637
  (40 other events, 336.0 us)

commit v6 on v5

--- a/solution.py
+++ b/solution.py
@@ -106,7 +106,7 @@
     return high, low
 
 
-def call_once(kernel, name, out_shape, place, args, scratch=()):
+def call_once(kernel, name, out_shape, place, args, scratch=(), cost=None):
     vmem = pl.BlockSpec(memory_space=pltpu.VMEM)
     return pl.pallas_call(
         kernel,
@@ -115,6 +115,7 @@
         out_specs=jax.tree.map(lambda _: vmem, out_shape),
         scratch_shapes=scratch,
         compiler_params=params(),
+        cost_estimate=cost,
         name=name,
     )(place, *[jnp.asarray(a) for a in args])
 
@@ -297,6 +298,11 @@
         ],
         place,
         [plan.r_early, plan.w_table, *pieces],
+        cost=pl.CostEstimate(
+            flops=6 * plan.tiles * plan.g * plan.ty * plan.length * plan.space * lane,
+            bytes_accessed=8 * sum(p.size for p in pieces),
+            transcendentals=0,
+        ),
     )
 
 
@@ -365,6 +371,11 @@
         place,
         [plan.r_early, plan.v_table, f, *ends],
         scratch=[pltpu.VMEM(f.shape, jnp.float32)],
+        cost=pl.CostEstimate(
+            flops=6 * f.shape[0] * f.shape[1] * plan.space * lane,
+            bytes_accessed=4 * (2 * f.size + sum(e.size for e in ends)),
+            transcendentals=0,
+        ),
     )
 
 

time: 241 us -> 241 us (level)
  no operation moved by 1% of the time
where the time goes in v6:
time: 241 us
  waiting for transfers between devices  114 us (47%)
  Pallas kernels  64.1 us (27%)
  starting transfers between devices  56.7 us (24%)
  local copies, waits for them, and re-layouts  3.85 us (2%)
    ppermute x22, waiting for transfers between devices, go_round(): lax.ppermute(both[0], 'subj', to_right)  88 us
    pallas_call x8, Pallas kernels, force_blocks(): pl.pallas_call(functools.partial(force_kernel, plan), out_shape=shapes, g...  42.3 us
    ppermute x22, starting transfers between devices, go_round(): lax.ppermute(both[0], 'subj', to_right)  41.1 us
    pallas_call x6, Pallas kernels, call_once(): pl.pallas_call(kernel, out_shape=out_shape, in_specs=[pl.BlockSpec(memory...  17.2 us
    ppermute x1, waiting for transfers between devices, ring_body(): far = lax.ppermute(far, 'space', [(i, i ^ top) for i in range(space)])  12.5 us
    ppermute x21, waiting for transfers between devices, go_round(): lax.ppermute(both[1], 'subj', to_left)  9.41 us
    ppermute x21, starting transfers between devices, go_round(): lax.ppermute(both[1], 'subj', to_left)  6.99 us
  transfers between devices with their start and end apart: 53, of which 28 were waited for; matrix products, arithmetic and copies ran while one was open for 1% of the time, Pallas kernels for 21%

profile of v6, /device:TPU:0, one launch (start us, length us, event | category | flops | bytes accessed | tf_op | source)
XLA Modules:
  0.0 240.7 jit_solution(5225585650716790002)
XLA Ops:
  1.7 5.3 %force.8 = (f32[96,1024]{1,0:T(8,128)S(1)}, f32[96,1024]{1,0:T(8,128)S(1)}, f32[64,1024]{1,0:T(8,128)S(1)}, f32[96,1024]{1,0:T(8,128)S(1)}, f32[96,1024]{1,0:T(8,128)S(1)}, /*index=5*/f32[64,1024]{1,0:T(8,128)S(1)}) custom-call(s32[18]{0:T(128)S(1)} %dynamic-slice_bitcast_fusion.place_ref, bf16[2,64,256,256]{3,2,1,0:T(8,128)(2,1)} %warped.15, ...), custom_call_target="tpu_custom_call" | custom-call | flops 1073741824 | bytes 8388608 | tf_op jit(solution)/shard_map/force/pallas_call | solution.py:181
  12.1 5.3 %force.9 = (f32[96,1024]{1,0:T(8,128)S(1)}, f32[96,1024]{1,0:T(8,128)S(1)}, f32[64,1024]{1,0:T(8,128)S(1)}, f32[96,1024]{1,0:T(8,128)S(1)}, f32[96,1024]{1,0:T(8,128)S(1)}, /*index=5*/f32[64,1024]{1,0:T(8,128)S(1)}) custom-call(s32[18]{0:T(128)S(1)} %dynamic-slice_bitcast_fusion.place_ref, bf16[2,64,256,256]{3,2,1,0:T(8,128)(2,1)} %warped.15, ...), custom_call_target="tpu_custom_call" | custom-call | flops 1073741824 | bytes 8388608 | tf_op jit(solution)/shard_map/force/pallas_call | solution.py:181
  22.3 6.1 %collective-permute-done.14 = f32[96,1024]{1,0:T(8,128)S(1)} collective-permute-done((f32[96,1024]{1,0:T(8,128)S(1)}, f32[96,1024]{1,0:T(8,128)S(1)}, u32[]{:S(2)}, u32[]{:S(2)}) %collective-permute-start.14) | collective-permute-done | bytes 393248 | tf_op jit(solution)/shard_map/ppermute | solution.py:588
  30.7 5.3 %force.10 = (f32[96,1024]{1,0:T(8,128)S(1)}, f32[96,1024]{1,0:T(8,128)S(1)}, f32[64,1024]{1,0:T(8,128)S(1)}, f32[96,1024]{1,0:T(8,128)S(1)}, f32[96,1024]{1,0:T(8,128)S(1)}, /*index=5*/f32[64,1024]{1,0:T(8,128)S(1)}) custom-call(s32[18]{0:T(128)S(1)} %dynamic-slice_bitcast_fusion.place_ref, bf16[2,64,256,256]{3,2,1,0:T(8,128)(2,1)} %warped.15, ...), custom_call_target="tpu_custom_call" | custom-call | flops 1073741824 | bytes 8388608 | tf_op jit(solution)/shard_map/force/pallas_call | solution.py:181
  39.2 6.1 %collective-permute-done.15 = f32[96,1024]{1,0:T(8,128)S(1)} collective-permute-done((f32[96,1024]{1,0:T(8,128)S(1)}, f32[96,1024]{1,0:T(8,128)S(1)}, u32[]{:S(2)}, u32[]{:S(2)}) %collective-permute-start.15) | collective-permute-done | bytes 393248 | tf_op jit(solution)/shard_map/ppermute | solution.py:588
  47.6 5.3 %force.11 = (f32[96,1024]{1,0:T(8,128)S(1)}, f32[96,1024]{1,0:T(8,128)S(1)}, f32[64,1024]{1,0:T(8,128)S(1)}, f32[96,1024]{1,0:T(8,128)S(1)}, f32[96,1024]{1,0:T(8,128)S(1)}, /*index=5*/f32[64,1024]{1,0:T(8,128)S(1)}) custom-call(s32[18]{0:T(128)S(1)} %dynamic-slice_bitcast_fusion.place_ref, bf16[2,64,256,256]{3,2,1,0:T(8,128)(2,1)} %warped.15, ...), custom_call_target="tpu_custom_call" | custom-call | flops 1073741824 | bytes 8388608 | tf_op jit(solution)/shard_map/force/pallas_call | solution.py:181
  56.0 6.1 %collective-permute-done.16 = f32[96,1024]{1,0:T(8,128)S(1)} collective-permute-done((f32[96,1024]{1,0:T(8,128)S(1)}, f32[96,1024]{1,0:T(8,128)S(1)}, u32[]{:S(2)}, u32[]{:S(2)}) %collective-permute-start.16) | collective-permute-done | bytes 393248 | tf_op jit(solution)/shard_map/ppermute | solution.py:588
  64.5 5.3 %force.12 = (f32[96,1024]{1,0:T(8,128)S(1)}, f32[96,1024]{1,0:T(8,128)S(1)}, f32[64,1024]{1,0:T(8,128)S(1)}, f32[96,1024]{1,0:T(8,128)S(1)}, f32[96,1024]{1,0:T(8,128)S(1)}, /*index=5*/f32[64,1024]{1,0:T(8,128)S(1)}) custom-call(s32[18]{0:T(128)S(1)} %dynamic-slice_bitcast_fusion.place_ref, bf16[2,64,256,256]{3,2,1,0:T(8,128)(2,1)} %warped.15, ...), custom_call_target="tpu_custom_call" | custom-call | flops 1073741824 | bytes 8388608 | tf_op jit(solution)/shard_map/force/pallas_call | solution.py:181
  72.9 6.1 %collective-permute-done.17 = f32[96,1024]{1,0:T(8,128)S(1)} collective-permute-done((f32[96,1024]{1,0:T(8,128)S(1)}, f32[96,1024]{1,0:T(8,128)S(1)}, u32[]{:S(2)}, u32[]{:S(2)}) %collective-permute-start.17) | collective-permute-done | bytes 393248 | tf_op jit(solution)/shard_map/ppermute | solution.py:588
  81.5 5.3 %force.13 = (f32[96,1024]{1,0:T(8,128)S(1)}, f32[96,1024]{1,0:T(8,128)S(1)}, f32[64,1024]{1,0:T(8,128)S(1)}, f32[96,1024]{1,0:T(8,128)S(1)}, f32[96,1024]{1,0:T(8,128)S(1)}, /*index=5*/f32[64,1024]{1,0:T(8,128)S(1)}) custom-call(s32[18]{0:T(128)S(1)} %dynamic-slice_bitcast_fusion.place_ref, bf16[2,64,256,256]{3,2,1,0:T(8,128)(2,1)} %warped.15, ...), custom_call_target="tpu_custom_call" | custom-call | flops 1073741824 | bytes 8388608 | tf_op jit(solution)/shard_map/force/pallas_call | solution.py:181
  89.7 6.1 %collective-permute-done.18 = f32[96,1024]{1,0:T(8,128)S(1)} collective-permute-done((f32[96,1024]{1,0:T(8,128)S(1)}, f32[96,1024]{1,0:T(8,128)S(1)}, u32[]{:S(2)}, u32[]{:S(2)}) %collective-permute-start.18) | collective-permute-done | bytes 393248 | tf_op jit(solution)/shard_map/ppermute | solution.py:588
  98.2 5.3 %force.15 = (f32[96,1024]{1,0:T(8,128)S(1)}, f32[96,1024]{1,0:T(8,128)S(1)}, f32[64,1024]{1,0:T(8,128)S(1)}, f32[96,1024]{1,0:T(8,128)S(1)}, f32[96,1024]{1,0:T(8,128)S(1)}, /*index=5*/f32[64,1024]{1,0:T(8,128)S(1)}) custom-call(s32[18]{0:T(128)S(1)} %dynamic-slice_bitcast_fusion.place_ref, bf16[2,64,256,256]{3,2,1,0:T(8,128)(2,1)} %warped.15, ...), custom_call_target="tpu_custom_call" | custom-call | flops 1073741824 | bytes 8388608 | tf_op jit(solution)/shard_map/force/pallas_call | solution.py:181
  104.2 5.3 %force.14 = (f32[96,1024]{1,0:T(8,128)S(1)}, f32[96,1024]{1,0:T(8,128)S(1)}, f32[64,1024]{1,0:T(8,128)S(1)}, f32[96,1024]{1,0:T(8,128)S(1)}, f32[96,1024]{1,0:T(8,128)S(1)}, /*index=5*/f32[64,1024]{1,0:T(8,128)S(1)}) custom-call(s32[18]{0:T(128)S(1)} %dynamic-slice_bitcast_fusion.place_ref, bf16[2,64,256,256]{3,2,1,0:T(8,128)(2,1)} %warped.15, ...), custom_call_target="tpu_custom_call" | custom-call | flops 1073741824 | bytes 8388608 | tf_op jit(solution)/shard_map/force/pallas_call | solution.py:181
  117.6 7.6 %collective-permute-done.6.rest_1_ = f32[96,1024]{1,0:T(8,128)S(1)} collective-permute-done((f32[96,1024]{1,0:T(8,128)S(1)}, f32[96,1024]{1,0:T(8,128)S(1)}, u32[]{:S(2)}, u32[]{:S(2)}) %collective-permute-start.6) | collective-permute-done | bytes 393248 | tf_op jit(solution)/shard_map/ppermute | solution.py:588
  136.6 3.9 %collective-permute-done.28 = f32[64,1024]{1,0:T(8,128)S(1)} collective-permute-done((f32[64,1024]{1,0:T(8,128)S(1)}, f32[64,1024]{1,0:T(8,128)S(1)}, u32[]{:S(2)}, u32[]{:S(2)}) %collective-permute-start.28) | collective-permute-done | bytes 262176 | tf_op jit(solution)/shard_map/ppermute | solution.py:588
  142.7 4.2 %collective-permute-done.29 = f32[64,1024]{1,0:T(8,128)S(1)} collective-permute-done((f32[64,1024]{1,0:T(8,128)S(1)}, f32[64,1024]{1,0:T(8,128)S(1)}, u32[]{:S(2)}, u32[]{:S(2)}) %collective-permute-start.29) | collective-permute-done | bytes 262176 | tf_op jit(solution)/shard_map/ppermute | solution.py:588
  150.9 4.2 %collective-permute-done.33 = f32[64,1024]{1,0:T(8,128)S(1)} collective-permute-done((f32[64,1024]{1,0:T(8,128)S(1)}, f32[64,1024]{1,0:T(8,128)S(1)}, u32[]{:S(2)}, u32[]{:S(2)}) %collective-permute-start.33) | collective-permute-done | bytes 262176 | tf_op jit(solution)/shard_map/ppermute | solution.py:588
  159.3 4.4 %first_forward.1 = (f32[768,512]{1,0:T(8,128)}, f32[48,1024]{1,0:T(8,128)S(1)}) custom-call(s32[18]{0:T(128)S(1)} %dynamic-slice_bitcast_fusion.place_ref, f32[4,4,48,256]{3,2,1,0:T(8,128)S(1)} %copy-done.2, bf16[4,384,512]{2,1,0:T(8,128)(2,1)} %constant.36.clone.w_ref, f32[48,2048]{1,0:T(8,128)S(1)} %get-tuple-element.158.rest_0_, ...), custom_call_target="tpu_custom_call" | custom-call | flops 1207959552 | bytes 3145728 | tf_op jit(solution)/shard_map/first_forward/pallas_call | solution.py:111
  169.0 10.9 %collective-permute-done.39 = f32[112,1024]{1,0:T(8,128)S(1)} collective-permute-done((f32[112,1024]{1,0:T(8,128)S(1)}, f32[112,1024]{1,0:T(8,128)S(1)}, u32[]{:S(2)}, u32[]{:S(2)}) %collective-permute-start.39) | collective-permute-done | bytes 458784 | tf_op jit(solution)/shard_map/ppermute | solution.py:588
  182.2 10.6 %collective-permute-done.40 = f32[112,1024]{1,0:T(8,128)S(1)} collective-permute-done((f32[112,1024]{1,0:T(8,128)S(1)}, f32[112,1024]{1,0:T(8,128)S(1)}, u32[]{:S(2)}, u32[]{:S(2)}) %collective-permute-start.40) | collective-permute-done | bytes 458784 | tf_op jit(solution)/shard_map/ppermute | solution.py:588
  195.2 7.1 %collective-permute-done.41.rest_2_ = f32[112,1024]{1,0:T(8,128)S(1)} collective-permute-done((f32[112,1024]{1,0:T(8,128)S(1)}, f32[112,1024]{1,0:T(8,128)S(1)}, u32[]{:S(2)}, u32[]{:S(2)}) %collective-permute-start.41) | collective-permute-done | bytes 458784 | tf_op jit(solution)/shard_map/ppermute | solution.py:588
  209.2 4.1 %second_and_back.1 = (f32[48,2048]{1,0:T(8,128)S(1)}, f32[48,2048]{1,0:T(8,128)S(1)}, f32[96,2048]{1,0:T(8,128)S(1)}) custom-call(s32[18]{0:T(128)S(1)} %dynamic-slice_bitcast_fusion.place_ref, f32[4,4,48,256]{3,2,1,0:T(8,128)S(1)} %copy-done.2, bf16[4,1536,128]{2,1,0:T(8,128)(2,1)} %constant.39.clone.v_ref, f32[768,512]{1,0:T(8,128)} %get-tuple-element.170.f_ref, ...), custom_call_target="tpu_custom_call" | custom-call | flops 1207959552 | bytes 4718592 | tf_op jit(solution)/shard_map/second_and_back/pallas_call | solution.py:111
  220.6 12.5 %collective-permute-done.50 = f32[96,2048]{1,0:T(8,128)} collective-permute-done((f32[96,2048]{1,0:T(8,128)S(1)}, f32[96,2048]{1,0:T(8,128)}, u32[]{:S(2)}, u32[]{:S(2)}) %collective-permute-start.50) | collective-permute-done | bytes 786464 | tf_op jit(solution)/shard_map/ppermute | solution.py:644
  236.1 4.6 %last_back.1 = f32[64,32,256]{2,1,0:T(8,128)} custom-call(s32[18]{0:T(128)S(1)} %dynamic-slice_bitcast_fusion.place_ref, bf16[2,256,256]{2,1,0:T(8,128)(2,1)S(1)} %copy-done.7, f32[64,32,256]{2,1,0:T(8,128)} %velocity.1, f32[48,2048]{1,0:T(8,128)S(1)} %get-tuple-element.179.rest_0_, f32[48,2048]{1,0:T(8,128)S(1)} %collective-permute-done.49.rest_1_, ...), custom_call_target="tpu_custom_call" | custom-call | tf_op jit(solution)/shard_map/last_back/pallas_call | solution.py:547
  (171 shorter events, 93.4 us)
Async XLA Ops:
  10.1 18.3 %collective-permute-start.14 = (f32[96,1024]{1,0:T(8,128)S(1)}, f32[96,1024]{1,0:T(8,128)S(1)}, u32[]{:S(2)}, u32[]{:S(2)}) collective-permute-start(f32[96,1024]{1,0:T(8,128)S(1)} %get-tuple-element.126), channel_id=1, source_target_pairs={{0,8},{8,16},{16,24},{24,28},{28,20},{20,12},{12,4},{4,0},{1,9},{9... | collective-permute-start | bytes 1179656 | tf_op jit(solution)/shard_map/ppermute | solution.py:588
  12.1 18.5 %collective-permute-start.21 = (f32[96,1024]{1,0:T(8,128)S(1)}, f32[96,1024]{1,0:T(8,128)S(1)}, u32[]{:S(2)}, u32[]{:S(2)}) collective-permute-start(f32[96,1024]{1,0:T(8,128)S(1)} %get-tuple-element.133), channel_id=1, source_target_pairs={{8,0},{16,8},{24,16},{28,24},{20,28},{12,20},{4,12},{0,4},{9,1},{1... | collective-permute-start | bytes 1179656 | tf_op jit(solution)/shard_map/ppermute | solution.py:588
  20.0 16.8 %collective-permute-start.1 = (f32[96,1024]{1,0:T(8,128)S(1)}, f32[96,1024]{1,0:T(8,128)S(1)}, u32[]{:S(2)}, u32[]{:S(2)}) collective-permute-start(f32[96,1024]{1,0:T(8,128)S(1)} %add.116), channel_id=1, source_target_pairs={{0,8},{8,16},{16,24},{24,28},{28,20},{20,12},{12,4},{4,0},{1,9},{9... | collective-permute-start | bytes 1179656 | tf_op jit(solution)/shard_map/ppermute | solution.py:588
  22.3 16.8 %collective-permute-start.8 = (f32[96,1024]{1,0:T(8,128)S(1)}, f32[96,1024]{1,0:T(8,128)S(1)}, u32[]{:S(2)}, u32[]{:S(2)}) collective-permute-start(f32[96,1024]{1,0:T(8,128)S(1)} %add.122), channel_id=1, source_target_pairs={{8,0},{16,8},{24,16},{28,24},{20,28},{12,20},{4,12},{0,4},{9,1},{1... | collective-permute-start | bytes 1179656 | tf_op jit(solution)/shard_map/ppermute | solution.py:588
  28.4 16.8 %collective-permute-start.15 = (f32[96,1024]{1,0:T(8,128)S(1)}, f32[96,1024]{1,0:T(8,128)S(1)}, u32[]{:S(2)}, u32[]{:S(2)}) collective-permute-start(f32[96,1024]{1,0:T(8,128)S(1)} %add.128), channel_id=1, source_target_pairs={{0,8},{8,16},{16,24},{24,28},{28,20},{20,12},{12,4},{4,0},{1,9},{9... | collective-permute-start | bytes 1179656 | tf_op jit(solution)/shard_map/ppermute | solution.py:588
  30.7 16.8 %collective-permute-start.22 = (f32[96,1024]{1,0:T(8,128)S(1)}, f32[96,1024]{1,0:T(8,128)S(1)}, u32[]{:S(2)}, u32[]{:S(2)}) collective-permute-start(f32[96,1024]{1,0:T(8,128)S(1)} %add.134), channel_id=1, source_target_pairs={{8,0},{16,8},{24,16},{28,24},{20,28},{12,20},{4,12},{0,4},{9,1},{1... | collective-permute-start | bytes 1179656 | tf_op jit(solution)/shard_map/ppermute | solution.py:588
  36.9 16.8 %collective-permute-start.2 = (f32[96,1024]{1,0:T(8,128)S(1)}, f32[96,1024]{1,0:T(8,128)S(1)}, u32[]{:S(2)}, u32[]{:S(2)}) collective-permute-start(f32[96,1024]{1,0:T(8,128)S(1)} %add.117), channel_id=1, source_target_pairs={{0,8},{8,16},{16,24},{24,28},{28,20},{20,12},{12,4},{4,0},{1,9},{9... | collective-permute-start | bytes 1179656 | tf_op jit(solution)/shard_map/ppermute | solution.py:588
  39.1 16.8 %collective-permute-start.9 = (f32[96,1024]{1,0:T(8,128)S(1)}, f32[96,1024]{1,0:T(8,128)S(1)}, u32[]{:S(2)}, u32[]{:S(2)}) collective-permute-start(f32[96,1024]{1,0:T(8,128)S(1)} %add.123), channel_id=1, source_target_pairs={{8,0},{16,8},{24,16},{28,24},{20,28},{12,20},{4,12},{0,4},{9,1},{1... | collective-permute-start | bytes 1179656 | tf_op jit(solution)/shard_map/ppermute | solution.py:588
  45.3 16.8 %collective-permute-start.16 = (f32[96,1024]{1,0:T(8,128)S(1)}, f32[96,1024]{1,0:T(8,128)S(1)}, u32[]{:S(2)}, u32[]{:S(2)}) collective-permute-start(f32[96,1024]{1,0:T(8,128)S(1)} %add.129), channel_id=1, source_target_pairs={{0,8},{8,16},{16,24},{24,28},{28,20},{20,12},{12,4},{4,0},{1,9},{9... | collective-permute-start | bytes 1179656 | tf_op jit(solution)/shard_map/ppermute | solution.py:588
  47.5 16.8 %collective-permute-start.23 = (f32[96,1024]{1,0:T(8,128)S(1)}, f32[96,1024]{1,0:T(8,128)S(1)}, u32[]{:S(2)}, u32[]{:S(2)}) collective-permute-start(f32[96,1024]{1,0:T(8,128)S(1)} %add.135), channel_id=1, source_target_pairs={{8,0},{16,8},{24,16},{28,24},{20,28},{12,20},{4,12},{0,4},{9,1},{1... | collective-permute-start | bytes 1179656 | tf_op jit(solution)/shard_map/ppermute | solution.py:588
  53.7 16.8 %collective-permute-start.3 = (f32[96,1024]{1,0:T(8,128)S(1)}, f32[96,1024]{1,0:T(8,128)S(1)}, u32[]{:S(2)}, u32[]{:S(2)}) collective-permute-start(f32[96,1024]{1,0:T(8,128)S(1)} %add.118), channel_id=1, source_target_pairs={{0,8},{8,16},{16,24},{24,28},{28,20},{20,12},{12,4},{4,0},{1,9},{9... | collective-permute-start | bytes 1179656 | tf_op jit(solution)/shard_map/ppermute | solution.py:588
  56.0 16.8 %collective-permute-start.10 = (f32[96,1024]{1,0:T(8,128)S(1)}, f32[96,1024]{1,0:T(8,128)S(1)}, u32[]{:S(2)}, u32[]{:S(2)}) collective-permute-start(f32[96,1024]{1,0:T(8,128)S(1)} %add.124), channel_id=1, source_target_pairs={{8,0},{16,8},{24,16},{28,24},{20,28},{12,20},{4,12},{0,4},{9,1},{1... | collective-permute-start | bytes 1179656 | tf_op jit(solution)/shard_map/ppermute | solution.py:588
  62.1 16.8 %collective-permute-start.17 = (f32[96,1024]{1,0:T(8,128)S(1)}, f32[96,1024]{1,0:T(8,128)S(1)}, u32[]{:S(2)}, u32[]{:S(2)}) collective-permute-start(f32[96,1024]{1,0:T(8,128)S(1)} %add.130), channel_id=1, source_target_pairs={{0,8},{8,16},{16,24},{24,28},{28,20},{20,12},{12,4},{4,0},{1,9},{9... | collective-permute-start | bytes 1179656 | tf_op jit(solution)/shard_map/ppermute | solution.py:588
  64.4 16.8 %collective-permute-start.24 = (f32[96,1024]{1,0:T(8,128)S(1)}, f32[96,1024]{1,0:T(8,128)S(1)}, u32[]{:S(2)}, u32[]{:S(2)}) collective-permute-start(f32[96,1024]{1,0:T(8,128)S(1)} %add.136), channel_id=1, source_target_pairs={{8,0},{16,8},{24,16},{28,24},{20,28},{12,20},{4,12},{0,4},{9,1},{1... | collective-permute-start | bytes 1179656 | tf_op jit(solution)/shard_map/ppermute | solution.py:588
  70.6 16.8 %collective-permute-start.4 = (f32[96,1024]{1,0:T(8,128)S(1)}, f32[96,1024]{1,0:T(8,128)S(1)}, u32[]{:S(2)}, u32[]{:S(2)}) collective-permute-start(f32[96,1024]{1,0:T(8,128)S(1)} %add.119), channel_id=1, source_target_pairs={{0,8},{8,16},{16,24},{24,28},{28,20},{20,12},{12,4},{4,0},{1,9},{9... | collective-permute-start | bytes 1179656 | tf_op jit(solution)/shard_map/ppermute | solution.py:588
  72.8 16.8 %collective-permute-start.11 = (f32[96,1024]{1,0:T(8,128)S(1)}, f32[96,1024]{1,0:T(8,128)S(1)}, u32[]{:S(2)}, u32[]{:S(2)}) collective-permute-start(f32[96,1024]{1,0:T(8,128)S(1)} %add.125), channel_id=1, source_target_pairs={{8,0},{16,8},{24,16},{28,24},{20,28},{12,20},{4,12},{0,4},{9,1},{1... | collective-permute-start | bytes 1179656 | tf_op jit(solution)/shard_map/ppermute | solution.py:588
  79.0 16.8 %collective-permute-start.18 = (f32[96,1024]{1,0:T(8,128)S(1)}, f32[96,1024]{1,0:T(8,128)S(1)}, u32[]{:S(2)}, u32[]{:S(2)}) collective-permute-start(f32[96,1024]{1,0:T(8,128)S(1)} %add.131), channel_id=1, source_target_pairs={{0,8},{8,16},{16,24},{24,28},{28,20},{20,12},{12,4},{4,0},{1,9},{9... | collective-permute-start | bytes 1179656 | tf_op jit(solution)/shard_map/ppermute | solution.py:588
  81.2 16.8 %collective-permute-start.25 = (f32[96,1024]{1,0:T(8,128)S(1)}, f32[96,1024]{1,0:T(8,128)S(1)}, u32[]{:S(2)}, u32[]{:S(2)}) collective-permute-start(f32[96,1024]{1,0:T(8,128)S(1)} %add.137), channel_id=1, source_target_pairs={{8,0},{16,8},{24,16},{28,24},{20,28},{12,20},{4,12},{0,4},{9,1},{1... | collective-permute-start | bytes 1179656 | tf_op jit(solution)/shard_map/ppermute | solution.py:588
  87.4 25.7 %collective-permute-start.5 = (f32[96,1024]{1,0:T(8,128)S(1)}, f32[96,1024]{1,0:T(8,128)S(1)}, u32[]{:S(2)}, u32[]{:S(2)}) collective-permute-start(f32[96,1024]{1,0:T(8,128)S(1)} %add.120), channel_id=1, source_target_pairs={{0,8},{8,16},{16,24},{24,28},{28,20},{20,12},{12,4},{4,0},{1,9},{9... | collective-permute-start | bytes 1179656 | tf_op jit(solution)/shard_map/ppermute | solution.py:588
  89.7 25.5 %collective-permute-start.12 = (f32[96,1024]{1,0:T(8,128)S(1)}, f32[96,1024]{1,0:T(8,128)S(1)}, u32[]{:S(2)}, u32[]{:S(2)}) collective-permute-start(f32[96,1024]{1,0:T(8,128)S(1)} %add.126), channel_id=1, source_target_pairs={{8,0},{16,8},{24,16},{28,24},{20,28},{12,20},{4,12},{0,4},{9,1},{1... | collective-permute-start | bytes 1179656 | tf_op jit(solution)/shard_map/ppermute | solution.py:588
  95.8 19.5 %collective-permute-start.19 = (f32[96,1024]{1,0:T(8,128)S(1)}, f32[96,1024]{1,0:T(8,128)S(1)}, u32[]{:S(2)}, u32[]{:S(2)}) collective-permute-start(f32[96,1024]{1,0:T(8,128)S(1)} %add.132), channel_id=1, source_target_pairs={{0,8},{8,16},{16,24},{24,28},{28,20},{20,12},{12,4},{4,0},{1,9},{9... | collective-permute-start | bytes 1179656 | tf_op jit(solution)/shard_map/ppermute | solution.py:588
  98.1 19.3 %collective-permute-start.26 = (f32[96,1024]{1,0:T(8,128)S(1)}, f32[96,1024]{1,0:T(8,128)S(1)}, u32[]{:S(2)}, u32[]{:S(2)}) collective-permute-start(f32[96,1024]{1,0:T(8,128)S(1)} %add.138), channel_id=1, source_target_pairs={{8,0},{16,8},{24,16},{28,24},{20,28},{12,20},{4,12},{0,4},{9,1},{1... | collective-permute-start | bytes 1179656 | tf_op jit(solution)/shard_map/ppermute | solution.py:588
  213.4 19.8 %collective-permute-start.50 = (f32[96,2048]{1,0:T(8,128)S(1)}, f32[96,2048]{1,0:T(8,128)}, u32[]{:S(2)}, u32[]{:S(2)}) collective-permute-start(f32[96,2048]{1,0:T(8,128)S(1)} %get-tuple-element.181), channel_id=1, source_target_pairs={{0,2},{1,3},{2,0},{3,1},{4,6},{5,7},{6,4},{7,5},{8,10},{9,11},{10,... | collective-permute-start | bytes 2359304 | tf_op jit(solution)/shard_map/ppermute | solution.py:644
  217.1 19.0 %all-to-all-start = ((f32[8,8,2048]{2,1,0:T(8,128)}), f32[8,8,2048]{2,1,0:T(8,128)S(1)}, u32[]{:S(2)}, u32[]{:S(2)}) async-start(f32[8,8,2048]{2,1,0:T(8,128)} %first_and_back.1), calls=%async_computation | async-start | bytes 1048576 | tf_op jit(solution)/shard_map/all_to_all | solution.py:648
  (40 other events, 336.0 us)
